TPU v7x, 256 devices: a whole 4x4x8 slice. The times are simulated.
256 devices in a mesh: prompt: 16 (over z, core), leaf: 16 (over y, x).
Axes of the slice: x: 4, y: 4, z: 8, core: 2. Of those that a mesh axis runs over, the one named last changes fastest.
Arguments:
- queries: bfloat16 [256, 2, 128, 5120], P(('prompt', 'leaf')), parts along dimension 0, may hold values from -6 to 6
- keys: bfloat16 [256, 2, 128, 1024], P(('prompt', 'leaf')), parts along dimension 0, may hold values from -6 to 6
- values: bfloat16 [256, 2, 128, 1024], P(('prompt', 'leaf')), parts along dimension 0, may hold values from -6 to 6
- out_grad: bfloat16 [256, 2, 128, 5120], P(('prompt', 'leaf')), parts along dimension 0, may hold values from -6 to 6
- seg_lengths: int32 [256, 2], P('prompt'), parts along dimension 0, may hold values from 64 to 128, as said below
Outputs:
- grad_queries: bfloat16 [256, 2, 128, 5120], P(('prompt', 'leaf')), parts along dimension 0
- grad_keys: bfloat16 [256, 2, 128, 1024], P(('prompt', 'leaf')), parts along dimension 0
- grad_values: bfloat16 [256, 2, 128, 1024], P(('prompt', 'leaf')), parts along dimension 0
There are 16 independent parts, one for each index of `prompt`. A program takes and returns all parts, laid end to end along the dimension named above; each array names one. Nothing has to cross between parts.
Inputs may be any that keep to these rules, and one draw needn't show every extreme that they name: `seg_lengths`: the number of leading slots of a segment that hold tokens; some segment of each prompt holds 128.
All inputs are finite; a program needn't handle non-finite values.
Results may differ from a plain program's by a relative error of at most 0.012.
Values may be sent and summed in bfloat16 or wider, within the bound.
No kernel may reach another device: no remote copies, remote signals or barrier semaphores. Data moves between devices by JAX's collectives and lax.ppermute only.
A program may use at most 128 MiB of HBM per device.

v0:
```python
import math

import jax
import jax.numpy as jnp
from jax import lax
from jax.sharding import PartitionSpec as P

QUERY_HEADS = 40
KEY_VALUE_HEADS = 8
HEAD_WIDTH = 128
QUERY_PER_KEY = 5


def allowed_mask(ctx_lengths, own_lengths, inner_place, seg_len):
    seg_total = ctx_lengths.shape[0]
    key_place = jnp.repeat(jnp.arange(seg_total, dtype=jnp.int32), seg_len)
    key_slot = jnp.tile(jnp.arange(seg_len, dtype=jnp.int32), seg_total)
    key_live = key_slot < jnp.repeat(ctx_lengths, seg_len)
    query_slot = jnp.tile(jnp.arange(seg_len, dtype=jnp.int32), 2)
    query_place = jnp.concatenate(
        [
            jnp.zeros((seg_len,), jnp.int32) + inner_place,
            jnp.full((seg_len,), seg_total - 1, jnp.int32),
        ]
    )
    earlier = key_place[None, :] < query_place[:, None]
    causal = (key_place[None, :] == query_place[:, None]) & (
        key_slot[None, :] <= query_slot[:, None]
    )
    allowed = key_live[None, :] & (earlier | causal)
    query_live = query_slot < jnp.repeat(own_lengths, seg_len)
    return (allowed, query_live)


def attend_backward(
    local_query_rows, context_key_rows, context_value_rows, own_grad, allowed, query_live
):
    total_row_number = local_query_rows.shape[0]
    score_scale = 1.0 / math.sqrt(HEAD_WIDTH)
    running_gradient = jnp.where(query_live[:, None], own_grad, jnp.zeros_like(own_grad))
    query_head_rows = local_query_rows.reshape(
        total_row_number, KEY_VALUE_HEADS, QUERY_PER_KEY, HEAD_WIDTH
    ).transpose(1, 0, 2, 3)
    head_gradient_rows = running_gradient.reshape(
        total_row_number, KEY_VALUE_HEADS, QUERY_PER_KEY, HEAD_WIDTH
    ).transpose(1, 0, 2, 3)
    key_head_rows = context_key_rows.reshape(-1, KEY_VALUE_HEADS, HEAD_WIDTH).transpose(1, 0, 2)
    value_head_rows = context_value_rows.reshape(-1, KEY_VALUE_HEADS, HEAD_WIDTH).transpose(1, 0, 2)

    def per_group(operands):
        query_group, key_group, value_group, grad_group = operands
        scores = (
            jnp.einsum("rgd,cd->grc", query_group, key_group, preferred_element_type=jnp.float32)
            * score_scale
        )
        scores = jnp.where(allowed[None], scores, -jnp.inf)
        highest = jnp.max(scores, axis=-1, keepdims=True)
        exponent = jnp.exp(scores - highest)
        weights = exponent / jnp.sum(exponent, axis=-1, keepdims=True)
        weights_half = weights.astype(jnp.bfloat16)
        output = jnp.einsum(
            "grc,cd->rgd", weights_half, value_group, preferred_element_type=jnp.float32
        )
        row_delta = jnp.transpose(jnp.sum(grad_group.astype(jnp.float32) * output, axis=-1))
        weight_grad = jnp.einsum(
            "rgd,cd->grc", grad_group, value_group, preferred_element_type=jnp.float32
        )
        score_grad = weights * (weight_grad - row_delta[:, :, None])
        score_half = score_grad.astype(jnp.bfloat16)
        query_gradient_block = (
            jnp.einsum("grc,cd->rgd", score_half, key_group, preferred_element_type=jnp.float32)
            * score_scale
        )
        key_gradient_block = (
            jnp.einsum("grc,rgd->cd", score_half, query_group, preferred_element_type=jnp.float32)
            * score_scale
        )
        value_gradient_block = jnp.einsum(
            "grc,rgd->cd", weights_half, grad_group, preferred_element_type=jnp.float32
        )
        return (query_gradient_block, key_gradient_block, value_gradient_block)

    query_gradient_block, key_gradient_block, value_gradient_block = lax.map(
        per_group, (query_head_rows, key_head_rows, value_head_rows, head_gradient_rows)
    )
    query_gradient_block = query_gradient_block.transpose(1, 0, 2, 3).reshape(
        total_row_number, QUERY_HEADS * HEAD_WIDTH
    )
    key_gradient_block = key_gradient_block.transpose(1, 0, 2).reshape(
        -1, KEY_VALUE_HEADS * HEAD_WIDTH
    )
    value_gradient_block = value_gradient_block.transpose(1, 0, 2).reshape(
        -1, KEY_VALUE_HEADS * HEAD_WIDTH
    )
    return (query_gradient_block, key_gradient_block, value_gradient_block)


def shards(queries, keys, values, out_grad, seg_lengths):
    leaf_total = lax.axis_size("leaf")
    depth_count = leaf_total.bit_length() - 1
    seg_len = queries.shape[2]
    kv_width = keys.shape[3]
    my_index = lax.axis_index("leaf")
    owner_list = [jnp.zeros((), jnp.int32)]
    inner_place = jnp.zeros((), jnp.int32)
    for position in range(1, depth_count + 1):
        span_width = 2 ** (depth_count - position + 1)
        owner_id = my_index // span_width * span_width + span_width // 2
        owner_list.append(owner_id)
        inner_place = jnp.where(owner_id == my_index, position, inner_place)
    owner_ids = jnp.stack(owner_list)
    device_ids = jnp.arange(leaf_total, dtype=jnp.int32)
    owner_match = owner_ids[:, None] == device_ids[None, :]
    ancestor_lengths = jnp.sum(jnp.where(owner_match, seg_lengths[None, :, 0], 0), axis=1)
    is_mine = my_index == device_ids
    own_lengths = jnp.sum(jnp.where(is_mine[:, None], seg_lengths, 0), axis=0)
    ctx_lengths = jnp.concatenate([ancestor_lengths, own_lengths[1:]])
    kv_inner = jnp.concatenate([keys[0, 0], values[0, 0]], axis=-1)
    all_inner = lax.all_gather(kv_inner[None], "leaf", axis=0, tiled=True)
    ancestors = jnp.take(all_inner, owner_ids, axis=0)
    leaf_kv = jnp.concatenate([keys[0, 1], values[0, 1]], axis=-1)
    ctx_kv = jnp.concatenate([ancestors, leaf_kv[None]], axis=0)
    context_key_rows = ctx_kv[:, :, :kv_width].reshape(-1, kv_width)
    context_value_rows = ctx_kv[:, :, kv_width:].reshape(-1, kv_width)
    allowed, query_live = allowed_mask(ctx_lengths, own_lengths, inner_place, seg_len)
    local_query_rows = queries[0].reshape(2 * seg_len, -1)
    own_grad = out_grad[0].reshape(2 * seg_len, -1)
    query_gradient_block, key_gradient_block, value_gradient_block = attend_backward(
        local_query_rows, context_key_rows, context_value_rows, own_grad, allowed, query_live
    )
    partial_value = jnp.concatenate([key_gradient_block, value_gradient_block], axis=-1).reshape(
        depth_count + 2, seg_len, 2 * kv_width
    )
    fanout_factor = (
        jnp.zeros((leaf_total, seg_len, 2 * kv_width), jnp.float32)
        .at[owner_ids]
        .set(partial_value[: depth_count + 1])
    )
    inner_total = lax.psum_scatter(fanout_factor, "leaf", scatter_dimension=0, tiled=True)[0]
    leaf_total_grad = partial_value[depth_count + 1]
    grad_keys = jnp.stack([inner_total[:, :kv_width], leaf_total_grad[:, :kv_width]])[None].astype(
        jnp.bfloat16
    )
    grad_values = jnp.stack([inner_total[:, kv_width:], leaf_total_grad[:, kv_width:]])[
        None
    ].astype(jnp.bfloat16)
    grad_queries = query_gradient_block.reshape(1, 2, seg_len, -1).astype(jnp.bfloat16)
    return (grad_queries, grad_keys, grad_values)


def solution(mesh):
    return jax.shard_map(
        shards,
        mesh=mesh,
        in_specs=(
            P(("prompt", "leaf"), None, None, None),
            P(("prompt", "leaf"), None, None, None),
            P(("prompt", "leaf"), None, None, None),
            P(("prompt", "leaf"), None, None, None),
            P("prompt", None),
        ),
        out_specs=(
            P(("prompt", "leaf"), None, None, None),
            P(("prompt", "leaf"), None, None, None),
            P(("prompt", "leaf"), None, None, None),
        ),
        check_vma=False,
    )
```

profile of v0, /device:TPU:128, one launch (start us, length us, event | category | flops | bytes accessed | tf_op | source)
XLA Modules:
  0.0 426.8 jit_solution(2921272890590014791)
XLA Ops:
  7.2 2.0 slice_bitcast_fusion.2
  11.0 5.9 %copy.72 = bf16[1,2,128,5120]{2,1,3,0:T(2,128)(2,1)S(1)} copy(bf16[1,2,128,5120]{3,2,1,0:T(8,128)(2,1)} %param.7) | data formatting | bytes 5242880 | tf_op args[0]
  16.8 3.5 reshape_reshape_squeeze.3
  20.3 7.5 %copy.73 = bf16[1,2,128,5120]{2,1,3,0:T(2,128)(2,1)} copy(bf16[1,2,128,5120]{3,2,1,0:T(8,128)(2,1)} %param.10) | data formatting | bytes 5242880 | tf_op args[3]
  27.8 4.2 reshape_squeeze.3
  36.1 52.3 %all-gather.3.cloned.1.call-done = bf16[2048,2048]{1,0:T(8,128)(2,1)} async-done(((bf16[128,2048]{1,0:T(8,128)(2,1)}), bf16[2048,2048]{1,0:T(8,128)(2,1)}) %all-gather.3.cloned.1.call-update) | async-done | bytes 8388624 | tf_op jit(solution)/shard_map/all_gather | solution.py:119
  88.4 4.1 gather_fusion
  97.0 174.4 %while.15 = (s32[]{:T(128)}, bf16[8,256,5,128]{1,3,2,0:T(8,128)(2,1)}, f32[8,768,128]{1,2,0:T(8,128)}, f32[8,768,128]{1,2,0:T(8,128)}, bf16[8,768,128]{2,1,0:T(8...) while((s32[]{:T(128)}, ...), condition=%wide.region_6.7_spmd.clone, body=%wide.region_2.6_spmd.clone.sunk | while | flops 1521712640 | bytes 54368212 | solution.py:83
  98.9 4.3 %fusion.104 = (f32[5,256]{1,0:T(8,128)S(1)}, f32[5,256,768]{1,2,0:T(8,128)}) fusion(pred[256,768]{0,1:T(8,128)(4,1)S(1)} %or_and_fusion.2, bf16[8,256,5,128]{1,3,2,0:T(8,128)(2,1)} %get-tuple-element.308, s32[]{:T(128)S(6)} %copy.110, bf16[8,768,128]{2,1,0:T(8,128)(2,1)} %get-tuple-element.307), kind=kOutput, calls=%fused_computation.94.clone.1 | convolution fusion | flops 255591168 | bytes 4659200 | tf_op jit(solution)/shard_map/while/body/eval_jaxpr/sub | solution.py:58
  103.2 2.6 fusion.105
  105.8 1.9 fusion.106
  112.7 2.8 fusion.108
  115.5 2.5 fusion.110
  120.7 4.3 %fusion.104 = (f32[5,256]{1,0:T(8,128)S(1)}, f32[5,256,768]{1,2,0:T(8,128)}) fusion(pred[256,768]{0,1:T(8,128)(4,1)S(1)} %or_and_fusion.2, bf16[8,256,5,128]{1,3,2,0:T(8,128)(2,1)} %get-tuple-element.308, s32[]{:T(128)S(6)} %copy.110, bf16[8,768,128]{2,1,0:T(8,128)(2,1)} %get-tuple-element.307), kind=kOutput, calls=%fused_computation.94.clone.1 | convolution fusion | flops 255591168 | bytes 4659200 | tf_op jit(solution)/shard_map/while/body/eval_jaxpr/sub | solution.py:58
  125.1 2.6 fusion.105
  134.5 2.8 fusion.108
  137.3 2.5 fusion.110
  142.6 4.3 %fusion.104 = (f32[5,256]{1,0:T(8,128)S(1)}, f32[5,256,768]{1,2,0:T(8,128)}) fusion(pred[256,768]{0,1:T(8,128)(4,1)S(1)} %or_and_fusion.2, bf16[8,256,5,128]{1,3,2,0:T(8,128)(2,1)} %get-tuple-element.308, s32[]{:T(128)S(6)} %copy.110, bf16[8,768,128]{2,1,0:T(8,128)(2,1)} %get-tuple-element.307), kind=kOutput, calls=%fused_computation.94.clone.1 | convolution fusion | flops 255591168 | bytes 4659200 | tf_op jit(solution)/shard_map/while/body/eval_jaxpr/sub | solution.py:58
  146.9 2.6 fusion.105
  156.3 2.8 fusion.108
  159.1 2.5 fusion.110
  164.4 4.3 %fusion.104 = (f32[5,256]{1,0:T(8,128)S(1)}, f32[5,256,768]{1,2,0:T(8,128)}) fusion(pred[256,768]{0,1:T(8,128)(4,1)S(1)} %or_and_fusion.2, bf16[8,256,5,128]{1,3,2,0:T(8,128)(2,1)} %get-tuple-element.308, s32[]{:T(128)S(6)} %copy.110, bf16[8,768,128]{2,1,0:T(8,128)(2,1)} %get-tuple-element.307), kind=kOutput, calls=%fused_computation.94.clone.1 | convolution fusion | flops 255591168 | bytes 4659200 | tf_op jit(solution)/shard_map/while/body/eval_jaxpr/sub | solution.py:58
  168.7 2.6 fusion.105
  178.1 2.8 fusion.108
  181.0 2.5 fusion.110
  186.1 4.3 %fusion.104 = (f32[5,256]{1,0:T(8,128)S(1)}, f32[5,256,768]{1,2,0:T(8,128)}) fusion(pred[256,768]{0,1:T(8,128)(4,1)S(1)} %or_and_fusion.2, bf16[8,256,5,128]{1,3,2,0:T(8,128)(2,1)} %get-tuple-element.308, s32[]{:T(128)S(6)} %copy.110, bf16[8,768,128]{2,1,0:T(8,128)(2,1)} %get-tuple-element.307), kind=kOutput, calls=%fused_computation.94.clone.1 | convolution fusion | flops 255591168 | bytes 4659200 | tf_op jit(solution)/shard_map/while/body/eval_jaxpr/sub | solution.py:58
  190.5 2.6 fusion.105
  199.9 2.8 fusion.108
  202.7 2.5 fusion.110
  207.9 4.3 %fusion.104 = (f32[5,256]{1,0:T(8,128)S(1)}, f32[5,256,768]{1,2,0:T(8,128)}) fusion(pred[256,768]{0,1:T(8,128)(4,1)S(1)} %or_and_fusion.2, bf16[8,256,5,128]{1,3,2,0:T(8,128)(2,1)} %get-tuple-element.308, s32[]{:T(128)S(6)} %copy.110, bf16[8,768,128]{2,1,0:T(8,128)(2,1)} %get-tuple-element.307), kind=kOutput, calls=%fused_computation.94.clone.1 | convolution fusion | flops 255591168 | bytes 4659200 | tf_op jit(solution)/shard_map/while/body/eval_jaxpr/sub | solution.py:58
  212.2 2.6 fusion.105
  221.7 2.8 fusion.108
  224.5 2.5 fusion.110
  229.7 4.3 %fusion.104 = (f32[5,256]{1,0:T(8,128)S(1)}, f32[5,256,768]{1,2,0:T(8,128)}) fusion(pred[256,768]{0,1:T(8,128)(4,1)S(1)} %or_and_fusion.2, bf16[8,256,5,128]{1,3,2,0:T(8,128)(2,1)} %get-tuple-element.308, s32[]{:T(128)S(6)} %copy.110, bf16[8,768,128]{2,1,0:T(8,128)(2,1)} %get-tuple-element.307), kind=kOutput, calls=%fused_computation.94.clone.1 | convolution fusion | flops 255591168 | bytes 4659200 | tf_op jit(solution)/shard_map/while/body/eval_jaxpr/sub | solution.py:58
  234.1 2.6 fusion.105
  243.5 2.8 fusion.108
  246.3 2.5 fusion.110
  251.5 4.3 %fusion.104 = (f32[5,256]{1,0:T(8,128)S(1)}, f32[5,256,768]{1,2,0:T(8,128)}) fusion(pred[256,768]{0,1:T(8,128)(4,1)S(1)} %or_and_fusion.2, bf16[8,256,5,128]{1,3,2,0:T(8,128)(2,1)} %get-tuple-element.308, s32[]{:T(128)S(6)} %copy.110, bf16[8,768,128]{2,1,0:T(8,128)(2,1)} %get-tuple-element.307), kind=kOutput, calls=%fused_computation.94.clone.1 | convolution fusion | flops 255591168 | bytes 4659200 | tf_op jit(solution)/shard_map/while/body/eval_jaxpr/sub | solution.py:58
  255.8 2.6 fusion.105
  265.3 2.8 fusion.108
  268.1 2.5 fusion.110
  271.4 5.2 %pad_maximum_fusion = f32[640,2048]{0,1:T(8,128)} fusion(f32[768,1024]{0,1:T(8,128)} %bitcast.223, f32[768,1024]{0,1:T(8,128)} %bitcast.225), kind=kLoop, calls=%fused_computation.57 | loop fusion | flops 1310720 | bytes 11534336 | tf_op jit(solution)/shard_map/concatenate | solution.py:131
  276.6 5.9 %copy.80 = f32[640,2048]{1,0:T(8,128)} copy(f32[640,2048]{0,1:T(8,128)} %pad_maximum_fusion) | data formatting | bytes 10485760 | tf_op jit(solution)/shard_map/slice | solution.py:137
  282.5 7.8 %broadcast_in_dim.123 = f32[16,128,2048]{2,1,0:T(8,128)} broadcast(f32[]{:T(128)} %constant.90.clone.1), dimensions={} | broadcast | bytes 16777220 | tf_op jit(solution)/shard_map/broadcast_in_dim | solution.py:135
  290.3 11.2 %scatter_fusion = f32[16,128,2048]{2,1,0:T(8,128)} fusion(f32[16,128,2048]{2,1,0:T(8,128)} %broadcast_in_dim.123, s32[5]{0:T(128)S(1)} %fusion.59, f32[5,128,2048]{2,1,0:T(8,128)} %bitcast.217), kind=kCustom, calls=%fused_computation.1 | custom fusion | bytes 15728660 | tf_op jit(solution)/shard_map/scatter | solution.py:137
  301.5 3.5 convert_element_type.46
  305.1 4.6 %copy.83 = bf16[1,2,128,5120]{3,2,1,0:T(8,128)(2,1)} copy(bf16[1,2,128,5120]{2,1,3,0:T(2,128)(2,1)S(1)} %convert_element_type.46) | data formatting | bytes 5242880
  312.2 104.7 %reduce-scatter.4.cloned.1.call-done = f32[1,128,2048]{2,1,0:T(8,128)} async-done(((f32[16,128,2048]{2,1,0:T(8,128)}), f32[1,128,2048]{2,1,0:T(8,128)}) %reduce-scatter.4.cloned.1.call-update) | async-done | bytes 1048592
  (138 shorter events, 89.4 us)
Async XLA Ops:
  7.2 3.0 copy-start.2
  7.2 81.2 %all-gather.3.cloned.1.call-start = ((), (), s32[]{:S(2)}) async-start(), calls=%async_computation.1 | async-start | bytes 8912896 | tf_op jit(solution)/shard_map/all_gather | solution.py:119
  10.0 406.9 %reduce-scatter.4.cloned.1.call-start = ((), (), s32[]{:S(2)}) async-start(), calls=%async_computation.2 | async-start | bytes 17825792
  103.2 4.5 %copy-start.1 = (f32[5,256,768]{1,2,0:T(8,128)S(1)}, f32[5,256,768]{1,2,0:T(8,128)}, u32[]{:S(2)}) copy-start(f32[5,256,768]{1,2,0:T(8,128)} %get-tuple-element.273) | copy-start | bytes 11796484 | tf_op jit(solution)/shard_map/while
  109.6 1.3 copy-start
  125.1 4.5 %copy-start.1 = (f32[5,256,768]{1,2,0:T(8,128)S(1)}, f32[5,256,768]{1,2,0:T(8,128)}, u32[]{:S(2)}) copy-start(f32[5,256,768]{1,2,0:T(8,128)} %get-tuple-element.273) | copy-start | bytes 11796484 | tf_op jit(solution)/shard_map/while
  131.4 1.3 copy-start
  146.9 4.5 %copy-start.1 = (f32[5,256,768]{1,2,0:T(8,128)S(1)}, f32[5,256,768]{1,2,0:T(8,128)}, u32[]{:S(2)}) copy-start(f32[5,256,768]{1,2,0:T(8,128)} %get-tuple-element.273) | copy-start | bytes 11796484 | tf_op jit(solution)/shard_map/while
  153.2 1.3 copy-start
  168.7 4.5 %copy-start.1 = (f32[5,256,768]{1,2,0:T(8,128)S(1)}, f32[5,256,768]{1,2,0:T(8,128)}, u32[]{:S(2)}) copy-start(f32[5,256,768]{1,2,0:T(8,128)} %get-tuple-element.273) | copy-start | bytes 11796484 | tf_op jit(solution)/shard_map/while
  175.0 1.3 copy-start
  190.5 4.5 %copy-start.1 = (f32[5,256,768]{1,2,0:T(8,128)S(1)}, f32[5,256,768]{1,2,0:T(8,128)}, u32[]{:S(2)}) copy-start(f32[5,256,768]{1,2,0:T(8,128)} %get-tuple-element.273) | copy-start | bytes 11796484 | tf_op jit(solution)/shard_map/while
  196.8 1.3 copy-start
  212.2 4.5 %copy-start.1 = (f32[5,256,768]{1,2,0:T(8,128)S(1)}, f32[5,256,768]{1,2,0:T(8,128)}, u32[]{:S(2)}) copy-start(f32[5,256,768]{1,2,0:T(8,128)} %get-tuple-element.273) | copy-start | bytes 11796484 | tf_op jit(solution)/shard_map/while
  218.6 1.3 copy-start
  234.1 4.5 %copy-start.1 = (f32[5,256,768]{1,2,0:T(8,128)S(1)}, f32[5,256,768]{1,2,0:T(8,128)}, u32[]{:S(2)}) copy-start(f32[5,256,768]{1,2,0:T(8,128)} %get-tuple-element.273) | copy-start | bytes 11796484 | tf_op jit(solution)/shard_map/while
  240.4 1.3 copy-start
  255.8 4.5 %copy-start.1 = (f32[5,256,768]{1,2,0:T(8,128)S(1)}, f32[5,256,768]{1,2,0:T(8,128)}, u32[]{:S(2)}) copy-start(f32[5,256,768]{1,2,0:T(8,128)} %get-tuple-element.273) | copy-start | bytes 11796484 | tf_op jit(solution)/shard_map/while
  262.2 1.3 copy-start
Sparse Core Ops, SparseCore 0:
  11.0 77.3 all-gather.2
  301.7 115.2 reduce-scatter.3
where the time goes:
time: 431 us; the launch traced here: 427 us
  waiting for transfers between devices  157 us (36%)
  matrix products  120 us (28%)
  local copies, waits for them, and re-layouts  94.6 us (22%)
  other arithmetic  39.9 us (9%)
  between operations  14.3 us (3%)
    unnamed x3, waiting for transfers between devices  105 us
    all_gather x1, waiting for transfers between devices, shards(): all_inner = lax.all_gather(kv_inner[None], 'leaf', axis=0, tiled=True)  52.3 us
    sub x8, matrix products, per_group(): exponent = jnp.exp(scores - highest)  34.5 us
    dot_general x8, matrix products, per_group(): jnp.einsum('grc,cd->rgd', score_half, key_group, preferred_element_type=j...  22.8 us
    unnamed x9, local copies, waits for them, and re-layouts  21.7 us
    convert_element_type x8, other arithmetic, per_group(): weights_half = weights.astype(jnp.bfloat16)  20.7 us
    dot_general x8, matrix products, per_group(): jnp.einsum('grc,rgd->cd', weights_half, grad_group, preferred_element_typ...  20.2 us
    dot_general x8, matrix products, per_group(): jnp.einsum('grc,cd->rgd', weights_half, value_group, preferred_element_ty...  15.5 us
  transfers between devices with their start and end apart: 2, of which 2 were waited for; matrix products, arithmetic and copies ran while one was open for 9% of the time, Pallas kernels for 0%

commit v1 on v0

v1 whole, which is shorter than its diff:
```python
import functools
import math

import jax
import jax.numpy as jnp
from jax import lax
from jax.experimental import pallas as pl
from jax.experimental.pallas import tpu as pltpu
from jax.sharding import PartitionSpec as P

HEADS = 8
GROUP = 5
D = 128
R = 128
BIG = 2.0**30
SCALE = 1.0 / math.sqrt(D)
EXP2_SCALE = SCALE * math.log2(math.e)
CHUNKS = (4, 4)

SWAP = ((0, 1), (1, 0), (2, 3), (3, 2))
ONWARD = ((0, 3), (1, 2), (2, 1), (3, 0))
X_SWAP = [(4 * y + s, 4 * y + t) for y in range(4) for s, t in SWAP]
X_ONWARD = [(4 * y + s, 4 * y + t) for y in range(4) for s, t in ONWARD]
Y_SWAP = [(4 * s + x, 4 * t + x) for x in range(4) for s, t in SWAP]
Y_ONWARD = [(4 * s + x, 4 * t + x) for x in range(4) for s, t in ONWARD]


def dot(a, b, ca, cb):
    return lax.dot_general(a, b, (((ca,), (cb,)), ((), ())), preferred_element_type=jnp.float32)


def kernel(count, info, q_ref, g_ref, *refs):
    k_refs, v_refs = refs[0:6], refs[6:12]
    dq_ref, out_refs = refs[-11], refs[-10:-4]
    w_s, ds_s, mask_s, tri_s = refs[-4:]
    bf = jnp.bfloat16
    row = lax.broadcasted_iota(jnp.int32, (R, D), 0)
    col = lax.broadcasted_iota(jnp.int32, (R, D), 1)

    @pl.when(pl.program_id(0) == 0)
    def _():
        tri_s[...] = jnp.where((col == 0) | (col > row), -BIG, 0.0).astype(bf)
        for t in range(2):
            for j in range(6):
                hot = (col == 0) & (row >= info[6 * t + j])
                if (t, j) in ((0, 0), (1, 5)):
                    hot = hot | ((col == row) & (col > 0))
                mask_s[t, j * R : (j + 1) * R, :] = jnp.where(hot, 1.0, 0.0).astype(bf)

    k = jnp.concatenate([r[...] for r in k_refs], axis=0)
    v = jnp.concatenate([r[...] for r in v_refs], axis=0)
    qs, gs = [], []
    for t in range(2):
        live = row < info[12 + t]
        heads = [slice(h * D, (h + 1) * D) for h in range(GROUP)]
        rows = slice(t * R, (t + 1) * R)
        qs.append(jnp.concatenate([q_ref[rows, h] for h in heads], axis=0))
        gs.append(
            jnp.concatenate([jnp.where(live, g_ref[rows, h], jnp.zeros((), bf)) for h in heads], axis=0)
        )
    tri = jnp.concatenate([tri_s[...]] * GROUP, axis=0)
    for t, places in ((0, 5), (1, 6)):
        n = places * R
        k_wide = jnp.concatenate([k[:n], mask_s[t, :n, :]], axis=1)
        q_wide = jnp.concatenate([qs[t], tri], axis=1)
        k_turned = k[:n].T
        for h0, h1 in ((0, 2), (2, 4), (4, 5)):
            part = slice(h0 * R, h1 * R)
            place = slice((t * GROUP + h0) * R, (t * GROUP + h1) * R)
            s = dot(k_wide, q_wide[part], 1, 1)
            dw = dot(v[:n], gs[t][part], 1, 1)
            m = jnp.max(s, axis=0, keepdims=True)
            e = jnp.exp2((s - m) * EXP2_SCALE)
            w = e * (1.0 / jnp.sum(e, axis=0, keepdims=True))
            delta = jnp.sum(w * dw, axis=0, keepdims=True)
            ds = (w * (dw - delta)).astype(bf)
            w_s[:n, place] = w.astype(bf)
            ds_s[:n, place] = ds
            dq = (dot(k_turned, ds, 1, 0) * SCALE).T
            for h in range(h0, h1):
                dq_ref[t * R : (t + 1) * R, h * D : (h + 1) * D] = dq[
                    (h - h0) * R : (h - h0 + 1) * R
                ].astype(bf)
    q_all = jnp.concatenate(qs, axis=0)
    g_all = jnp.concatenate(gs, axis=0)
    n = 5 * R
    dk = dot(ds_s[:n, :], q_all, 1, 0) * SCALE
    dv = dot(w_s[:n, :], g_all, 1, 0)
    i = pl.program_id(0)
    k_cols = pl.ds(pl.multiple_of(i * D, D), D)
    v_cols = pl.ds(pl.multiple_of((count + i) * D, D), D)
    for j in range(5):
        out_refs[j][:, k_cols] = dk[j * R : (j + 1) * R].astype(out_refs[j].dtype)
        out_refs[j][:, v_cols] = dv[j * R : (j + 1) * R].astype(out_refs[j].dtype)
    out_refs[5][:, k_cols] = (dot(ds_s[n:, GROUP * R :], qs[1], 1, 0) * SCALE).astype(bf)
    out_refs[5][:, v_cols] = dot(w_s[n:, GROUP * R :], gs[1], 1, 0).astype(bf)


def attend_backward(info, q, g, k_slots, v_slots, first, count, grad_queries):
    specs = [pl.BlockSpec((2 * R, GROUP * D), lambda i, _: (0, first + i))] * 2
    arrays = [q, g]
    for array, block, offset in k_slots + v_slots:
        specs.append(pl.BlockSpec((R, D), functools.partial(lambda b, o, i, _: (b, o + i), block, offset)))
        arrays.append(array)
    kinds = [jnp.float32] + [jnp.bfloat16] * 5
    aliases = {}
    if grad_queries is not None:
        aliases = {1 + len(arrays): 0}
        specs.append(pl.BlockSpec(memory_space=pl.ANY))
        arrays.append(grad_queries)
    return pl.pallas_call(
        functools.partial(kernel, count),
        input_output_aliases=aliases,
        out_shape=[jax.ShapeDtypeStruct(q.shape, jnp.bfloat16)]
        + [jax.ShapeDtypeStruct((R, count * 2 * D), kind) for kind in kinds],
        grid_spec=pltpu.PrefetchScalarGridSpec(
            num_scalar_prefetch=1,
            grid=(count,),
            in_specs=specs,
            out_specs=[pl.BlockSpec((2 * R, GROUP * D), lambda i, _: (0, first + i))]
            + [pl.BlockSpec((R, count * 2 * D), lambda i, _: (0, 0))] * 6,
            scratch_shapes=[
                pltpu.VMEM((6 * R, 2 * GROUP * R), jnp.bfloat16),
                pltpu.VMEM((6 * R, 2 * GROUP * R), jnp.bfloat16),
                pltpu.VMEM((2, 6 * R, D), jnp.bfloat16),
                pltpu.VMEM((R, D), jnp.bfloat16),
            ],
        ),
        compiler_params=pltpu.CompilerParams(vmem_limit_bytes=40 * 2**20),
        cost_estimate=pl.CostEstimate(
            flops=count * 3_000_000_000, bytes_accessed=count * 2**20, transcendentals=count * 900_000
        ),
    )(info, *arrays)


def neighbours(x):
    swap = x ^ 1
    onward = jnp.where(x < 2, 2, 0)
    return swap, onward


def place_of(index):
    place = jnp.zeros_like(index)
    for bit in (3, 2, 1, 0):
        place = jnp.where((index >> bit) & 1 == 1, 4 - bit, place)
    return place


def shards(queries, keys, values, out_grad, seg_lengths):
    me = lax.axis_index("leaf")
    x, y = me & 3, me >> 2
    x_even, y_even = (x & 1) == 0, (y & 1) == 0
    x_swap, x_on = neighbours(x)
    y_swap, y_on = neighbours(y)
    ids = jnp.stack([me, 4 * y + x_swap, 4 * y + x_on, 4 * y_swap, 4 * y_on, me])
    lengths = jnp.take(seg_lengths[:, 0], ids).at[5].set(jnp.take(seg_lengths[:, 1], me))
    my_place = place_of(me)
    inner_limit = jnp.where((place_of(ids) < my_place) | (ids == me), lengths, 0)
    info = jnp.concatenate([inner_limit, lengths, lengths[:1], lengths[5:], jnp.zeros((2,), jnp.int32)])

    q = queries.reshape(2 * R, -1)
    g = out_grad.reshape(2 * R, -1)
    keys2, values2 = keys.reshape(2 * R, -1), values.reshape(2 * R, -1)

    def permute(array, pairs):
        return lax.ppermute(array, "leaf", pairs)

    grad_queries = None
    inner, leaf = [], []
    first = 0
    for count in CHUNKS:
        cols = slice(first * D, (first + count) * D)
        own = jnp.concatenate([keys2[:R, cols], values2[:R, cols]], axis=1)
        a = permute(own, X_SWAP)
        b = permute(jnp.where(x_even, own, a), X_ONWARD)
        upper = jnp.where(x == 0, own, jnp.where(x == 1, a, b))
        c = permute(upper, Y_SWAP)
        d = permute(jnp.where(y_even, upper, c), Y_ONWARD)
        got = [a, b, c, d]
        k_slots = [(keys2, 0, first)] + [(s, 0, 0) for s in got] + [(keys2, 1, first)]
        v_slots = [(values2, 0, first)] + [(s, 0, count) for s in got] + [(values2, 1, first)]
        grad_queries, g_own, g_a, g_b, g_c, g_d, g_leaf = attend_backward(
            info, q, g, k_slots, v_slots, first, count, grad_queries
        )
        f32, bf = jnp.float32, jnp.bfloat16
        back = permute(g_d, Y_ONWARD).astype(f32)
        up = jnp.where(y_even, back, 0.0)
        back2 = permute((g_c.astype(f32) + jnp.where(y_even, 0.0, back)).astype(bf), Y_SWAP).astype(f32)
        up = up + back2
        g_own = g_own + jnp.where(x == 0, up, 0.0)
        g_a = g_a.astype(f32) + jnp.where(x == 1, up, 0.0)
        g_b = g_b.astype(f32) + jnp.where(x >= 2, up, 0.0)
        back = permute(g_b.astype(bf), X_ONWARD).astype(f32)
        back2 = permute((g_a + jnp.where(x_even, 0.0, back)).astype(bf), X_SWAP).astype(f32)
        g_own = g_own + jnp.where(x_even, back, 0.0) + back2
        inner.append(g_own.astype(bf))
        leaf.append(g_leaf)
        first += count

    def assemble(half):
        rows = []
        for pieces in (inner, leaf):
            cut = [p[:, half * c * D : (half + 1) * c * D] for p, c in zip(pieces, CHUNKS)]
            rows.append(jnp.concatenate(cut, axis=1))
        return jnp.stack(rows)[None]

    return grad_queries.reshape(queries.shape), assemble(0), assemble(1)


def solution(mesh):
    rows = P(("prompt", "leaf"), None, None, None)
    return jax.shard_map(
        shards,
        mesh=mesh,
        in_specs=(rows, rows, rows, rows, P("prompt", None)),
        out_specs=(rows, rows, rows),
        check_vma=False,
    )
```

time: 431 us -> 126 us (0.29)
  matrix products: 120 us -> 0 us
  waiting for transfers between devices: 157 us -> 46.4 us
  local copies, waits for them, and re-layouts: 94.6 us -> 7.05 us
  Pallas kernels: 0 us -> 43.6 us
  other arithmetic: 39.9 us -> 4.09 us
  starting transfers between devices: 0.08 us -> 23.9 us
  between operations: 14.3 us -> 0.88 us
    unnamed x3 -> x0, waiting for transfers between devices: 105 us -> none
    dot_general x40 -> x0, matrix products: 85.8 us -> none  [the longest x8 22.8 us: per_group(): jnp.einsum('grc,cd->rgd', score_half, key_group, preferred_element_type=j...]
    all_gather x1 -> x0, waiting for transfers between devices: 52.3 us -> none  [shards(): all_inner = lax.all_gather(kv_inner[None], 'leaf', axis=0, tiled=True)]
    ppermute x0 -> x16, waiting for transfers between devices: none -> 46.4 us  [permute(): return lax.ppermute(array, 'leaf', pairs)]
    pallas_call x0 -> x2, Pallas kernels: none -> 43.6 us  [attend_backward(): pl.pallas_call(functools.partial(kernel, count), input_output_aliases=ali...]
    sub x8 -> x0, matrix products: 34.5 us -> none  [per_group(): exponent = jnp.exp(scores - highest)]
    ppermute x0 -> x16, starting transfers between devices: none -> 23.9 us  [permute(): return lax.ppermute(array, 'leaf', pairs)]
    convert_element_type x8, other arithmetic: 20.7 us -> 1.28 us  [the longest x2 0.45 us: shards(): inner.append(g_own.astype(bf))]
  transfers between devices with their start and end apart: 2 -> 16, of which waited for: 2 -> 10; matrix products, arithmetic and copies ran while one was open for 9% -> 4% of each run, Pallas kernels for 0% -> 35%
where the time goes in v1:
time: 126 us
  waiting for transfers between devices  46.4 us (37%)
  Pallas kernels  43.6 us (35%)
  starting transfers between devices  23.9 us (19%)
  local copies, waits for them, and re-layouts  7.05 us (6%)
  other arithmetic  4.09 us (3%)
    ppermute x16, waiting for transfers between devices, permute(): return lax.ppermute(array, 'leaf', pairs)  46.4 us
    pallas_call x2, Pallas kernels, attend_backward(): pl.pallas_call(functools.partial(kernel, count), input_output_aliases=ali...  43.6 us
    ppermute x16, starting transfers between devices, permute(): return lax.ppermute(array, 'leaf', pairs)  23.9 us
    unnamed x8, local copies, waits for them, and re-layouts  3.49 us
  transfers between devices with their start and end apart: 16, of which 10 were waited for; matrix products, arithmetic and copies ran while one was open for 4% of the time, Pallas kernels for 35%

profile of v1, /device:TPU:128, one launch (start us, length us, event | category | flops | bytes accessed | tf_op | source)
XLA Modules:
  0.0 126.0 jit_solution(154904645159605407)
XLA Ops:
  0.6 1.1 fusion.17
  1.8 1.6 %collective-permute-start = (bf16[128,1024]{1,0:T(8,128)(2,1)S(1)}, bf16[128,1024]{1,0:T(8,128)(2,1)S(1)}, u32[]{:S(2)}, u32[]{:S(2)}) collective-permute-start(bf16[128,1024]{1,0:T(8,128)(2,1)S(1)} %pad_maximum_fusion), channel_id=1, source_target_pairs={{0,1},{1,0},{2,3},{3,2},{4,5},{5,4},{6,7},{7,6},{8,9},{9,8},{10,11... | collective-permute-start | bytes 786440 | tf_op jit(solution)/shard_map/ppermute | solution.py:166
  3.4 0.6 collective-permute-start.4
  4.0 0.1 stack.60
  4.1 0.8 fusion.23
  4.9 10.7 %collective-permute-done.4.refs_1_.refs_7_ = bf16[128,1024]{1,0:T(8,128)(2,1)S(1)} collective-permute-done((bf16[128,1024]{1,0:T(8,128)(2,1)S(1)}, bf16[128,1024]{1,0:T(8,128)(2,1)S(1)}, u32[]{:S(2)}, u32[]{:S(2)}) %collective-permute-start.4) | collective-permute-done | bytes 262176 | tf_op jit(solution)/shard_map/ppermute | solution.py:166
  15.6 2.8 %collective-permute-start.5 = (bf16[128,1024]{1,0:T(8,128)(2,1)S(1)}, bf16[128,1024]{1,0:T(8,128)(2,1)S(1)}, u32[]{:S(2)}, u32[]{:S(2)}) collective-permute-start(bf16[128,1024]{1,0:T(8,128)(2,1)S(1)} %broadcast_select_fusion.2), channel_id=1, source_target_pairs={{0,3},{1,2},{2,1},{3,0},{4,7},{5,6},{6,5},{7,4},{8,11},{9,10},{10,... | collective-permute-start | bytes 786440 | tf_op jit(solution)/shard_map/ppermute | solution.py:166
  18.5 0.6 gather_fusion
  19.1 0.1 stack.54
  19.3 0.6 collective-permute-start.1
  19.9 6.3 %collective-permute-done.5.refs_2_.refs_8_ = bf16[128,1024]{1,0:T(8,128)(2,1)S(1)} collective-permute-done((bf16[128,1024]{1,0:T(8,128)(2,1)S(1)}, bf16[128,1024]{1,0:T(8,128)(2,1)S(1)}, u32[]{:S(2)}, u32[]{:S(2)}) %collective-permute-start.5) | collective-permute-done | bytes 262176 | tf_op jit(solution)/shard_map/ppermute | solution.py:166
  26.2 0.1 select_select_fusion
  26.3 1.7 %collective-permute-start.6 = (bf16[128,1024]{1,0:T(8,128)(2,1)S(1)}, bf16[128,1024]{1,0:T(8,128)(2,1)S(1)}, u32[]{:S(2)}, u32[]{:S(2)}) collective-permute-start(bf16[128,1024]{1,0:T(8,128)(2,1)S(1)} %select_select_fusion), channel_id=1, source_target_pairs={{0,4},{4,0},{8,12},{12,8},{1,5},{5,1},{9,13},{13,9},{2,6},{6,2},{1... | collective-permute-start | bytes 786440 | tf_op jit(solution)/shard_map/ppermute | solution.py:166
  28.0 0.6 constant_dynamic-update-slice_fusion
  28.5 1.2 collective-permute-done.1.refs_2_.refs_8_
  29.7 0.1 select_select_fusion.1
  29.8 1.7 %collective-permute-start.2 = (bf16[128,1024]{1,0:T(8,128)(2,1)S(1)}, bf16[128,1024]{1,0:T(8,128)(2,1)S(1)}, u32[]{:S(2)}, u32[]{:S(2)}) collective-permute-start(bf16[128,1024]{1,0:T(8,128)(2,1)S(1)} %select_select_fusion.1), channel_id=1, source_target_pairs={{0,4},{4,0},{8,12},{12,8},{1,5},{5,1},{9,13},{13,9},{2,6},{6,2},{1... | collective-permute-start | bytes 786440 | tf_op jit(solution)/shard_map/ppermute | solution.py:166
  31.5 3.5 %collective-permute-done.6.refs_3_.refs_9_ = bf16[128,1024]{1,0:T(8,128)(2,1)S(1)} collective-permute-done((bf16[128,1024]{1,0:T(8,128)(2,1)S(1)}, bf16[128,1024]{1,0:T(8,128)(2,1)S(1)}, u32[]{:S(2)}, u32[]{:S(2)}) %collective-permute-start.6) | collective-permute-done | bytes 262176 | tf_op jit(solution)/shard_map/ppermute | solution.py:166
  35.0 3.1 %collective-permute-start.7 = (bf16[128,1024]{1,0:T(8,128)(2,1)S(1)}, bf16[128,1024]{1,0:T(8,128)(2,1)S(1)}, u32[]{:S(2)}, u32[]{:S(2)}) collective-permute-start(bf16[128,1024]{1,0:T(8,128)(2,1)S(1)} %broadcast_select_fusion), channel_id=1, source_target_pairs={{0,12},{4,8},{8,4},{12,0},{1,13},{5,9},{9,5},{13,1},{2,14},{6,10},... | collective-permute-start | bytes 786440 | tf_op jit(solution)/shard_map/ppermute | solution.py:166
  38.2 0.8 concatenate.44.info
  39.0 2.6 %collective-permute-start.3 = (bf16[128,1024]{1,0:T(8,128)(2,1)S(1)}, bf16[128,1024]{1,0:T(8,128)(2,1)S(1)}, u32[]{:S(2)}, u32[]{:S(2)}) collective-permute-start(bf16[128,1024]{1,0:T(8,128)(2,1)S(1)} %broadcast_select_fusion.1), channel_id=1, source_target_pairs={{0,12},{4,8},{8,4},{12,0},{1,13},{5,9},{9,5},{13,1},{2,14},{6,10},... | collective-permute-start | bytes 786440 | tf_op jit(solution)/shard_map/ppermute | solution.py:166
  41.5 3.7 %collective-permute-done.7.refs_4_.refs_10_ = bf16[128,1024]{1,0:T(8,128)(2,1)S(1)} collective-permute-done((bf16[128,1024]{1,0:T(8,128)(2,1)S(1)}, bf16[128,1024]{1,0:T(8,128)(2,1)S(1)}, u32[]{:S(2)}, u32[]{:S(2)}) %collective-permute-start.7) | collective-permute-done | bytes 262176 | tf_op jit(solution)/shard_map/ppermute | solution.py:166
  45.2 1.7 %copy-done.2 = bf16[1,2,128,5120]{3,2,1,0:T(8,128)(2,1)S(1)} copy-done((bf16[1,2,128,5120]{3,2,1,0:T(8,128)(2,1)S(1)}, bf16[1,2,128,5120]{3,2,1,0:T(8,128)(2,1)}, u32[]{:S(2)}) %copy-start.2) | copy-done | bytes 2621464
  46.9 1.7 %copy-done.3 = bf16[1,2,128,5120]{3,2,1,0:T(8,128)(2,1)S(1)} copy-done((bf16[1,2,128,5120]{3,2,1,0:T(8,128)(2,1)S(1)}, bf16[1,2,128,5120]{3,2,1,0:T(8,128)(2,1)}, u32[]{:S(2)}) %copy-start.3) | copy-done | bytes 2621464
  48.6 21.8 %shard_map.76 = (bf16[256,5120]{1,0:T(8,128)(2,1)}, f32[128,1024]{1,0:T(8,128)S(1)}, bf16[128,1024]{1,0:T(8,128)(2,1)S(1)}, bf16[128,1024]{1,0:T(8,128)(2,1)S(1)...) custom-call(s32[16]{0:T(128)S(1)} %concatenate.44.info, ...), custom_call_target="tpu_custom_call" | custom-call | flops 12000000000 | bytes 4194304 | tf_op jit(solution)/shard_map/pallas_call | solution.py:111
  70.5 3.1 %collective-permute-start.8 = (bf16[128,1024]{1,0:T(8,128)(2,1)S(1)}, bf16[128,1024]{1,0:T(8,128)(2,1)S(1)}, u32[]{:S(2)}, u32[]{:S(2)}) collective-permute-start(bf16[128,1024]{1,0:T(8,128)(2,1)S(1)} %get-tuple-element.32), channel_id=1, source_target_pairs={{0,12},{4,8},{8,4},{12,0},{1,13},{5,9},{9,5},{13,1},{2,14},{6,10},... | collective-permute-start | bytes 786440 | tf_op jit(solution)/shard_map/ppermute | solution.py:166
  73.5 21.8 %shard_map.77 = (bf16[256,5120]{1,0:T(8,128)(2,1)}, f32[128,1024]{1,0:T(8,128)S(1)}, bf16[128,1024]{1,0:T(8,128)(2,1)S(1)}, bf16[128,1024]{1,0:T(8,128)(2,1)S(1)...) custom-call(s32[16]{0:T(128)S(1)} %concatenate.44.info, ...), custom_call_target="tpu_custom_call", output_to_operand_aliasing={{0}: (15, {})} | custom-call | flops 12000000000 | bytes 4194304 | tf_op jit(solution)/shard_map/pallas_call | solution.py:111
  95.4 0.2 collective-permute-start.12
  95.6 0.1 fusion.2
  95.6 0.1 collective-permute-start.9
  95.8 7.2 %collective-permute-done.12 = bf16[128,1024]{1,0:T(8,128)(2,1)S(1)} collective-permute-done((bf16[128,1024]{1,0:T(8,128)(2,1)S(1)}, bf16[128,1024]{1,0:T(8,128)(2,1)S(1)}, u32[]{:S(2)}, u32[]{:S(2)}) %collective-permute-start.12) | collective-permute-done | bytes 262176 | tf_op jit(solution)/shard_map/ppermute | solution.py:166
  103.0 0.1 collective-permute-start.13
  103.1 0.1 add_convert_fusion.1
  103.3 2.8 %collective-permute-start.10 = (bf16[128,1024]{1,0:T(8,128)(2,1)S(1)}, bf16[128,1024]{1,0:T(8,128)(2,1)S(1)}, u32[]{:S(2)}, u32[]{:S(2)}) collective-permute-start(bf16[128,1024]{1,0:T(8,128)(2,1)S(1)} %add_convert_fusion.1), channel_id=1, source_target_pairs={{0,3},{1,2},{2,1},{3,0},{4,7},{5,6},{6,5},{7,4},{8,11},{9,10},{10,... | collective-permute-start | bytes 786440 | tf_op jit(solution)/shard_map/ppermute | solution.py:166
  106.2 3.3 %collective-permute-done.13 = bf16[128,1024]{1,0:T(8,128)(2,1)S(1)} collective-permute-done((bf16[128,1024]{1,0:T(8,128)(2,1)S(1)}, bf16[128,1024]{1,0:T(8,128)(2,1)S(1)}, u32[]{:S(2)}, u32[]{:S(2)}) %collective-permute-start.13) | collective-permute-done | bytes 262176 | tf_op jit(solution)/shard_map/ppermute | solution.py:166
  109.5 0.1 add_convert_fusion
  109.6 2.8 %collective-permute-start.14 = (bf16[128,1024]{1,0:T(8,128)(2,1)S(1)}, bf16[128,1024]{1,0:T(8,128)(2,1)S(1)}, u32[]{:S(2)}, u32[]{:S(2)}) collective-permute-start(bf16[128,1024]{1,0:T(8,128)(2,1)S(1)} %add_convert_fusion), channel_id=1, source_target_pairs={{0,3},{1,2},{2,1},{3,0},{4,7},{5,6},{6,5},{7,4},{8,11},{9,10},{10,... | collective-permute-start | bytes 786440 | tf_op jit(solution)/shard_map/ppermute | solution.py:166
  112.5 0.2 fusion.7
  112.7 0.1 collective-permute-start.11
  112.8 4.5 %collective-permute-done.14 = bf16[128,1024]{1,0:T(8,128)(2,1)S(1)} collective-permute-done((bf16[128,1024]{1,0:T(8,128)(2,1)S(1)}, bf16[128,1024]{1,0:T(8,128)(2,1)S(1)}, u32[]{:S(2)}, u32[]{:S(2)}) %collective-permute-start.14) | collective-permute-done | bytes 262176 | tf_op jit(solution)/shard_map/ppermute | solution.py:166
  117.3 0.2 fusion.15
  117.5 0.1 collective-permute-start.15
  117.6 1.5 %collective-permute-done.11 = bf16[128,1024]{1,0:T(8,128)(2,1)S(1)} collective-permute-done((bf16[128,1024]{1,0:T(8,128)(2,1)S(1)}, bf16[128,1024]{1,0:T(8,128)(2,1)S(1)}, u32[]{:S(2)}, u32[]{:S(2)}) %collective-permute-start.11) | collective-permute-done | bytes 262176 | tf_op jit(solution)/shard_map/ppermute | solution.py:166
  119.1 0.2 fusion.5
  119.4 4.6 %collective-permute-done.15 = bf16[128,1024]{1,0:T(8,128)(2,1)S(1)} collective-permute-done((bf16[128,1024]{1,0:T(8,128)(2,1)S(1)}, bf16[128,1024]{1,0:T(8,128)(2,1)S(1)}, u32[]{:S(2)}, u32[]{:S(2)}) %collective-permute-start.15) | collective-permute-done | bytes 262176 | tf_op jit(solution)/shard_map/ppermute | solution.py:166
  124.0 0.2 fusion.13
  124.2 0.8 maximum_bitcast_fusion.1
  125.1 0.8 maximum_bitcast_fusion
  (32 shorter events, 0.5 us)
Async XLA Ops:
  1.8 17.4 %collective-permute-start = (bf16[128,1024]{1,0:T(8,128)(2,1)S(1)}, bf16[128,1024]{1,0:T(8,128)(2,1)S(1)}, u32[]{:S(2)}, u32[]{:S(2)}) collective-permute-start(bf16[128,1024]{1,0:T(8,128)(2,1)S(1)} %pad_maximum_fusion), channel_id=1, source_target_pairs={{0,1},{1,0},{2,3},{3,2},{4,5},{5,4},{6,7},{7,6},{8,9},{9,8},{10,11... | collective-permute-start | bytes 786440 | tf_op jit(solution)/shard_map/ppermute | solution.py:166
  3.4 12.1 %collective-permute-start.4 = (bf16[128,1024]{1,0:T(8,128)(2,1)S(1)}, bf16[128,1024]{1,0:T(8,128)(2,1)S(1)}, u32[]{:S(2)}, u32[]{:S(2)}) collective-permute-start(bf16[128,1024]{1,0:T(8,128)(2,1)S(1)} %pad_maximum_fusion.1), channel_id=1, source_target_pairs={{0,1},{1,0},{2,3},{3,2},{4,5},{5,4},{6,7},{7,6},{8,9},{9,8},{10,11... | collective-permute-start | bytes 786440 | tf_op jit(solution)/shard_map/ppermute | solution.py:166
  15.6 29.5 %copy-start = (bf16[1,2,128,1024]{3,2,1,0:T(8,128)(2,1)S(1)}, bf16[1,2,128,1024]{3,2,1,0:T(8,128)(2,1)}, u32[]{:S(2)}) copy-start(bf16[1,2,128,1024]{3,2,1,0:T(8,128)(2,1)} %param.8) | copy-start | bytes 1572868
  15.6 29.5 %copy-start.1 = (bf16[1,2,128,1024]{3,2,1,0:T(8,128)(2,1)S(1)}, bf16[1,2,128,1024]{3,2,1,0:T(8,128)(2,1)}, u32[]{:S(2)}) copy-start(bf16[1,2,128,1024]{3,2,1,0:T(8,128)(2,1)} %param.9) | copy-start | bytes 1572868
  15.6 10.5 %collective-permute-start.5 = (bf16[128,1024]{1,0:T(8,128)(2,1)S(1)}, bf16[128,1024]{1,0:T(8,128)(2,1)S(1)}, u32[]{:S(2)}, u32[]{:S(2)}) collective-permute-start(bf16[128,1024]{1,0:T(8,128)(2,1)S(1)} %broadcast_select_fusion.2), channel_id=1, source_target_pairs={{0,3},{1,2},{2,1},{3,0},{4,7},{5,6},{6,5},{7,4},{8,11},{9,10},{10,... | collective-permute-start | bytes 786440 | tf_op jit(solution)/shard_map/ppermute | solution.py:166
  19.3 10.4 %collective-permute-start.1 = (bf16[128,1024]{1,0:T(8,128)(2,1)S(1)}, bf16[128,1024]{1,0:T(8,128)(2,1)S(1)}, u32[]{:S(2)}, u32[]{:S(2)}) collective-permute-start(bf16[128,1024]{1,0:T(8,128)(2,1)S(1)} %broadcast_select_fusion.3), channel_id=1, source_target_pairs={{0,3},{1,2},{2,1},{3,0},{4,7},{5,6},{6,5},{7,4},{8,11},{9,10},{10,... | collective-permute-start | bytes 786440 | tf_op jit(solution)/shard_map/ppermute | solution.py:166
  26.3 8.7 %collective-permute-start.6 = (bf16[128,1024]{1,0:T(8,128)(2,1)S(1)}, bf16[128,1024]{1,0:T(8,128)(2,1)S(1)}, u32[]{:S(2)}, u32[]{:S(2)}) collective-permute-start(bf16[128,1024]{1,0:T(8,128)(2,1)S(1)} %select_select_fusion), channel_id=1, source_target_pairs={{0,4},{4,0},{8,12},{12,8},{1,5},{5,1},{9,13},{13,9},{2,6},{6,2},{1... | collective-permute-start | bytes 786440 | tf_op jit(solution)/shard_map/ppermute | solution.py:166
  29.8 9.1 %collective-permute-start.2 = (bf16[128,1024]{1,0:T(8,128)(2,1)S(1)}, bf16[128,1024]{1,0:T(8,128)(2,1)S(1)}, u32[]{:S(2)}, u32[]{:S(2)}) collective-permute-start(bf16[128,1024]{1,0:T(8,128)(2,1)S(1)} %select_select_fusion.1), channel_id=1, source_target_pairs={{0,4},{4,0},{8,12},{12,8},{1,5},{5,1},{9,13},{13,9},{2,6},{6,2},{1... | collective-permute-start | bytes 786440 | tf_op jit(solution)/shard_map/ppermute | solution.py:166
  35.0 10.1 %collective-permute-start.7 = (bf16[128,1024]{1,0:T(8,128)(2,1)S(1)}, bf16[128,1024]{1,0:T(8,128)(2,1)S(1)}, u32[]{:S(2)}, u32[]{:S(2)}) collective-permute-start(bf16[128,1024]{1,0:T(8,128)(2,1)S(1)} %broadcast_select_fusion), channel_id=1, source_target_pairs={{0,12},{4,8},{8,4},{12,0},{1,13},{5,9},{9,5},{13,1},{2,14},{6,10},... | collective-permute-start | bytes 786440 | tf_op jit(solution)/shard_map/ppermute | solution.py:166
  39.0 34.6 %collective-permute-start.3 = (bf16[128,1024]{1,0:T(8,128)(2,1)S(1)}, bf16[128,1024]{1,0:T(8,128)(2,1)S(1)}, u32[]{:S(2)}, u32[]{:S(2)}) collective-permute-start(bf16[128,1024]{1,0:T(8,128)(2,1)S(1)} %broadcast_select_fusion.1), channel_id=1, source_target_pairs={{0,12},{4,8},{8,4},{12,0},{1,13},{5,9},{9,5},{13,1},{2,14},{6,10},... | collective-permute-start | bytes 786440 | tf_op jit(solution)/shard_map/ppermute | solution.py:166
  45.2 1.7 %copy-start.2 = (bf16[1,2,128,5120]{3,2,1,0:T(8,128)(2,1)S(1)}, bf16[1,2,128,5120]{3,2,1,0:T(8,128)(2,1)}, u32[]{:S(2)}) copy-start(bf16[1,2,128,5120]{3,2,1,0:T(8,128)(2,1)} %param.7) | copy-start | bytes 7864324
  46.9 1.7 %copy-start.3 = (bf16[1,2,128,5120]{3,2,1,0:T(8,128)(2,1)S(1)}, bf16[1,2,128,5120]{3,2,1,0:T(8,128)(2,1)}, u32[]{:S(2)}) copy-start(bf16[1,2,128,5120]{3,2,1,0:T(8,128)(2,1)} %param.10) | copy-start | bytes 7864324
  70.5 25.1 %collective-permute-start.8 = (bf16[128,1024]{1,0:T(8,128)(2,1)S(1)}, bf16[128,1024]{1,0:T(8,128)(2,1)S(1)}, u32[]{:S(2)}, u32[]{:S(2)}) collective-permute-start(bf16[128,1024]{1,0:T(8,128)(2,1)S(1)} %get-tuple-element.32), channel_id=1, source_target_pairs={{0,12},{4,8},{8,4},{12,0},{1,13},{5,9},{9,5},{13,1},{2,14},{6,10},... | collective-permute-start | bytes 786440 | tf_op jit(solution)/shard_map/ppermute | solution.py:166
  95.4 7.6 %collective-permute-start.12 = (bf16[128,1024]{1,0:T(8,128)(2,1)S(1)}, bf16[128,1024]{1,0:T(8,128)(2,1)S(1)}, u32[]{:S(2)}, u32[]{:S(2)}) collective-permute-start(bf16[128,1024]{1,0:T(8,128)(2,1)S(1)} %get-tuple-element.37), channel_id=1, source_target_pairs={{0,12},{4,8},{8,4},{12,0},{1,13},{5,9},{9,5},{13,1},{2,14},{6,10},... | collective-permute-start | bytes 786440 | tf_op jit(solution)/shard_map/ppermute | solution.py:166
  95.6 7.5 %collective-permute-start.9 = (bf16[128,1024]{1,0:T(8,128)(2,1)S(1)}, bf16[128,1024]{1,0:T(8,128)(2,1)S(1)}, u32[]{:S(2)}, u32[]{:S(2)}) collective-permute-start(bf16[128,1024]{1,0:T(8,128)(2,1)S(1)} %fusion.2), channel_id=1, source_target_pairs={{0,4},{4,0},{8,12},{12,8},{1,5},{5,1},{9,13},{13,9},{2,6},{6,2},{1... | collective-permute-start | bytes 786440 | tf_op jit(solution)/shard_map/ppermute | solution.py:166
  103.0 6.5 %collective-permute-start.13 = (bf16[128,1024]{1,0:T(8,128)(2,1)S(1)}, bf16[128,1024]{1,0:T(8,128)(2,1)S(1)}, u32[]{:S(2)}, u32[]{:S(2)}) collective-permute-start(bf16[128,1024]{1,0:T(8,128)(2,1)S(1)} %fusion.10), channel_id=1, source_target_pairs={{0,4},{4,0},{8,12},{12,8},{1,5},{5,1},{9,13},{13,9},{2,6},{6,2},{1... | collective-permute-start | bytes 786440 | tf_op jit(solution)/shard_map/ppermute | solution.py:166
  103.3 9.2 %collective-permute-start.10 = (bf16[128,1024]{1,0:T(8,128)(2,1)S(1)}, bf16[128,1024]{1,0:T(8,128)(2,1)S(1)}, u32[]{:S(2)}, u32[]{:S(2)}) collective-permute-start(bf16[128,1024]{1,0:T(8,128)(2,1)S(1)} %add_convert_fusion.1), channel_id=1, source_target_pairs={{0,3},{1,2},{2,1},{3,0},{4,7},{5,6},{6,5},{7,4},{8,11},{9,10},{10,... | collective-permute-start | bytes 786440 | tf_op jit(solution)/shard_map/ppermute | solution.py:166
  109.6 7.7 %collective-permute-start.14 = (bf16[128,1024]{1,0:T(8,128)(2,1)S(1)}, bf16[128,1024]{1,0:T(8,128)(2,1)S(1)}, u32[]{:S(2)}, u32[]{:S(2)}) collective-permute-start(bf16[128,1024]{1,0:T(8,128)(2,1)S(1)} %add_convert_fusion), channel_id=1, source_target_pairs={{0,3},{1,2},{2,1},{3,0},{4,7},{5,6},{6,5},{7,4},{8,11},{9,10},{10,... | collective-permute-start | bytes 786440 | tf_op jit(solution)/shard_map/ppermute | solution.py:166
  112.7 6.5 %collective-permute-start.11 = (bf16[128,1024]{1,0:T(8,128)(2,1)S(1)}, bf16[128,1024]{1,0:T(8,128)(2,1)S(1)}, u32[]{:S(2)}, u32[]{:S(2)}) collective-permute-start(bf16[128,1024]{1,0:T(8,128)(2,1)S(1)} %fusion.7), channel_id=1, source_target_pairs={{0,1},{1,0},{2,3},{3,2},{4,5},{5,4},{6,7},{7,6},{8,9},{9,8},{10,11... | collective-permute-start | bytes 786440 | tf_op jit(solution)/shard_map/ppermute | solution.py:166
  117.5 6.5 %collective-permute-start.15 = (bf16[128,1024]{1,0:T(8,128)(2,1)S(1)}, bf16[128,1024]{1,0:T(8,128)(2,1)S(1)}, u32[]{:S(2)}, u32[]{:S(2)}) collective-permute-start(bf16[128,1024]{1,0:T(8,128)(2,1)S(1)} %fusion.15), channel_id=1, source_target_pairs={{0,1},{1,0},{2,3},{3,2},{4,5},{5,4},{6,7},{7,6},{8,9},{9,8},{10,11... | collective-permute-start | bytes 786440 | tf_op jit(solution)/shard_map/ppermute | solution.py:166

commit v2 on v1

--- a/solution.py
+++ b/solution.py
@@ -15,7 +15,7 @@
 BIG = 2.0**30
 SCALE = 1.0 / math.sqrt(D)
 EXP2_SCALE = SCALE * math.log2(math.e)
-CHUNKS = (4, 4)
+CHUNKS = (3, 3, 2)
 
 SWAP = ((0, 1), (1, 0), (2, 3), (3, 2))
 ONWARD = ((0, 3), (1, 2), (2, 1), (3, 0))
@@ -59,41 +59,61 @@
             jnp.concatenate([jnp.where(live, g_ref[rows, h], jnp.zeros((), bf)) for h in heads], axis=0)
         )
     tri = jnp.concatenate([tri_s[...]] * GROUP, axis=0)
-    for t, places in ((0, 5), (1, 6)):
-        n = places * R
-        k_wide = jnp.concatenate([k[:n], mask_s[t, :n, :]], axis=1)
-        q_wide = jnp.concatenate([qs[t], tri], axis=1)
-        k_turned = k[:n].T
-        for h0, h1 in ((0, 2), (2, 4), (4, 5)):
-            part = slice(h0 * R, h1 * R)
-            place = slice((t * GROUP + h0) * R, (t * GROUP + h1) * R)
-            s = dot(k_wide, q_wide[part], 1, 1)
-            dw = dot(v[:n], gs[t][part], 1, 1)
-            m = jnp.max(s, axis=0, keepdims=True)
-            e = jnp.exp2((s - m) * EXP2_SCALE)
-            w = e * (1.0 / jnp.sum(e, axis=0, keepdims=True))
-            delta = jnp.sum(w * dw, axis=0, keepdims=True)
-            ds = (w * (dw - delta)).astype(bf)
-            w_s[:n, place] = w.astype(bf)
-            ds_s[:n, place] = ds
-            dq = (dot(k_turned, ds, 1, 0) * SCALE).T
-            for h in range(h0, h1):
-                dq_ref[t * R : (t + 1) * R, h * D : (h + 1) * D] = dq[
-                    (h - h0) * R : (h - h0 + 1) * R
-                ].astype(bf)
-    q_all = jnp.concatenate(qs, axis=0)
-    g_all = jnp.concatenate(gs, axis=0)
+    sizes = (5 * R, 6 * R)
+    k_wide = [jnp.concatenate([k[:n], mask_s[t, :n, :]], axis=1) for t, n in enumerate(sizes)]
+    q_wide = [jnp.concatenate([qs[t], tri], axis=1) for t in range(2)]
+    k_turned = k.T
+
+    def products(t, h0, h1):
+        n, part = sizes[t], slice(h0 * R, h1 * R)
+        return dot(k_wide[t], q_wide[t][part], 1, 1), dot(v[:n], gs[t][part], 1, 1)
+
+    def softmax_backward(t, h0, h1, s, dw):
+        n, place = sizes[t], slice((t * GROUP + h0) * R, (t * GROUP + h1) * R)
+        m = jnp.max(s, axis=0, keepdims=True)
+        e = jnp.exp2((s - m) * EXP2_SCALE)
+        w = e * (1.0 / jnp.sum(e, axis=0, keepdims=True))
+        delta = jnp.sum(w * dw, axis=0, keepdims=True)
+        w_s[:n, place] = w.astype(bf)
+        ds_s[:n, place] = (w * (dw - delta)).astype(bf)
+
+    total = {}
+
+    def gradients(t, h0, h1):
+        n, place = sizes[t], slice((t * GROUP + h0) * R, (t * GROUP + h1) * R)
+        part = slice(h0 * R, h1 * R)
+        ds = ds_s[:n, place]
+        for name, term in (
+            (("k", t), dot(ds, qs[t][part], 1, 0)),
+            (("v", t), dot(w_s[:n, place], gs[t][part], 1, 0)),
+        ):
+            total[name] = term if name not in total else total[name] + term
+        dq = (dot(k_turned[:, :n], ds, 1, 0) * SCALE).T
+        for h in range(h0, h1):
+            dq_ref[t * R : (t + 1) * R, h * D : (h + 1) * D] = dq[
+                (h - h0) * R : (h - h0 + 1) * R
+            ].astype(bf)
+
+    todo = [(t, h0, h1) for t in range(2) for h0, h1 in ((0, 2), (2, 4), (4, 5))]
+    ahead = products(*todo[0])
+    for step, part in enumerate(todo):
+        now = ahead
+        if step + 1 < len(todo):
+            ahead = products(*todo[step + 1])
+        if step:
+            gradients(*todo[step - 1])
+        softmax_backward(*part, *now)
+    gradients(*todo[-1])
+
+    i = pl.program_id(0)
     n = 5 * R
-    dk = dot(ds_s[:n, :], q_all, 1, 0) * SCALE
-    dv = dot(w_s[:n, :], g_all, 1, 0)
-    i = pl.program_id(0)
-    k_cols = pl.ds(pl.multiple_of(i * D, D), D)
-    v_cols = pl.ds(pl.multiple_of((count + i) * D, D), D)
-    for j in range(5):
-        out_refs[j][:, k_cols] = dk[j * R : (j + 1) * R].astype(out_refs[j].dtype)
-        out_refs[j][:, v_cols] = dv[j * R : (j + 1) * R].astype(out_refs[j].dtype)
-    out_refs[5][:, k_cols] = (dot(ds_s[n:, GROUP * R :], qs[1], 1, 0) * SCALE).astype(bf)
-    out_refs[5][:, v_cols] = dot(w_s[n:, GROUP * R :], gs[1], 1, 0).astype(bf)
+    for name, at, scale in (("k", i, SCALE), ("v", count + i, 1.0)):
+        cols = pl.ds(pl.multiple_of(at * D, D), D)
+        inner, leaf = total[name, 0], total[name, 1]
+        both = (inner + leaf[:n]) * scale
+        for j in range(5):
+            out_refs[j][:, cols] = both[j * R : (j + 1) * R].astype(out_refs[j].dtype)
+        out_refs[5][:, cols] = (leaf[n:] * scale).astype(bf)
 
 
 def attend_backward(info, q, g, k_slots, v_slots, first, count, grad_queries):
@@ -126,9 +146,9 @@
                 pltpu.VMEM((R, D), jnp.bfloat16),
             ],
         ),
-        compiler_params=pltpu.CompilerParams(vmem_limit_bytes=40 * 2**20),
+        compiler_params=pltpu.CompilerParams(vmem_limit_bytes=50 * 2**20),
         cost_estimate=pl.CostEstimate(
-            flops=count * 3_000_000_000, bytes_accessed=count * 2**20, transcendentals=count * 900_000
+            flops=count * 4_600_000_000, bytes_accessed=count * 2**20, transcendentals=count * 900_000
         ),
     )(info, *arrays)
 
@@ -171,6 +191,8 @@
     for count in CHUNKS:
         cols = slice(first * D, (first + count) * D)
         own = jnp.concatenate([keys2[:R, cols], values2[:R, cols]], axis=1)
+        if first:
+            own, _ = lax.optimization_barrier((own, a))
         a = permute(own, X_SWAP)
         b = permute(jnp.where(x_even, own, a), X_ONWARD)
         upper = jnp.where(x == 0, own, jnp.where(x == 1, a, b))

time: 126 us -> 117 us (0.929)
  waiting for transfers between devices: 46.4 us -> 33.9 us
  starting transfers between devices: 23.9 us -> 34.5 us
  Pallas kernels: 43.6 us -> 38.3 us
  local copies, waits for them, and re-layouts: 7.05 us -> 5.23 us
    ppermute x16 -> x24, waiting for transfers between devices: 46.4 us -> 33.9 us  [permute(): return lax.ppermute(array, 'leaf', pairs)]
    ppermute x16 -> x24, starting transfers between devices: 23.9 us -> 34.5 us  [permute(): return lax.ppermute(array, 'leaf', pairs)]
    pallas_call x2 -> x3, Pallas kernels: 43.6 us -> 38.3 us  [attend_backward(): pl.pallas_call(functools.partial(kernel, count), input_output_aliases=ali...]
    unnamed x8 -> x4, local copies, waits for them, and re-layouts: 3.49 us -> 0.01 us
    slice x1 -> x3, local copies, waits for them, and re-layouts: 1.13 us -> 2.77 us  [shards(): own = jnp.concatenate([keys2[:R, cols], values2[:R, cols]], axis=1)]
  transfers between devices with their start and end apart: 16 -> 24, of which waited for: 10 -> 13; matrix products, arithmetic and copies ran while one was open for 4% -> 5% of each run, Pallas kernels for 35% -> 33%
where the time goes in v2:
time: 117 us
  Pallas kernels  38.3 us (33%)
  starting transfers between devices  34.5 us (29%)
  waiting for transfers between devices  33.9 us (29%)
  local copies, waits for them, and re-layouts  5.23 us (4%)
  other arithmetic  3.96 us (3%)
    pallas_call x3, Pallas kernels, attend_backward(): pl.pallas_call(functools.partial(kernel, count), input_output_aliases=ali...  38.3 us
    ppermute x24, starting transfers between devices, permute(): return lax.ppermute(array, 'leaf', pairs)  34.5 us
    ppermute x24, waiting for transfers between devices, permute(): return lax.ppermute(array, 'leaf', pairs)  33.9 us
    slice x3, local copies, waits for them, and re-layouts, shards(): own = jnp.concatenate([keys2[:R, cols], values2[:R, cols]], axis=1)  2.77 us
  transfers between devices with their start and end apart: 24, of which 13 were waited for; matrix products, arithmetic and copies ran while one was open for 5% of the time, Pallas kernels for 33%

profile of v2, /device:TPU:128, one launch (start us, length us, event | category | flops | bytes accessed | tf_op | source)
XLA Modules:
  0.0 116.8 jit_solution(15543925200513089287)
XLA Ops:
  0.6 1.1 fusion.25
  1.7 1.6 %collective-permute-start = (bf16[128,768]{1,0:T(8,128)(2,1)S(1)}, bf16[128,768]{1,0:T(8,128)(2,1)S(1)}, u32[]{:S(2)}, u32[]{:S(2)}) collective-permute-start(bf16[128,768]{1,0:T(8,128)(2,1)S(1)} %pad_maximum_fusion.1), channel_id=1, source_target_pairs={{0,1},{1,0},{2,3},{3,2},{4,5},{5,4},{6,7},{7,6},{8,9},{9,8},{10,11... | collective-permute-start | bytes 589832 | tf_op jit(solution)/shard_map/ppermute | solution.py:186
  3.3 0.8 slice.105
  4.2 0.8 slice.106
  5.1 0.8 fusion.33
  5.9 0.6 gather_fusion
  6.6 0.6 constant_dynamic-update-slice_fusion
  7.3 0.8 concatenate.47.info
  8.0 0.5 collective-permute-done.refs_1_.refs_7_
  8.5 2.8 %collective-permute-start.9 = (bf16[128,768]{1,0:T(8,128)(2,1)S(1)}, bf16[128,768]{1,0:T(8,128)(2,1)S(1)}, u32[]{:S(2)}, u32[]{:S(2)}) collective-permute-start(bf16[128,768]{1,0:T(8,128)(2,1)S(1)} %broadcast_select_fusion.2), channel_id=1, source_target_pairs={{0,3},{1,2},{2,1},{3,0},{4,7},{5,6},{6,5},{7,4},{8,11},{9,10},{10,... | collective-permute-start | bytes 589832 | tf_op jit(solution)/shard_map/ppermute | solution.py:186
  11.4 0.3 collective-permute-start.1
  11.7 4.0 %collective-permute-done.9.refs_2_.refs_8_ = bf16[128,768]{1,0:T(8,128)(2,1)S(1)} collective-permute-done((bf16[128,768]{1,0:T(8,128)(2,1)S(1)}, bf16[128,768]{1,0:T(8,128)(2,1)S(1)}, u32[]{:S(2)}, u32[]{:S(2)}) %collective-permute-start.9) | collective-permute-done | bytes 196640 | tf_op jit(solution)/shard_map/ppermute | solution.py:186
  15.8 1.7 %collective-permute-start.10 = (bf16[128,768]{1,0:T(8,128)(2,1)S(1)}, bf16[128,768]{1,0:T(8,128)(2,1)S(1)}, u32[]{:S(2)}, u32[]{:S(2)}) collective-permute-start(bf16[128,768]{1,0:T(8,128)(2,1)S(1)} %select_select_fusion), channel_id=1, source_target_pairs={{0,4},{4,0},{8,12},{12,8},{1,5},{5,1},{9,13},{13,9},{2,6},{6,2},{1... | collective-permute-start | bytes 589832 | tf_op jit(solution)/shard_map/ppermute | solution.py:186
  17.7 2.6 %collective-permute-start.6 = (bf16[128,768]{1,0:T(8,128)(2,1)S(1)}, bf16[128,768]{1,0:T(8,128)(2,1)S(1)}, u32[]{:S(2)}, u32[]{:S(2)}) collective-permute-start(bf16[128,768]{1,0:T(8,128)(2,1)S(1)} %broadcast_select_fusion.3), channel_id=1, source_target_pairs={{0,3},{1,2},{2,1},{3,0},{4,7},{5,6},{6,5},{7,4},{8,11},{9,10},{10,... | collective-permute-start | bytes 589832 | tf_op jit(solution)/shard_map/ppermute | solution.py:186
  20.2 2.2 %collective-permute-done.2.refs_1_.refs_7_ = bf16[128,512]{1,0:T(8,128)(2,1)S(1)} collective-permute-done((bf16[128,512]{1,0:T(8,128)(2,1)S(1)}, bf16[128,512]{1,0:T(8,128)(2,1)S(1)}, u32[]{:S(2)}, u32[]{:S(2)}) %collective-permute-start.2) | collective-permute-done | bytes 131104 | tf_op jit(solution)/shard_map/ppermute | solution.py:186
  22.5 2.7 %collective-permute-start.3 = (bf16[128,512]{1,0:T(8,128)(2,1)S(1)}, bf16[128,512]{1,0:T(8,128)(2,1)S(1)}, u32[]{:S(2)}, u32[]{:S(2)}) collective-permute-start(bf16[128,512]{1,0:T(8,128)(2,1)S(1)} %broadcast_select_fusion.5), channel_id=1, source_target_pairs={{0,3},{1,2},{2,1},{3,0},{4,7},{5,6},{6,5},{7,4},{8,11},{9,10},{10,... | collective-permute-start | bytes 393224 | tf_op jit(solution)/shard_map/ppermute | solution.py:186
  25.2 2.3 %collective-permute-start.11 = (bf16[128,768]{1,0:T(8,128)(2,1)S(1)}, bf16[128,768]{1,0:T(8,128)(2,1)S(1)}, u32[]{:S(2)}, u32[]{:S(2)}) collective-permute-start(bf16[128,768]{1,0:T(8,128)(2,1)S(1)} %broadcast_select_fusion), channel_id=1, source_target_pairs={{0,12},{4,8},{8,4},{12,0},{1,13},{5,9},{9,5},{13,1},{2,14},{6,10},... | collective-permute-start | bytes 589832 | tf_op jit(solution)/shard_map/ppermute | solution.py:186
  27.5 0.8 collective-permute-start.7
  28.3 0.5 collective-permute-done.3.refs_2_.refs_8_
  28.8 1.3 %collective-permute-start.4 = (bf16[128,512]{1,0:T(8,128)(2,1)S(1)}, bf16[128,512]{1,0:T(8,128)(2,1)S(1)}, u32[]{:S(2)}, u32[]{:S(2)}) collective-permute-start(bf16[128,512]{1,0:T(8,128)(2,1)S(1)} %select_select_fusion.2), channel_id=1, source_target_pairs={{0,4},{4,0},{8,12},{12,8},{1,5},{5,1},{9,13},{13,9},{2,6},{6,2},{1... | collective-permute-start | bytes 393224 | tf_op jit(solution)/shard_map/ppermute | solution.py:186
  30.1 2.1 %collective-permute-done.11.refs_4_.refs_10_ = bf16[128,768]{1,0:T(8,128)(2,1)S(1)} collective-permute-done((bf16[128,768]{1,0:T(8,128)(2,1)S(1)}, bf16[128,768]{1,0:T(8,128)(2,1)S(1)}, u32[]{:S(2)}, u32[]{:S(2)}) %collective-permute-start.11) | collective-permute-done | bytes 196640 | tf_op jit(solution)/shard_map/ppermute | solution.py:186
  32.2 14.1 %shard_map.76 = (bf16[256,5120]{1,0:T(8,128)(2,1)}, f32[128,768]{1,0:T(8,128)S(1)}, bf16[128,768]{1,0:T(8,128)(2,1)S(1)}, bf16[128,768]{1,0:T(8,128)(2,1)S(1)}, ...) custom-call(s32[16]{0:T(128)S(1)} %concatenate.47.info, ...), custom_call_target="tpu_custom_call" | custom-call | flops 13799999488 | bytes 3145728 | tf_op jit(solution)/shard_map/pallas_call | solution.py:131
  46.2 2.2 %collective-permute-start.12 = (bf16[128,768]{1,0:T(8,128)(2,1)S(1)}, bf16[128,768]{1,0:T(8,128)(2,1)S(1)}, u32[]{:S(2)}, u32[]{:S(2)}) collective-permute-start(bf16[128,768]{1,0:T(8,128)(2,1)S(1)} %get-tuple-element.44), channel_id=1, source_target_pairs={{0,12},{4,8},{8,4},{12,0},{1,13},{5,9},{9,5},{13,1},{2,14},{6,10},... | collective-permute-start | bytes 589832 | tf_op jit(solution)/shard_map/ppermute | solution.py:186
  48.5 1.1 collective-permute-start.8
  49.6 2.3 %collective-permute-start.5 = (bf16[128,512]{1,0:T(8,128)(2,1)S(1)}, bf16[128,512]{1,0:T(8,128)(2,1)S(1)}, u32[]{:S(2)}, u32[]{:S(2)}) collective-permute-start(bf16[128,512]{1,0:T(8,128)(2,1)S(1)} %broadcast_select_fusion.4), channel_id=1, source_target_pairs={{0,12},{4,8},{8,4},{12,0},{1,13},{5,9},{9,5},{13,1},{2,14},{6,10},... | collective-permute-start | bytes 393224 | tf_op jit(solution)/shard_map/ppermute | solution.py:186
  51.9 1.3 %collective-permute-done.12 = bf16[128,768]{1,0:T(8,128)(2,1)S(1)} collective-permute-done((bf16[128,768]{1,0:T(8,128)(2,1)S(1)}, bf16[128,768]{1,0:T(8,128)(2,1)S(1)}, u32[]{:S(2)}, u32[]{:S(2)}) %collective-permute-start.12) | collective-permute-done | bytes 196640 | tf_op jit(solution)/shard_map/ppermute | solution.py:186
  53.3 0.3 collective-permute-start.13
  53.6 1.8 %collective-permute-done.8.refs_4_.refs_10_ = bf16[128,768]{1,0:T(8,128)(2,1)S(1)} collective-permute-done((bf16[128,768]{1,0:T(8,128)(2,1)S(1)}, bf16[128,768]{1,0:T(8,128)(2,1)S(1)}, u32[]{:S(2)}, u32[]{:S(2)}) %collective-permute-start.8) | collective-permute-done | bytes 196640 | tf_op jit(solution)/shard_map/ppermute | solution.py:186
  55.4 14.1 %shard_map.77 = (bf16[256,5120]{1,0:T(8,128)(2,1)}, f32[128,768]{1,0:T(8,128)S(1)}, bf16[128,768]{1,0:T(8,128)(2,1)S(1)}, bf16[128,768]{1,0:T(8,128)(2,1)S(1)}, ...) custom-call(s32[16]{0:T(128)S(1)} %concatenate.47.info, ...), custom_call_target="tpu_custom_call", output_to_operand_aliasing={{0}: (15, {})} | custom-call | flops 13799999488 | bytes 3145728 | tf_op jit(solution)/shard_map/pallas_call | solution.py:131
  69.5 2.0 %collective-permute-start.16 = (bf16[128,768]{1,0:T(8,128)(2,1)S(1)}, bf16[128,768]{1,0:T(8,128)(2,1)S(1)}, u32[]{:S(2)}, u32[]{:S(2)}) collective-permute-start(bf16[128,768]{1,0:T(8,128)(2,1)S(1)} %get-tuple-element.49), channel_id=1, source_target_pairs={{0,12},{4,8},{8,4},{12,0},{1,13},{5,9},{9,5},{13,1},{2,14},{6,10},... | collective-permute-start | bytes 589832 | tf_op jit(solution)/shard_map/ppermute | solution.py:186
  71.5 10.1 %shard_map.78 = (bf16[256,5120]{1,0:T(8,128)(2,1)}, f32[128,512]{1,0:T(8,128)S(1)}, bf16[128,512]{1,0:T(8,128)(2,1)S(1)}, bf16[128,512]{1,0:T(8,128)(2,1)S(1)}, ...) custom-call(s32[16]{0:T(128)S(1)} %concatenate.47.info, ...), custom_call_target="tpu_custom_call", output_to_operand_aliasing={{0}: (15, {})} | custom-call | flops 9200000000 | bytes 2097152 | tf_op jit(solution)/shard_map/pallas_call | solution.py:131
  81.6 1.2 %collective-permute-start.20 = (bf16[128,512]{1,0:T(8,128)(2,1)S(1)}, bf16[128,512]{1,0:T(8,128)(2,1)S(1)}, u32[]{:S(2)}, u32[]{:S(2)}) collective-permute-start(bf16[128,512]{1,0:T(8,128)(2,1)S(1)} %get-tuple-element.54), channel_id=1, source_target_pairs={{0,12},{4,8},{8,4},{12,0},{1,13},{5,9},{9,5},{13,1},{2,14},{6,10},... | collective-permute-start | bytes 393224 | tf_op jit(solution)/shard_map/ppermute | solution.py:186
  83.0 4.8 %collective-permute-done.20 = bf16[128,512]{1,0:T(8,128)(2,1)S(1)} collective-permute-done((bf16[128,512]{1,0:T(8,128)(2,1)S(1)}, bf16[128,512]{1,0:T(8,128)(2,1)S(1)}, u32[]{:S(2)}, u32[]{:S(2)}) %collective-permute-start.20) | collective-permute-done | bytes 131104 | tf_op jit(solution)/shard_map/ppermute | solution.py:186
  88.1 2.1 %collective-permute-start.14 = (bf16[128,768]{1,0:T(8,128)(2,1)S(1)}, bf16[128,768]{1,0:T(8,128)(2,1)S(1)}, u32[]{:S(2)}, u32[]{:S(2)}) collective-permute-start(bf16[128,768]{1,0:T(8,128)(2,1)S(1)} %add_convert_fusion.1), channel_id=1, source_target_pairs={{0,3},{1,2},{2,1},{3,0},{4,7},{5,6},{6,5},{7,4},{8,11},{9,10},{10,... | collective-permute-start | bytes 589832 | tf_op jit(solution)/shard_map/ppermute | solution.py:186
  90.2 2.7 %collective-permute-done.21 = bf16[128,512]{1,0:T(8,128)(2,1)S(1)} collective-permute-done((bf16[128,512]{1,0:T(8,128)(2,1)S(1)}, bf16[128,512]{1,0:T(8,128)(2,1)S(1)}, u32[]{:S(2)}, u32[]{:S(2)}) %collective-permute-start.21) | collective-permute-done | bytes 131104 | tf_op jit(solution)/shard_map/ppermute | solution.py:186
  93.0 2.1 %collective-permute-start.22 = (bf16[128,512]{1,0:T(8,128)(2,1)S(1)}, bf16[128,512]{1,0:T(8,128)(2,1)S(1)}, u32[]{:S(2)}, u32[]{:S(2)}) collective-permute-start(bf16[128,512]{1,0:T(8,128)(2,1)S(1)} %add_convert_fusion.2), channel_id=1, source_target_pairs={{0,3},{1,2},{2,1},{3,0},{4,7},{5,6},{6,5},{7,4},{8,11},{9,10},{10,... | collective-permute-start | bytes 393224 | tf_op jit(solution)/shard_map/ppermute | solution.py:186
  95.3 3.9 %collective-permute-done.22 = bf16[128,512]{1,0:T(8,128)(2,1)S(1)} collective-permute-done((bf16[128,512]{1,0:T(8,128)(2,1)S(1)}, bf16[128,512]{1,0:T(8,128)(2,1)S(1)}, u32[]{:S(2)}, u32[]{:S(2)}) %collective-permute-start.22) | collective-permute-done | bytes 131104 | tf_op jit(solution)/shard_map/ppermute | solution.py:186
  99.3 0.3 collective-permute-start.23
  99.7 0.1 fusion.7
  99.8 2.1 %collective-permute-start.15 = (bf16[128,768]{1,0:T(8,128)(2,1)S(1)}, bf16[128,768]{1,0:T(8,128)(2,1)S(1)}, u32[]{:S(2)}, u32[]{:S(2)}) collective-permute-start(bf16[128,768]{1,0:T(8,128)(2,1)S(1)} %fusion.7), channel_id=1, source_target_pairs={{0,1},{1,0},{2,3},{3,2},{4,5},{5,4},{6,7},{7,6},{8,9},{9,8},{10,11... | collective-permute-start | bytes 589832 | tf_op jit(solution)/shard_map/ppermute | solution.py:186
  102.0 2.2 %collective-permute-start.18 = (bf16[128,768]{1,0:T(8,128)(2,1)S(1)}, bf16[128,768]{1,0:T(8,128)(2,1)S(1)}, u32[]{:S(2)}, u32[]{:S(2)}) collective-permute-start(bf16[128,768]{1,0:T(8,128)(2,1)S(1)} %add_convert_fusion), channel_id=1, source_target_pairs={{0,3},{1,2},{2,1},{3,0},{4,7},{5,6},{6,5},{7,4},{8,11},{9,10},{10,... | collective-permute-start | bytes 589832 | tf_op jit(solution)/shard_map/ppermute | solution.py:186
  104.3 0.3 collective-permute-done.23
  104.7 4.2 %collective-permute-done.18 = bf16[128,768]{1,0:T(8,128)(2,1)S(1)} collective-permute-done((bf16[128,768]{1,0:T(8,128)(2,1)S(1)}, bf16[128,768]{1,0:T(8,128)(2,1)S(1)}, u32[]{:S(2)}, u32[]{:S(2)}) %collective-permute-start.18) | collective-permute-done | bytes 196640 | tf_op jit(solution)/shard_map/ppermute | solution.py:186
  109.2 0.2 fusion.5
  109.4 5.5 %collective-permute-done.19 = bf16[128,768]{1,0:T(8,128)(2,1)S(1)} collective-permute-done((bf16[128,768]{1,0:T(8,128)(2,1)S(1)}, bf16[128,768]{1,0:T(8,128)(2,1)S(1)}, u32[]{:S(2)}, u32[]{:S(2)}) %collective-permute-start.19) | collective-permute-done | bytes 196640 | tf_op jit(solution)/shard_map/ppermute | solution.py:186
  114.9 0.2 fusion.13
  115.1 0.8 maximum_bitcast_fusion.1
  116.0 0.8 maximum_bitcast_fusion
  (57 shorter events, 2.0 us)
Async XLA Ops:
  1.7 6.7 %collective-permute-start = (bf16[128,768]{1,0:T(8,128)(2,1)S(1)}, bf16[128,768]{1,0:T(8,128)(2,1)S(1)}, u32[]{:S(2)}, u32[]{:S(2)}) collective-permute-start(bf16[128,768]{1,0:T(8,128)(2,1)S(1)} %pad_maximum_fusion.1), channel_id=1, source_target_pairs={{0,1},{1,0},{2,3},{3,2},{4,5},{5,4},{6,7},{7,6},{8,9},{9,8},{10,11... | collective-permute-start | bytes 589832 | tf_op jit(solution)/shard_map/ppermute | solution.py:186
  5.9 26.3 %copy-start = (bf16[1,2,128,1024]{3,2,1,0:T(8,128)(2,1)S(1)}, bf16[1,2,128,1024]{3,2,1,0:T(8,128)(2,1)}, u32[]{:S(2)}) copy-start(bf16[1,2,128,1024]{3,2,1,0:T(8,128)(2,1)} %param.8) | copy-start | bytes 1572868
  5.9 26.3 %copy-start.1 = (bf16[1,2,128,1024]{3,2,1,0:T(8,128)(2,1)S(1)}, bf16[1,2,128,1024]{3,2,1,0:T(8,128)(2,1)}, u32[]{:S(2)}) copy-start(bf16[1,2,128,1024]{3,2,1,0:T(8,128)(2,1)} %param.9) | copy-start | bytes 1572868
  8.5 7.2 %collective-permute-start.9 = (bf16[128,768]{1,0:T(8,128)(2,1)S(1)}, bf16[128,768]{1,0:T(8,128)(2,1)S(1)}, u32[]{:S(2)}, u32[]{:S(2)}) collective-permute-start(bf16[128,768]{1,0:T(8,128)(2,1)S(1)} %broadcast_select_fusion.2), channel_id=1, source_target_pairs={{0,3},{1,2},{2,1},{3,0},{4,7},{5,6},{6,5},{7,4},{8,11},{9,10},{10,... | collective-permute-start | bytes 589832 | tf_op jit(solution)/shard_map/ppermute | solution.py:186
  11.4 6.1 %collective-permute-start.1 = (bf16[128,768]{1,0:T(8,128)(2,1)S(1)}, bf16[128,768]{1,0:T(8,128)(2,1)S(1)}, u32[]{:S(2)}, u32[]{:S(2)}) collective-permute-start(bf16[128,768]{1,0:T(8,128)(2,1)S(1)} %pad_maximum_fusion), channel_id=1, source_target_pairs={{0,1},{1,0},{2,3},{3,2},{4,5},{5,4},{6,7},{7,6},{8,9},{9,8},{10,11... | collective-permute-start | bytes 589832 | tf_op jit(solution)/shard_map/ppermute | solution.py:186
  15.8 9.4 %collective-permute-start.10 = (bf16[128,768]{1,0:T(8,128)(2,1)S(1)}, bf16[128,768]{1,0:T(8,128)(2,1)S(1)}, u32[]{:S(2)}, u32[]{:S(2)}) collective-permute-start(bf16[128,768]{1,0:T(8,128)(2,1)S(1)} %select_select_fusion), channel_id=1, source_target_pairs={{0,4},{4,0},{8,12},{12,8},{1,5},{5,1},{9,13},{13,9},{2,6},{6,2},{1... | collective-permute-start | bytes 589832 | tf_op jit(solution)/shard_map/ppermute | solution.py:186
  17.5 5.0 %collective-permute-start.2 = (bf16[128,512]{1,0:T(8,128)(2,1)S(1)}, bf16[128,512]{1,0:T(8,128)(2,1)S(1)}, u32[]{:S(2)}, u32[]{:S(2)}) collective-permute-start(bf16[128,512]{1,0:T(8,128)(2,1)S(1)} %pad_maximum_fusion.2), channel_id=1, source_target_pairs={{0,1},{1,0},{2,3},{3,2},{4,5},{5,4},{6,7},{7,6},{8,9},{9,8},{10,11... | collective-permute-start | bytes 393224 | tf_op jit(solution)/shard_map/ppermute | solution.py:186
  17.7 9.8 %collective-permute-start.6 = (bf16[128,768]{1,0:T(8,128)(2,1)S(1)}, bf16[128,768]{1,0:T(8,128)(2,1)S(1)}, u32[]{:S(2)}, u32[]{:S(2)}) collective-permute-start(bf16[128,768]{1,0:T(8,128)(2,1)S(1)} %broadcast_select_fusion.3), channel_id=1, source_target_pairs={{0,3},{1,2},{2,1},{3,0},{4,7},{5,6},{6,5},{7,4},{8,11},{9,10},{10,... | collective-permute-start | bytes 589832 | tf_op jit(solution)/shard_map/ppermute | solution.py:186
  22.5 6.3 %collective-permute-start.3 = (bf16[128,512]{1,0:T(8,128)(2,1)S(1)}, bf16[128,512]{1,0:T(8,128)(2,1)S(1)}, u32[]{:S(2)}, u32[]{:S(2)}) collective-permute-start(bf16[128,512]{1,0:T(8,128)(2,1)S(1)} %broadcast_select_fusion.5), channel_id=1, source_target_pairs={{0,3},{1,2},{2,1},{3,0},{4,7},{5,6},{6,5},{7,4},{8,11},{9,10},{10,... | collective-permute-start | bytes 393224 | tf_op jit(solution)/shard_map/ppermute | solution.py:186
  25.2 7.0 %collective-permute-start.11 = (bf16[128,768]{1,0:T(8,128)(2,1)S(1)}, bf16[128,768]{1,0:T(8,128)(2,1)S(1)}, u32[]{:S(2)}, u32[]{:S(2)}) collective-permute-start(bf16[128,768]{1,0:T(8,128)(2,1)S(1)} %broadcast_select_fusion), channel_id=1, source_target_pairs={{0,12},{4,8},{8,4},{12,0},{1,13},{5,9},{9,5},{13,1},{2,14},{6,10},... | collective-permute-start | bytes 589832 | tf_op jit(solution)/shard_map/ppermute | solution.py:186
  27.5 20.9 %collective-permute-start.7 = (bf16[128,768]{1,0:T(8,128)(2,1)S(1)}, bf16[128,768]{1,0:T(8,128)(2,1)S(1)}, u32[]{:S(2)}, u32[]{:S(2)}) collective-permute-start(bf16[128,768]{1,0:T(8,128)(2,1)S(1)} %select_select_fusion.1), channel_id=1, source_target_pairs={{0,4},{4,0},{8,12},{12,8},{1,5},{5,1},{9,13},{13,9},{2,6},{6,2},{1... | collective-permute-start | bytes 589832 | tf_op jit(solution)/shard_map/ppermute | solution.py:186
  28.8 20.8 %collective-permute-start.4 = (bf16[128,512]{1,0:T(8,128)(2,1)S(1)}, bf16[128,512]{1,0:T(8,128)(2,1)S(1)}, u32[]{:S(2)}, u32[]{:S(2)}) collective-permute-start(bf16[128,512]{1,0:T(8,128)(2,1)S(1)} %select_select_fusion.2), channel_id=1, source_target_pairs={{0,4},{4,0},{8,12},{12,8},{1,5},{5,1},{9,13},{13,9},{2,6},{6,2},{1... | collective-permute-start | bytes 393224 | tf_op jit(solution)/shard_map/ppermute | solution.py:186
  46.2 7.0 %collective-permute-start.12 = (bf16[128,768]{1,0:T(8,128)(2,1)S(1)}, bf16[128,768]{1,0:T(8,128)(2,1)S(1)}, u32[]{:S(2)}, u32[]{:S(2)}) collective-permute-start(bf16[128,768]{1,0:T(8,128)(2,1)S(1)} %get-tuple-element.44), channel_id=1, source_target_pairs={{0,12},{4,8},{8,4},{12,0},{1,13},{5,9},{9,5},{13,1},{2,14},{6,10},... | collective-permute-start | bytes 589832 | tf_op jit(solution)/shard_map/ppermute | solution.py:186
  48.5 7.0 %collective-permute-start.8 = (bf16[128,768]{1,0:T(8,128)(2,1)S(1)}, bf16[128,768]{1,0:T(8,128)(2,1)S(1)}, u32[]{:S(2)}, u32[]{:S(2)}) collective-permute-start(bf16[128,768]{1,0:T(8,128)(2,1)S(1)} %broadcast_select_fusion.1), channel_id=1, source_target_pairs={{0,12},{4,8},{8,4},{12,0},{1,13},{5,9},{9,5},{13,1},{2,14},{6,10},... | collective-permute-start | bytes 589832 | tf_op jit(solution)/shard_map/ppermute | solution.py:186
  49.6 21.8 %collective-permute-start.5 = (bf16[128,512]{1,0:T(8,128)(2,1)S(1)}, bf16[128,512]{1,0:T(8,128)(2,1)S(1)}, u32[]{:S(2)}, u32[]{:S(2)}) collective-permute-start(bf16[128,512]{1,0:T(8,128)(2,1)S(1)} %broadcast_select_fusion.4), channel_id=1, source_target_pairs={{0,12},{4,8},{8,4},{12,0},{1,13},{5,9},{9,5},{13,1},{2,14},{6,10},... | collective-permute-start | bytes 393224 | tf_op jit(solution)/shard_map/ppermute | solution.py:186
  53.3 34.6 %collective-permute-start.13 = (bf16[128,768]{1,0:T(8,128)(2,1)S(1)}, bf16[128,768]{1,0:T(8,128)(2,1)S(1)}, u32[]{:S(2)}, u32[]{:S(2)}) collective-permute-start(bf16[128,768]{1,0:T(8,128)(2,1)S(1)} %fusion.2), channel_id=1, source_target_pairs={{0,4},{4,0},{8,12},{12,8},{1,5},{5,1},{9,13},{13,9},{2,6},{6,2},{1... | collective-permute-start | bytes 589832 | tf_op jit(solution)/shard_map/ppermute | solution.py:186
  69.5 25.6 %collective-permute-start.16 = (bf16[128,768]{1,0:T(8,128)(2,1)S(1)}, bf16[128,768]{1,0:T(8,128)(2,1)S(1)}, u32[]{:S(2)}, u32[]{:S(2)}) collective-permute-start(bf16[128,768]{1,0:T(8,128)(2,1)S(1)} %get-tuple-element.49), channel_id=1, source_target_pairs={{0,12},{4,8},{8,4},{12,0},{1,13},{5,9},{9,5},{13,1},{2,14},{6,10},... | collective-permute-start | bytes 589832 | tf_op jit(solution)/shard_map/ppermute | solution.py:186
  81.6 6.2 %collective-permute-start.20 = (bf16[128,512]{1,0:T(8,128)(2,1)S(1)}, bf16[128,512]{1,0:T(8,128)(2,1)S(1)}, u32[]{:S(2)}, u32[]{:S(2)}) collective-permute-start(bf16[128,512]{1,0:T(8,128)(2,1)S(1)} %get-tuple-element.54), channel_id=1, source_target_pairs={{0,12},{4,8},{8,4},{12,0},{1,13},{5,9},{9,5},{13,1},{2,14},{6,10},... | collective-permute-start | bytes 393224 | tf_op jit(solution)/shard_map/ppermute | solution.py:186
  87.8 5.1 %collective-permute-start.21 = (bf16[128,512]{1,0:T(8,128)(2,1)S(1)}, bf16[128,512]{1,0:T(8,128)(2,1)S(1)}, u32[]{:S(2)}, u32[]{:S(2)}) collective-permute-start(bf16[128,512]{1,0:T(8,128)(2,1)S(1)} %fusion.18), channel_id=1, source_target_pairs={{0,4},{4,0},{8,12},{12,8},{1,5},{5,1},{9,13},{13,9},{2,6},{6,2},{1... | collective-permute-start | bytes 393224 | tf_op jit(solution)/shard_map/ppermute | solution.py:186
  88.1 11.6 %collective-permute-start.14 = (bf16[128,768]{1,0:T(8,128)(2,1)S(1)}, bf16[128,768]{1,0:T(8,128)(2,1)S(1)}, u32[]{:S(2)}, u32[]{:S(2)}) collective-permute-start(bf16[128,768]{1,0:T(8,128)(2,1)S(1)} %add_convert_fusion.1), channel_id=1, source_target_pairs={{0,3},{1,2},{2,1},{3,0},{4,7},{5,6},{6,5},{7,4},{8,11},{9,10},{10,... | collective-permute-start | bytes 589832 | tf_op jit(solution)/shard_map/ppermute | solution.py:186
  93.0 6.3 %collective-permute-start.22 = (bf16[128,512]{1,0:T(8,128)(2,1)S(1)}, bf16[128,512]{1,0:T(8,128)(2,1)S(1)}, u32[]{:S(2)}, u32[]{:S(2)}) collective-permute-start(bf16[128,512]{1,0:T(8,128)(2,1)S(1)} %add_convert_fusion.2), channel_id=1, source_target_pairs={{0,3},{1,2},{2,1},{3,0},{4,7},{5,6},{6,5},{7,4},{8,11},{9,10},{10,... | collective-permute-start | bytes 393224 | tf_op jit(solution)/shard_map/ppermute | solution.py:186
  95.2 6.7 %collective-permute-start.17 = (bf16[128,768]{1,0:T(8,128)(2,1)S(1)}, bf16[128,768]{1,0:T(8,128)(2,1)S(1)}, u32[]{:S(2)}, u32[]{:S(2)}) collective-permute-start(bf16[128,768]{1,0:T(8,128)(2,1)S(1)} %fusion.10), channel_id=1, source_target_pairs={{0,4},{4,0},{8,12},{12,8},{1,5},{5,1},{9,13},{13,9},{2,6},{6,2},{1... | collective-permute-start | bytes 589832 | tf_op jit(solution)/shard_map/ppermute | solution.py:186
  99.3 5.3 %collective-permute-start.23 = (bf16[128,512]{1,0:T(8,128)(2,1)S(1)}, bf16[128,512]{1,0:T(8,128)(2,1)S(1)}, u32[]{:S(2)}, u32[]{:S(2)}) collective-permute-start(bf16[128,512]{1,0:T(8,128)(2,1)S(1)} %fusion.23), channel_id=1, source_target_pairs={{0,1},{1,0},{2,3},{3,2},{4,5},{5,4},{6,7},{7,6},{8,9},{9,8},{10,11... | collective-permute-start | bytes 393224 | tf_op jit(solution)/shard_map/ppermute | solution.py:186
  99.8 9.4 %collective-permute-start.15 = (bf16[128,768]{1,0:T(8,128)(2,1)S(1)}, bf16[128,768]{1,0:T(8,128)(2,1)S(1)}, u32[]{:S(2)}, u32[]{:S(2)}) collective-permute-start(bf16[128,768]{1,0:T(8,128)(2,1)S(1)} %fusion.7), channel_id=1, source_target_pairs={{0,1},{1,0},{2,3},{3,2},{4,5},{5,4},{6,7},{7,6},{8,9},{9,8},{10,11... | collective-permute-start | bytes 589832 | tf_op jit(solution)/shard_map/ppermute | solution.py:186
  102.0 7.0 %collective-permute-start.18 = (bf16[128,768]{1,0:T(8,128)(2,1)S(1)}, bf16[128,768]{1,0:T(8,128)(2,1)S(1)}, u32[]{:S(2)}, u32[]{:S(2)}) collective-permute-start(bf16[128,768]{1,0:T(8,128)(2,1)S(1)} %add_convert_fusion), channel_id=1, source_target_pairs={{0,3},{1,2},{2,1},{3,0},{4,7},{5,6},{6,5},{7,4},{8,11},{9,10},{10,... | collective-permute-start | bytes 589832 | tf_op jit(solution)/shard_map/ppermute | solution.py:186
  109.1 5.8 %collective-permute-start.19 = (bf16[128,768]{1,0:T(8,128)(2,1)S(1)}, bf16[128,768]{1,0:T(8,128)(2,1)S(1)}, u32[]{:S(2)}, u32[]{:S(2)}) collective-permute-start(bf16[128,768]{1,0:T(8,128)(2,1)S(1)} %fusion.15), channel_id=1, source_target_pairs={{0,1},{1,0},{2,3},{3,2},{4,5},{5,4},{6,7},{7,6},{8,9},{9,8},{10,11... | collective-permute-start | bytes 589832 | tf_op jit(solution)/shard_map/ppermute | solution.py:186

commit v3 on v2

v3 whole, which is shorter than its diff:
```python
import functools
import math

import jax
import jax.numpy as jnp
from jax import lax
from jax.experimental import pallas as pl
from jax.experimental.pallas import tpu as pltpu
from jax.sharding import PartitionSpec as P

HEADS = 8
GROUP = 5
D = 128
R = 128
BIG = 2.0**30
SCALE = 1.0 / math.sqrt(D)
EXP2_SCALE = SCALE * math.log2(math.e)
CHUNKS = (3, 3, 2)

SWAP = ((0, 1), (1, 0), (2, 3), (3, 2))
ONWARD = ((0, 3), (1, 2), (2, 1), (3, 0))
X_SWAP = [(4 * y + s, 4 * y + t) for y in range(4) for s, t in SWAP]
X_ONWARD = [(4 * y + s, 4 * y + t) for y in range(4) for s, t in ONWARD]
Y_SWAP = [(4 * s + x, 4 * t + x) for x in range(4) for s, t in SWAP]
Y_ONWARD = [(4 * s + x, 4 * t + x) for x in range(4) for s, t in ONWARD]


def dot(a, b, ca, cb):
    return lax.dot_general(a, b, (((ca,), (cb,)), ((), ())), preferred_element_type=jnp.float32)


def stacked(q_ref, g_ref, info):
    row = lax.broadcasted_iota(jnp.int32, (R, D), 0)
    qs, gs = [], []
    for t in range(2):
        live = row < info[12 + t]
        heads = [slice(h * D, (h + 1) * D) for h in range(GROUP)]
        rows = slice(t * R, (t + 1) * R)
        qs.append(jnp.concatenate([q_ref[rows, h] for h in heads], axis=0))
        gs.append(
            jnp.concatenate(
                [jnp.where(live, g_ref[rows, h], jnp.zeros((), jnp.bfloat16)) for h in heads], axis=0
            )
        )
    return qs, gs


def columns(count):
    i = pl.program_id(0)
    return [pl.ds(pl.multiple_of(at * D, D), D) for at in (i, count + i)]


def score_kernel(count, info, q_ref, g_ref, *refs):
    k_refs, v_refs = refs[0:6], refs[6:12]
    out_refs, ds_ref, wo_ref = refs[12:16], refs[16], refs[17]
    w_s, mask_s, tri_s = refs[18:21]
    bf = jnp.bfloat16
    row = lax.broadcasted_iota(jnp.int32, (R, D), 0)
    col = lax.broadcasted_iota(jnp.int32, (R, D), 1)

    @pl.when(pl.program_id(0) == 0)
    def _():
        tri_s[...] = jnp.where((col == 0) | (col > row), -BIG, 0.0).astype(bf)
        for t in range(2):
            for j in range(6):
                hot = (col == 0) & (row >= info[6 * t + j])
                if (t, j) in ((0, 0), (1, 5)):
                    hot = hot | ((col == row) & (col > 0))
                mask_s[t, j * R : (j + 1) * R, :] = jnp.where(hot, 1.0, 0.0).astype(bf)

    k = jnp.concatenate([r[...] for r in k_refs], axis=0)
    v = jnp.concatenate([r[...] for r in v_refs], axis=0)
    qs, gs = stacked(q_ref, g_ref, info)
    tri = jnp.concatenate([tri_s[...]] * GROUP, axis=0)
    sizes = (5 * R, 6 * R)
    k_wide = [jnp.concatenate([k[:n], mask_s[t, :n, :]], axis=1) for t, n in enumerate(sizes)]
    q_wide = [jnp.concatenate([qs[t], tri], axis=1) for t in range(2)]

    def products(t, h0, h1):
        n, part = sizes[t], slice(h0 * R, h1 * R)
        return dot(k_wide[t], q_wide[t][part], 1, 1), dot(v[:n], gs[t][part], 1, 1)

    def softmax_backward(t, h0, h1, s, dw):
        n, place = sizes[t], slice((t * GROUP + h0) * R, (t * GROUP + h1) * R)
        m = jnp.max(s, axis=0, keepdims=True)
        e = jnp.exp2((s - m) * EXP2_SCALE)
        w = e * (1.0 / jnp.sum(e, axis=0, keepdims=True))
        delta = jnp.sum(w * dw, axis=0, keepdims=True)
        ds_ref[:n, place] = (w * (dw - delta)).astype(bf)
        w_half = w.astype(bf)
        wo_ref[:R, place] = w_half[:R]
        w_s[:, place] = w_half[R : 5 * R]
        if t:
            wo_ref[R:, place] = w_half[5 * R :]

    total = []

    def gradients(t, h0, h1):
        place, part = slice((t * GROUP + h0) * R, (t * GROUP + h1) * R), slice(h0 * R, h1 * R)
        terms = [
            dot(ds_ref[R : 5 * R, place], qs[t][part], 1, 0),
            dot(w_s[:, place], gs[t][part], 1, 0),
        ]
        total[:] = [a + b for a, b in zip(total, terms)] if total else terms

    todo = [(t, h0, h1) for t in range(2) for h0, h1 in ((0, 2), (2, 4), (4, 5))]
    ahead = products(*todo[0])
    for step, part in enumerate(todo):
        now = ahead
        if step + 1 < len(todo):
            ahead = products(*todo[step + 1])
        if step:
            gradients(*todo[step - 1])
        softmax_backward(*part, *now)
    gradients(*todo[-1])
    for cols, value, scale in zip(columns(count), total, (SCALE, 1.0)):
        for j in range(4):
            out_refs[j][:, cols] = (value[j * R : (j + 1) * R] * scale).astype(bf)


def own_kernel(count, info, q_ref, g_ref, *refs):
    k_refs, ds_ref, wo_ref = refs[0:6], refs[6], refs[7]
    dq_ref, inner_ref, leaf_ref = refs[-3:]
    bf = jnp.bfloat16
    k_turned = jnp.concatenate([r[...] for r in k_refs], axis=0).T
    qs, gs = stacked(q_ref, g_ref, info)
    half = GROUP * R
    for t, n in ((0, 5 * R), (1, 6 * R)):
        dq = (dot(k_turned[:, :n], ds_ref[:n, t * half : (t + 1) * half], 1, 0) * SCALE).T
        for h in range(GROUP):
            dq_ref[t * R : (t + 1) * R, h * D : (h + 1) * D] = dq[h * R : (h + 1) * R].astype(bf)
    k_cols, v_cols = columns(count)
    inner_ref[:, k_cols] = dot(ds_ref[:R, :], jnp.concatenate(qs, axis=0), 1, 0) * SCALE
    inner_ref[:, v_cols] = dot(wo_ref[:R, :], jnp.concatenate(gs, axis=0), 1, 0)
    leaf_ref[:, k_cols] = (dot(ds_ref[5 * R :, half:], qs[1], 1, 0) * SCALE).astype(bf)
    leaf_ref[:, v_cols] = dot(wo_ref[R:, half:], gs[1], 1, 0).astype(bf)


def slot_specs(slots):
    return [
        pl.BlockSpec((R, D), functools.partial(lambda b, o, i, _: (b, o + i), block, offset))
        for _, block, offset in slots
    ]


def score_gradients(info, q, g, k_slots, v_slots, first, count):
    bf = jnp.bfloat16
    wide = 2 * GROUP * R
    return pl.pallas_call(
        functools.partial(score_kernel, count),
        out_shape=[jax.ShapeDtypeStruct((R, count * 2 * D), bf)] * 4
        + [jax.ShapeDtypeStruct((count * n * R, wide), bf) for n in (6, 2)],
        grid_spec=pltpu.PrefetchScalarGridSpec(
            num_scalar_prefetch=1,
            grid=(count,),
            in_specs=[pl.BlockSpec((2 * R, GROUP * D), lambda i, _: (0, first + i))] * 2
            + slot_specs(k_slots + v_slots),
            out_specs=[pl.BlockSpec((R, count * 2 * D), lambda i, _: (0, 0))] * 4
            + [pl.BlockSpec((n * R, wide), lambda i, _: (i, 0)) for n in (6, 2)],
            scratch_shapes=[
                pltpu.VMEM((4 * R, wide), bf),
                pltpu.VMEM((2, 6 * R, D), bf),
                pltpu.VMEM((R, D), bf),
            ],
        ),
        compiler_params=pltpu.CompilerParams(vmem_limit_bytes=50 * 2**20),
        cost_estimate=pl.CostEstimate(
            flops=count * 3_600_000_000, bytes_accessed=count * 2**22, transcendentals=count * 900_000
        ),
    )(info, q, g, *[s[0] for s in k_slots + v_slots])


def own_gradients(info, q, g, k_slots, ds, wo, first, count, grad_queries):
    wide = 2 * GROUP * R
    specs = [pl.BlockSpec((2 * R, GROUP * D), lambda i, _: (0, first + i))] * 2 + slot_specs(k_slots)
    specs += [pl.BlockSpec((n * R, wide), lambda i, _: (i, 0)) for n in (6, 2)]
    arrays = [q, g] + [s[0] for s in k_slots] + [ds, wo]
    aliases = {}
    if grad_queries is not None:
        aliases = {1 + len(arrays): 0}
        specs.append(pl.BlockSpec(memory_space=pl.ANY))
        arrays.append(grad_queries)
    return pl.pallas_call(
        functools.partial(own_kernel, count),
        input_output_aliases=aliases,
        out_shape=[
            jax.ShapeDtypeStruct(q.shape, jnp.bfloat16),
            jax.ShapeDtypeStruct((R, count * 2 * D), jnp.float32),
            jax.ShapeDtypeStruct((R, count * 2 * D), jnp.bfloat16),
        ],
        grid_spec=pltpu.PrefetchScalarGridSpec(
            num_scalar_prefetch=1,
            grid=(count,),
            in_specs=specs,
            out_specs=[pl.BlockSpec((2 * R, GROUP * D), lambda i, _: (0, first + i))]
            + [pl.BlockSpec((R, count * 2 * D), lambda i, _: (0, 0))] * 2,
        ),
        compiler_params=pltpu.CompilerParams(vmem_limit_bytes=50 * 2**20),
        cost_estimate=pl.CostEstimate(
            flops=count * 1_300_000_000, bytes_accessed=count * 2**22, transcendentals=0
        ),
    )(info, *arrays)


def neighbours(x):
    swap = x ^ 1
    onward = jnp.where(x < 2, 2, 0)
    return swap, onward


def place_of(index):
    place = jnp.zeros_like(index)
    for bit in (3, 2, 1, 0):
        place = jnp.where((index >> bit) & 1 == 1, 4 - bit, place)
    return place


def shards(queries, keys, values, out_grad, seg_lengths):
    me = lax.axis_index("leaf")
    x, y = me & 3, me >> 2
    x_even, y_even = (x & 1) == 0, (y & 1) == 0
    x_swap, x_on = neighbours(x)
    y_swap, y_on = neighbours(y)
    ids = jnp.stack([me, 4 * y + x_swap, 4 * y + x_on, 4 * y_swap, 4 * y_on, me])
    lengths = jnp.take(seg_lengths[:, 0], ids).at[5].set(jnp.take(seg_lengths[:, 1], me))
    my_place = place_of(me)
    inner_limit = jnp.where((place_of(ids) < my_place) | (ids == me), lengths, 0)
    info = jnp.concatenate([inner_limit, lengths, lengths[:1], lengths[5:], jnp.zeros((2,), jnp.int32)])

    q = queries.reshape(2 * R, -1)
    g = out_grad.reshape(2 * R, -1)
    keys2, values2 = keys.reshape(2 * R, -1), values.reshape(2 * R, -1)

    f32, bf = jnp.float32, jnp.bfloat16
    firsts = [sum(CHUNKS[:c]) for c in range(len(CHUNKS))]
    sent, got, scored, owned = {}, {}, {}, {}

    def hop(number, c):
        pairs = (X_SWAP, X_ONWARD, Y_SWAP, Y_ONWARD, Y_ONWARD, Y_SWAP, X_ONWARD, X_SWAP)[number]
        if number == 0:
            cols = slice(firsts[c] * D, (firsts[c] + CHUNKS[c]) * D)
            value = sent[c] = jnp.concatenate([keys2[:R, cols], values2[:R, cols]], axis=1)
        elif number == 1:
            value = jnp.where(x_even, sent[c], got[0, c])
        elif number == 2:
            value = sent[c] = jnp.where(x == 0, sent[c], jnp.where(x == 1, got[0, c], got[1, c]))
        elif number == 3:
            value = jnp.where(y_even, sent[c], got[2, c])
        elif number == 4:
            value = scored[c][3]
        elif number == 5:
            value = (scored[c][2].astype(f32) + jnp.where(y_even, 0.0, got[4, c].astype(f32))).astype(bf)
        else:
            upper = jnp.where(y_even, got[4, c].astype(f32), 0.0) + got[5, c].astype(f32)
            if number == 6:
                value = (scored[c][1].astype(f32) + jnp.where(x >= 2, upper, 0.0)).astype(bf)
            else:
                value = scored[c][0].astype(f32) + jnp.where(x == 1, upper, 0.0)
                value = (value + jnp.where(x_even, 0.0, got[6, c].astype(f32))).astype(bf)
        return value, pairs

    def stage(hops, after):
        values, pairs = zip(*[hop(*h) for h in hops])
        if after:
            values = lax.optimization_barrier((values, tuple(after)))[0]
        for h, value, p in zip(hops, values, pairs):
            got[h] = lax.ppermute(value, "leaf", p)
        return [got[h] for h in hops]

    def slots(c):
        keys_in = [(keys2, 0, firsts[c])] + [(got[n, c], 0, 0) for n in range(4)] + [(keys2, 1, firsts[c])]
        values_in = [(values2, 0, firsts[c])] + [(got[n, c], 0, CHUNKS[c]) for n in range(4)]
        return keys_in, values_in + [(values2, 1, firsts[c])]

    def score(c, after):
        held = lax.optimization_barrier((info, tuple(after)))[0]
        scored[c] = score_gradients(held, q, g, *slots(c), firsts[c], CHUNKS[c])
        return list(scored[c][:1])

    grad_queries = None

    def own(c, after):
        held = lax.optimization_barrier((info, tuple(after)))[0]
        ds, wo = scored[c][4:]
        owned[c] = own_gradients(held, q, g, slots(c)[0], ds, wo, firsts[c], CHUNKS[c], grad_queries)
        return owned[c][0], list(owned[c][1:2])

    last = stage([(0, 0)], [])
    last = stage([(1, 0), (0, 1)], last)
    last = stage([(2, 0), (1, 1), (0, 2)], last)
    last = stage([(3, 0), (2, 1), (1, 2)], last)
    ready, last = last, stage([(3, 1), (2, 2)], last)
    done = score(0, ready)
    ready, last = last, stage([(3, 2), (4, 0)], last + done)
    done = score(1, ready + done)
    ready, last = last, stage([(5, 0), (4, 1)], last + done)
    done = score(2, ready + done)
    ready, last = last, stage([(4, 2), (5, 1), (6, 0)], last + done)
    grad_queries, done = own(0, ready + done)
    ready, last = last, stage([(5, 2), (6, 1), (7, 0)], last + done)
    grad_queries, done = own(1, ready + done)
    ready, last = last, stage([(6, 2), (7, 1)], last + done)
    grad_queries, done = own(2, ready + done)
    stage([(7, 2)], last + done)

    inner, leaf = [], []
    for c in range(len(CHUNKS)):
        upper = jnp.where(y_even, got[4, c].astype(f32), 0.0) + got[5, c].astype(f32)
        mine = owned[c][1] + jnp.where(x == 0, upper, 0.0)
        mine = mine + jnp.where(x_even, got[6, c].astype(f32), 0.0) + got[7, c].astype(f32)
        inner.append(mine.astype(bf))
        leaf.append(owned[c][2])

    def assemble(half):
        rows = []
        for pieces in (inner, leaf):
            cut = [p[:, half * c * D : (half + 1) * c * D] for p, c in zip(pieces, CHUNKS)]
            rows.append(jnp.concatenate(cut, axis=1))
        return jnp.stack(rows)[None]

    return grad_queries.reshape(queries.shape), assemble(0), assemble(1)


def solution(mesh):
    rows = P(("prompt", "leaf"), None, None, None)
    return jax.shard_map(
        shards,
        mesh=mesh,
        in_specs=(rows, rows, rows, rows, P("prompt", None)),
        out_specs=(rows, rows, rows),
        check_vma=False,
    )
```

time: 117 us -> 123 us (1.051)
  Pallas kernels: 38.3 us -> 53.2 us
  waiting for transfers between devices: 33.9 us -> 24.6 us
    pallas_call x3 -> x6, Pallas kernels: 38.3 us -> 53.2 us  [the longest x3 35.6 us: score_gradients(): pl.pallas_call(functools.partial(score_kernel, count), out_shape=[jax.Sha...]
    ppermute x24, waiting for transfers between devices: 33.9 us -> 24.6 us  [stage(): got[h] = lax.ppermute(value, 'leaf', p)]
  transfers between devices with their start and end apart: 24 -> 24, of which waited for: 13 -> 10; matrix products, arithmetic and copies ran while one was open for 5% -> 5% of each run, Pallas kernels for 33% -> 40%
where the time goes in v3:
time: 123 us
  Pallas kernels  53.2 us (43%)
  starting transfers between devices  34.6 us (28%)
  waiting for transfers between devices  24.6 us (20%)
  local copies, waits for them, and re-layouts  5.25 us (4%)
  other arithmetic  4.1 us (3%)
    pallas_call x3, Pallas kernels, score_gradients(): pl.pallas_call(functools.partial(score_kernel, count), out_shape=[jax.Sha...  35.6 us
    ppermute x24, starting transfers between devices, stage(): got[h] = lax.ppermute(value, 'leaf', p)  34.6 us
    ppermute x24, waiting for transfers between devices, stage(): got[h] = lax.ppermute(value, 'leaf', p)  24.6 us
    pallas_call x3, Pallas kernels, own_gradients(): pl.pallas_call(functools.partial(own_kernel, count), input_output_aliases...  17.6 us
  transfers between devices with their start and end apart: 24, of which 10 were waited for; matrix products, arithmetic and copies ran while one was open for 5% of the time, Pallas kernels for 40%

profile of v3, /device:TPU:128, one launch (start us, length us, event | category | flops | bytes accessed | tf_op | source)
XLA Modules:
  0.0 122.7 jit_solution(16734786066713304389)
XLA Ops:
  0.6 1.1 fusion.25
  1.7 1.6 %collective-permute-start = (bf16[128,768]{1,0:T(8,128)(2,1)S(1)}, bf16[128,768]{1,0:T(8,128)(2,1)S(1)}, u32[]{:S(2)}, u32[]{:S(2)}) collective-permute-start(bf16[128,768]{1,0:T(8,128)(2,1)S(1)} %pad_maximum_fusion), channel_id=1, source_target_pairs={{0,1},{1,0},{2,3},{3,2},{4,5},{5,4},{6,7},{7,6},{8,9},{9,8},{10,11... | collective-permute-start | bytes 589832 | tf_op jit(solution)/shard_map/ppermute | solution.py:267
  3.3 0.8 slice.105
  4.2 0.8 slice.106
  5.0 0.8 fusion.33
  5.9 2.6 %collective-permute-done.refs_1_.refs_7_ = bf16[128,768]{1,0:T(8,128)(2,1)S(1)} collective-permute-done((bf16[128,768]{1,0:T(8,128)(2,1)S(1)}, bf16[128,768]{1,0:T(8,128)(2,1)S(1)}, u32[]{:S(2)}, u32[]{:S(2)}) %collective-permute-start) | collective-permute-done | bytes 196640 | tf_op jit(solution)/shard_map/ppermute | solution.py:267
  8.5 1.6 %collective-permute-start.2 = (bf16[128,768]{1,0:T(8,128)(2,1)S(1)}, bf16[128,768]{1,0:T(8,128)(2,1)S(1)}, u32[]{:S(2)}, u32[]{:S(2)}) collective-permute-start(bf16[128,768]{1,0:T(8,128)(2,1)S(1)} %pad_maximum_fusion.1), channel_id=1, source_target_pairs={{0,1},{1,0},{2,3},{3,2},{4,5},{5,4},{6,7},{7,6},{8,9},{9,8},{10,11... | collective-permute-start | bytes 589832 | tf_op jit(solution)/shard_map/ppermute | solution.py:267
  10.1 0.6 gather_fusion
  10.9 2.2 %collective-permute-start.1 = (bf16[128,768]{1,0:T(8,128)(2,1)S(1)}, bf16[128,768]{1,0:T(8,128)(2,1)S(1)}, u32[]{:S(2)}, u32[]{:S(2)}) collective-permute-start(bf16[128,768]{1,0:T(8,128)(2,1)S(1)} %broadcast_select_fusion.3), channel_id=1, source_target_pairs={{0,3},{1,2},{2,1},{3,0},{4,7},{5,6},{6,5},{7,4},{8,11},{9,10},{10,... | collective-permute-start | bytes 589832 | tf_op jit(solution)/shard_map/ppermute | solution.py:267
  13.1 1.3 %collective-permute-done.2.refs_1_.refs_7_ = bf16[128,768]{1,0:T(8,128)(2,1)S(1)} collective-permute-done((bf16[128,768]{1,0:T(8,128)(2,1)S(1)}, bf16[128,768]{1,0:T(8,128)(2,1)S(1)}, u32[]{:S(2)}, u32[]{:S(2)}) %collective-permute-start.2) | collective-permute-done | bytes 196640 | tf_op jit(solution)/shard_map/ppermute | solution.py:267
  14.5 3.4 %collective-permute-done.1.refs_2_.refs_8_ = bf16[128,768]{1,0:T(8,128)(2,1)S(1)} collective-permute-done((bf16[128,768]{1,0:T(8,128)(2,1)S(1)}, bf16[128,768]{1,0:T(8,128)(2,1)S(1)}, u32[]{:S(2)}, u32[]{:S(2)}) %collective-permute-start.1) | collective-permute-done | bytes 196640 | tf_op jit(solution)/shard_map/ppermute | solution.py:267
  18.0 0.6 constant_dynamic-update-slice_fusion
  18.6 1.6 %collective-permute-start.4 = (bf16[128,768]{1,0:T(8,128)(2,1)S(1)}, bf16[128,768]{1,0:T(8,128)(2,1)S(1)}, u32[]{:S(2)}, u32[]{:S(2)}) collective-permute-start(bf16[128,768]{1,0:T(8,128)(2,1)S(1)} %select_select_fusion.1), channel_id=1, source_target_pairs={{0,4},{4,0},{8,12},{12,8},{1,5},{5,1},{9,13},{13,9},{2,6},{6,2},{1... | collective-permute-start | bytes 589832 | tf_op jit(solution)/shard_map/ppermute | solution.py:267
  20.2 2.1 %collective-permute-start.5 = (bf16[128,768]{1,0:T(8,128)(2,1)S(1)}, bf16[128,768]{1,0:T(8,128)(2,1)S(1)}, u32[]{:S(2)}, u32[]{:S(2)}) collective-permute-start(bf16[128,768]{1,0:T(8,128)(2,1)S(1)} %broadcast_select_fusion.2), channel_id=1, source_target_pairs={{0,3},{1,2},{2,1},{3,0},{4,7},{5,6},{6,5},{7,4},{8,11},{9,10},{10,... | collective-permute-start | bytes 589832 | tf_op jit(solution)/shard_map/ppermute | solution.py:267
  22.3 0.7 collective-permute-done.3.refs_1_.refs_7_
  23.0 4.1 %collective-permute-done.5.refs_2_.refs_8_ = bf16[128,768]{1,0:T(8,128)(2,1)S(1)} collective-permute-done((bf16[128,768]{1,0:T(8,128)(2,1)S(1)}, bf16[128,768]{1,0:T(8,128)(2,1)S(1)}, u32[]{:S(2)}, u32[]{:S(2)}) %collective-permute-start.5) | collective-permute-done | bytes 196640 | tf_op jit(solution)/shard_map/ppermute | solution.py:267
  27.2 2.2 %collective-permute-start.6 = (bf16[128,512]{1,0:T(8,128)(2,1)S(1)}, bf16[128,512]{1,0:T(8,128)(2,1)S(1)}, u32[]{:S(2)}, u32[]{:S(2)}) collective-permute-start(bf16[128,512]{1,0:T(8,128)(2,1)S(1)} %broadcast_select_fusion.4), channel_id=1, source_target_pairs={{0,3},{1,2},{2,1},{3,0},{4,7},{5,6},{6,5},{7,4},{8,11},{9,10},{10,... | collective-permute-start | bytes 393224 | tf_op jit(solution)/shard_map/ppermute | solution.py:267
  29.4 0.8 concatenate.47.info
  30.2 0.5 collective-permute-start.7
  30.6 3.0 %collective-permute-start.8 = (bf16[128,768]{1,0:T(8,128)(2,1)S(1)}, bf16[128,768]{1,0:T(8,128)(2,1)S(1)}, u32[]{:S(2)}, u32[]{:S(2)}) collective-permute-start(bf16[128,768]{1,0:T(8,128)(2,1)S(1)} %broadcast_select_fusion.1), channel_id=1, source_target_pairs={{0,12},{4,8},{8,4},{12,0},{1,13},{5,9},{9,5},{13,1},{2,14},{6,10},... | collective-permute-start | bytes 589832 | tf_op jit(solution)/shard_map/ppermute | solution.py:267
  33.7 3.0 %collective-permute-done.7.refs_3_.refs_9_ = bf16[128,768]{1,0:T(8,128)(2,1)S(1)} collective-permute-done((bf16[128,768]{1,0:T(8,128)(2,1)S(1)}, bf16[128,768]{1,0:T(8,128)(2,1)S(1)}, u32[]{:S(2)}, u32[]{:S(2)}) %collective-permute-start.7) | collective-permute-done | bytes 196640 | tf_op jit(solution)/shard_map/ppermute | solution.py:267
  36.7 2.0 %collective-permute-done.8.refs_4_.refs_10_ = bf16[128,768]{1,0:T(8,128)(2,1)S(1)} collective-permute-done((bf16[128,768]{1,0:T(8,128)(2,1)S(1)}, bf16[128,768]{1,0:T(8,128)(2,1)S(1)}, u32[]{:S(2)}, u32[]{:S(2)}) %collective-permute-start.8) | collective-permute-done | bytes 196640 | tf_op jit(solution)/shard_map/ppermute | solution.py:267
  38.9 3.2 %collective-permute-start.10 = (bf16[128,768]{1,0:T(8,128)(2,1)S(1)}, bf16[128,768]{1,0:T(8,128)(2,1)S(1)}, u32[]{:S(2)}, u32[]{:S(2)}) collective-permute-start(bf16[128,768]{1,0:T(8,128)(2,1)S(1)} %broadcast_select_fusion), channel_id=1, source_target_pairs={{0,12},{4,8},{8,4},{12,0},{1,13},{5,9},{9,5},{13,1},{2,14},{6,10},... | collective-permute-start | bytes 589832 | tf_op jit(solution)/shard_map/ppermute | solution.py:267
  42.1 13.1 %shard_map.76 = (bf16[128,768]{1,0:T(8,128)(2,1)S(1)}, bf16[128,768]{1,0:T(8,128)(2,1)S(1)}, bf16[128,768]{1,0:T(8,128)(2,1)S(1)}, bf16[128,768]{1,0:T(8,128)(2,...) custom-call(s32[16]{0:T(128)S(1)} %concatenate.47.info, bf16[256,5120]{1,0:T(8,128)(2,1)} %bitcast.57, ...), custom_call_target="tpu_custom_call" | custom-call | flops 10800000000 | bytes 12582912 | tf_op jit(solution)/shard_map/pallas_call | solution.py:149
  55.2 0.2 collective-permute-start.11
  55.4 3.1 %collective-permute-start.12 = (bf16[128,768]{1,0:T(8,128)(2,1)S(1)}, bf16[128,768]{1,0:T(8,128)(2,1)S(1)}, u32[]{:S(2)}, u32[]{:S(2)}) collective-permute-start(bf16[128,768]{1,0:T(8,128)(2,1)S(1)} %get-tuple-element.85), channel_id=1, source_target_pairs={{0,12},{4,8},{8,4},{12,0},{1,13},{5,9},{9,5},{13,1},{2,14},{6,10},... | collective-permute-start | bytes 589832 | tf_op jit(solution)/shard_map/ppermute | solution.py:267
  58.5 13.1 %shard_map.77 = (bf16[128,768]{1,0:T(8,128)(2,1)S(1)}, bf16[128,768]{1,0:T(8,128)(2,1)S(1)}, bf16[128,768]{1,0:T(8,128)(2,1)S(1)}, bf16[128,768]{1,0:T(8,128)(2,...) custom-call(s32[16]{0:T(128)S(1)} %concatenate.47.info, bf16[256,5120]{1,0:T(8,128)(2,1)} %bitcast.58, ...), custom_call_target="tpu_custom_call" | custom-call | flops 10800000000 | bytes 12582912 | tf_op jit(solution)/shard_map/pallas_call | solution.py:149
  71.7 0.4 collective-permute-start.13
  72.2 9.4 %shard_map.78 = (bf16[128,512]{1,0:T(8,128)(2,1)S(1)}, bf16[128,512]{1,0:T(8,128)(2,1)S(1)}, bf16[128,512]{1,0:T(8,128)(2,1)S(1)}, bf16[128,512]{1,0:T(8,128)(2,...) custom-call(s32[16]{0:T(128)S(1)} %concatenate.47.info, bf16[256,5120]{1,0:T(8,128)(2,1)} %bitcast.59, ...), custom_call_target="tpu_custom_call" | custom-call | flops 7200000000 | bytes 8388608 | tf_op jit(solution)/shard_map/pallas_call | solution.py:149
  81.8 2.9 %collective-permute-start.15 = (bf16[128,512]{1,0:T(8,128)(2,1)S(1)}, bf16[128,512]{1,0:T(8,128)(2,1)S(1)}, u32[]{:S(2)}, u32[]{:S(2)}) collective-permute-start(bf16[128,512]{1,0:T(8,128)(2,1)S(1)} %get-tuple-element.98), channel_id=1, source_target_pairs={{0,12},{4,8},{8,4},{12,0},{1,13},{5,9},{9,5},{13,1},{2,14},{6,10},... | collective-permute-start | bytes 393224 | tf_op jit(solution)/shard_map/ppermute | solution.py:267
  84.8 1.4 %collective-permute-start.16 = (bf16[128,768]{1,0:T(8,128)(2,1)S(1)}, bf16[128,768]{1,0:T(8,128)(2,1)S(1)}, u32[]{:S(2)}, u32[]{:S(2)}) collective-permute-start(bf16[128,768]{1,0:T(8,128)(2,1)S(1)} %fusion.4), channel_id=1, source_target_pairs={{0,4},{4,0},{8,12},{12,8},{1,5},{5,1},{9,13},{13,9},{2,6},{6,2},{1... | collective-permute-start | bytes 589832 | tf_op jit(solution)/shard_map/ppermute | solution.py:267
  86.2 1.5 %collective-permute-start.17 = (bf16[128,768]{1,0:T(8,128)(2,1)S(1)}, bf16[128,768]{1,0:T(8,128)(2,1)S(1)}, u32[]{:S(2)}, u32[]{:S(2)}) collective-permute-start(bf16[128,768]{1,0:T(8,128)(2,1)S(1)} %add_convert_fusion.1), channel_id=1, source_target_pairs={{0,3},{1,2},{2,1},{3,0},{4,7},{5,6},{6,5},{7,4},{8,11},{9,10},{10,... | collective-permute-start | bytes 589832 | tf_op jit(solution)/shard_map/ppermute | solution.py:267
  87.7 6.5 %shard_map.79 = (bf16[256,5120]{1,0:T(8,128)(2,1)}, f32[128,768]{1,0:T(8,128)S(1)}, bf16[128,768]{1,0:T(8,128)(2,1)S(1)}) custom-call(s32[16]{0:T(128)S(1)} %concatenate.47.info, bf16[256,5120]{1,0:T(8,128)(2,1)} %bitcast.60, bf16[256,5120]{1,0:T(8,128)(2,1)} %bitcast.66, bf16[256,1024]{1,0:T(8,128)(2,1)S(1)} %bitcast.43, ...), custom_call_target="tpu_custom_call" | custom-call | flops 3900000000 | bytes 12582912 | tf_op jit(solution)/shard_map/pallas_call | solution.py:183
  94.5 0.7 collective-permute-start.18
  95.3 2.3 %collective-permute-start.19 = (bf16[128,768]{1,0:T(8,128)(2,1)S(1)}, bf16[128,768]{1,0:T(8,128)(2,1)S(1)}, u32[]{:S(2)}, u32[]{:S(2)}) collective-permute-start(bf16[128,768]{1,0:T(8,128)(2,1)S(1)} %add_convert_fusion), channel_id=1, source_target_pairs={{0,3},{1,2},{2,1},{3,0},{4,7},{5,6},{6,5},{7,4},{8,11},{9,10},{10,... | collective-permute-start | bytes 589832 | tf_op jit(solution)/shard_map/ppermute | solution.py:267
  97.6 6.5 %shard_map.80 = (bf16[256,5120]{1,0:T(8,128)(2,1)}, f32[128,768]{1,0:T(8,128)S(1)}, bf16[128,768]{1,0:T(8,128)(2,1)S(1)}) custom-call(s32[16]{0:T(128)S(1)} %concatenate.47.info, bf16[256,5120]{1,0:T(8,128)(2,1)} %bitcast.61, bf16[256,5120]{1,0:T(8,128)(2,1)} %bitcast.67, bf16[256,1024]{1,0:T(8,128)(2,1)S(1)} %bitcast.45, ...), custom_call_target="tpu_custom_call", output_to_operand_aliasing={{0}: (11, {})} | custom-call | flops 3900000000 | bytes 12582912 | tf_op jit(solution)/shard_map/pallas_call | solution.py:183
  104.2 0.2 fusion.10
  104.4 0.2 fusion.15
  104.6 4.6 %shard_map.81 = (bf16[256,5120]{1,0:T(8,128)(2,1)}, f32[128,512]{1,0:T(8,128)S(1)}, bf16[128,512]{1,0:T(8,128)(2,1)S(1)}) custom-call(s32[16]{0:T(128)S(1)} %concatenate.47.info, bf16[256,5120]{1,0:T(8,128)(2,1)} %bitcast.62, bf16[256,5120]{1,0:T(8,128)(2,1)} %bitcast.68, bf16[256,1024]{1,0:T(8,128)(2,1)S(1)} %bitcast.47, ...), custom_call_target="tpu_custom_call", output_to_operand_aliasing={{0}: (11, {})} | custom-call | flops 2600000000 | bytes 8388608 | tf_op jit(solution)/shard_map/pallas_call | solution.py:183
  109.2 1.0 collective-permute-start.22
  110.2 1.4 %collective-permute-start.21 = (bf16[128,768]{1,0:T(8,128)(2,1)S(1)}, bf16[128,768]{1,0:T(8,128)(2,1)S(1)}, u32[]{:S(2)}, u32[]{:S(2)}) collective-permute-start(bf16[128,768]{1,0:T(8,128)(2,1)S(1)} %fusion.15), channel_id=1, source_target_pairs={{0,1},{1,0},{2,3},{3,2},{4,5},{5,4},{6,7},{7,6},{8,9},{9,8},{10,11... | collective-permute-start | bytes 589832 | tf_op jit(solution)/shard_map/ppermute | solution.py:267
  111.7 3.8 %collective-permute-done.22 = bf16[128,512]{1,0:T(8,128)(2,1)S(1)} collective-permute-done((bf16[128,512]{1,0:T(8,128)(2,1)S(1)}, bf16[128,512]{1,0:T(8,128)(2,1)S(1)}, u32[]{:S(2)}, u32[]{:S(2)}) %collective-permute-start.22) | collective-permute-done | bytes 131104 | tf_op jit(solution)/shard_map/ppermute | solution.py:267
  115.5 0.3 collective-permute-done.21
  115.9 1.4 %collective-permute-start.23 = (bf16[128,512]{1,0:T(8,128)(2,1)S(1)}, bf16[128,512]{1,0:T(8,128)(2,1)S(1)}, u32[]{:S(2)}, u32[]{:S(2)}) collective-permute-start(bf16[128,512]{1,0:T(8,128)(2,1)S(1)} %fusion.23), channel_id=1, source_target_pairs={{0,1},{1,0},{2,3},{3,2},{4,5},{5,4},{6,7},{7,6},{8,9},{9,8},{10,11... | collective-permute-start | bytes 393224 | tf_op jit(solution)/shard_map/ppermute | solution.py:267
  117.3 0.2 fusion.13
  117.5 3.4 %collective-permute-done.23 = bf16[128,512]{1,0:T(8,128)(2,1)S(1)} collective-permute-done((bf16[128,512]{1,0:T(8,128)(2,1)S(1)}, bf16[128,512]{1,0:T(8,128)(2,1)S(1)}, u32[]{:S(2)}, u32[]{:S(2)}) %collective-permute-start.23) | collective-permute-done | bytes 131104 | tf_op jit(solution)/shard_map/ppermute | solution.py:267
  121.0 0.8 maximum_bitcast_fusion.1
  121.9 0.8 maximum_bitcast_fusion
  (64 shorter events, 2.0 us)
Async XLA Ops:
  1.7 6.7 %collective-permute-start = (bf16[128,768]{1,0:T(8,128)(2,1)S(1)}, bf16[128,768]{1,0:T(8,128)(2,1)S(1)}, u32[]{:S(2)}, u32[]{:S(2)}) collective-permute-start(bf16[128,768]{1,0:T(8,128)(2,1)S(1)} %pad_maximum_fusion), channel_id=1, source_target_pairs={{0,1},{1,0},{2,3},{3,2},{4,5},{5,4},{6,7},{7,6},{8,9},{9,8},{10,11... | collective-permute-start | bytes 589832 | tf_op jit(solution)/shard_map/ppermute | solution.py:267
  8.5 33.6 %copy-start = (bf16[1,2,128,1024]{3,2,1,0:T(8,128)(2,1)S(1)}, bf16[1,2,128,1024]{3,2,1,0:T(8,128)(2,1)}, u32[]{:S(2)}) copy-start(bf16[1,2,128,1024]{3,2,1,0:T(8,128)(2,1)} %param.8) | copy-start | bytes 1572868
  8.5 33.5 %copy-start.3 = (bf16[1,2,128,1024]{3,2,1,0:T(8,128)(2,1)S(1)}, bf16[1,2,128,1024]{3,2,1,0:T(8,128)(2,1)}, u32[]{:S(2)}) copy-start(bf16[1,2,128,1024]{3,2,1,0:T(8,128)(2,1)} %param.9) | copy-start | bytes 1572868
  8.5 5.9 %collective-permute-start.2 = (bf16[128,768]{1,0:T(8,128)(2,1)S(1)}, bf16[128,768]{1,0:T(8,128)(2,1)S(1)}, u32[]{:S(2)}, u32[]{:S(2)}) collective-permute-start(bf16[128,768]{1,0:T(8,128)(2,1)S(1)} %pad_maximum_fusion.1), channel_id=1, source_target_pairs={{0,1},{1,0},{2,3},{3,2},{4,5},{5,4},{6,7},{7,6},{8,9},{9,8},{10,11... | collective-permute-start | bytes 589832 | tf_op jit(solution)/shard_map/ppermute | solution.py:267
  10.9 7.0 %collective-permute-start.1 = (bf16[128,768]{1,0:T(8,128)(2,1)S(1)}, bf16[128,768]{1,0:T(8,128)(2,1)S(1)}, u32[]{:S(2)}, u32[]{:S(2)}) collective-permute-start(bf16[128,768]{1,0:T(8,128)(2,1)S(1)} %broadcast_select_fusion.3), channel_id=1, source_target_pairs={{0,3},{1,2},{2,1},{3,0},{4,7},{5,6},{6,5},{7,4},{8,11},{9,10},{10,... | collective-permute-start | bytes 589832 | tf_op jit(solution)/shard_map/ppermute | solution.py:267
  17.9 5.1 %collective-permute-start.3 = (bf16[128,512]{1,0:T(8,128)(2,1)S(1)}, bf16[128,512]{1,0:T(8,128)(2,1)S(1)}, u32[]{:S(2)}, u32[]{:S(2)}) collective-permute-start(bf16[128,512]{1,0:T(8,128)(2,1)S(1)} %pad_maximum_fusion.2), channel_id=1, source_target_pairs={{0,1},{1,0},{2,3},{3,2},{4,5},{5,4},{6,7},{7,6},{8,9},{9,8},{10,11... | collective-permute-start | bytes 393224 | tf_op jit(solution)/shard_map/ppermute | solution.py:267
  18.6 8.5 %collective-permute-start.4 = (bf16[128,768]{1,0:T(8,128)(2,1)S(1)}, bf16[128,768]{1,0:T(8,128)(2,1)S(1)}, u32[]{:S(2)}, u32[]{:S(2)}) collective-permute-start(bf16[128,768]{1,0:T(8,128)(2,1)S(1)} %select_select_fusion.1), channel_id=1, source_target_pairs={{0,4},{4,0},{8,12},{12,8},{1,5},{5,1},{9,13},{13,9},{2,6},{6,2},{1... | collective-permute-start | bytes 589832 | tf_op jit(solution)/shard_map/ppermute | solution.py:267
  20.2 6.9 %collective-permute-start.5 = (bf16[128,768]{1,0:T(8,128)(2,1)S(1)}, bf16[128,768]{1,0:T(8,128)(2,1)S(1)}, u32[]{:S(2)}, u32[]{:S(2)}) collective-permute-start(bf16[128,768]{1,0:T(8,128)(2,1)S(1)} %broadcast_select_fusion.2), channel_id=1, source_target_pairs={{0,3},{1,2},{2,1},{3,0},{4,7},{5,6},{6,5},{7,4},{8,11},{9,10},{10,... | collective-permute-start | bytes 589832 | tf_op jit(solution)/shard_map/ppermute | solution.py:267
  27.2 6.5 %collective-permute-start.6 = (bf16[128,512]{1,0:T(8,128)(2,1)S(1)}, bf16[128,512]{1,0:T(8,128)(2,1)S(1)}, u32[]{:S(2)}, u32[]{:S(2)}) collective-permute-start(bf16[128,512]{1,0:T(8,128)(2,1)S(1)} %broadcast_select_fusion.4), channel_id=1, source_target_pairs={{0,3},{1,2},{2,1},{3,0},{4,7},{5,6},{6,5},{7,4},{8,11},{9,10},{10,... | collective-permute-start | bytes 393224 | tf_op jit(solution)/shard_map/ppermute | solution.py:267
  30.2 6.5 %collective-permute-start.7 = (bf16[128,768]{1,0:T(8,128)(2,1)S(1)}, bf16[128,768]{1,0:T(8,128)(2,1)S(1)}, u32[]{:S(2)}, u32[]{:S(2)}) collective-permute-start(bf16[128,768]{1,0:T(8,128)(2,1)S(1)} %select_select_fusion), channel_id=1, source_target_pairs={{0,4},{4,0},{8,12},{12,8},{1,5},{5,1},{9,13},{13,9},{2,6},{6,2},{1... | collective-permute-start | bytes 589832 | tf_op jit(solution)/shard_map/ppermute | solution.py:267
  30.6 8.1 %collective-permute-start.8 = (bf16[128,768]{1,0:T(8,128)(2,1)S(1)}, bf16[128,768]{1,0:T(8,128)(2,1)S(1)}, u32[]{:S(2)}, u32[]{:S(2)}) collective-permute-start(bf16[128,768]{1,0:T(8,128)(2,1)S(1)} %broadcast_select_fusion.1), channel_id=1, source_target_pairs={{0,12},{4,8},{8,4},{12,0},{1,13},{5,9},{9,5},{13,1},{2,14},{6,10},... | collective-permute-start | bytes 589832 | tf_op jit(solution)/shard_map/ppermute | solution.py:267
  38.8 16.4 %collective-permute-start.9 = (bf16[128,512]{1,0:T(8,128)(2,1)S(1)}, bf16[128,512]{1,0:T(8,128)(2,1)S(1)}, u32[]{:S(2)}, u32[]{:S(2)}) collective-permute-start(bf16[128,512]{1,0:T(8,128)(2,1)S(1)} %select_select_fusion.2), channel_id=1, source_target_pairs={{0,4},{4,0},{8,12},{12,8},{1,5},{5,1},{9,13},{13,9},{2,6},{6,2},{1... | collective-permute-start | bytes 393224 | tf_op jit(solution)/shard_map/ppermute | solution.py:267
  38.9 16.3 %collective-permute-start.10 = (bf16[128,768]{1,0:T(8,128)(2,1)S(1)}, bf16[128,768]{1,0:T(8,128)(2,1)S(1)}, u32[]{:S(2)}, u32[]{:S(2)}) collective-permute-start(bf16[128,768]{1,0:T(8,128)(2,1)S(1)} %broadcast_select_fusion), channel_id=1, source_target_pairs={{0,12},{4,8},{8,4},{12,0},{1,13},{5,9},{9,5},{13,1},{2,14},{6,10},... | collective-permute-start | bytes 589832 | tf_op jit(solution)/shard_map/ppermute | solution.py:267
  55.2 16.5 %collective-permute-start.11 = (bf16[128,512]{1,0:T(8,128)(2,1)S(1)}, bf16[128,512]{1,0:T(8,128)(2,1)S(1)}, u32[]{:S(2)}, u32[]{:S(2)}) collective-permute-start(bf16[128,512]{1,0:T(8,128)(2,1)S(1)} %broadcast_select_fusion.5), channel_id=1, source_target_pairs={{0,12},{4,8},{8,4},{12,0},{1,13},{5,9},{9,5},{13,1},{2,14},{6,10},... | collective-permute-start | bytes 393224 | tf_op jit(solution)/shard_map/ppermute | solution.py:267
  55.4 16.2 %collective-permute-start.12 = (bf16[128,768]{1,0:T(8,128)(2,1)S(1)}, bf16[128,768]{1,0:T(8,128)(2,1)S(1)}, u32[]{:S(2)}, u32[]{:S(2)}) collective-permute-start(bf16[128,768]{1,0:T(8,128)(2,1)S(1)} %get-tuple-element.85), channel_id=1, source_target_pairs={{0,12},{4,8},{8,4},{12,0},{1,13},{5,9},{9,5},{13,1},{2,14},{6,10},... | collective-permute-start | bytes 589832 | tf_op jit(solution)/shard_map/ppermute | solution.py:267
  71.7 15.9 %copy-start.2 = (bf16[768,1280]{1,0:T(8,128)(2,1)S(1)}, bf16[768,1280]{1,0:T(8,128)(2,1)}, u32[]{:S(2)}) copy-start(bf16[768,1280]{1,0:T(8,128)(2,1)} %get-tuple-element.104.refs_7_) | copy-start | bytes 5898244
  71.7 9.9 %collective-permute-start.13 = (bf16[128,768]{1,0:T(8,128)(2,1)S(1)}, bf16[128,768]{1,0:T(8,128)(2,1)S(1)}, u32[]{:S(2)}, u32[]{:S(2)}) collective-permute-start(bf16[128,768]{1,0:T(8,128)(2,1)S(1)} %get-tuple-element.94), channel_id=1, source_target_pairs={{0,12},{4,8},{8,4},{12,0},{1,13},{5,9},{9,5},{13,1},{2,14},{6,10},... | collective-permute-start | bytes 589832 | tf_op jit(solution)/shard_map/ppermute | solution.py:267
  72.1 9.6 %collective-permute-start.14 = (bf16[128,768]{1,0:T(8,128)(2,1)S(1)}, bf16[128,768]{1,0:T(8,128)(2,1)S(1)}, u32[]{:S(2)}, u32[]{:S(2)}) collective-permute-start(bf16[128,768]{1,0:T(8,128)(2,1)S(1)} %fusion.1), channel_id=1, source_target_pairs={{0,4},{4,0},{8,12},{12,8},{1,5},{5,1},{9,13},{13,9},{2,6},{6,2},{1... | collective-permute-start | bytes 589832 | tf_op jit(solution)/shard_map/ppermute | solution.py:267
  81.8 12.4 %collective-permute-start.15 = (bf16[128,512]{1,0:T(8,128)(2,1)S(1)}, bf16[128,512]{1,0:T(8,128)(2,1)S(1)}, u32[]{:S(2)}, u32[]{:S(2)}) collective-permute-start(bf16[128,512]{1,0:T(8,128)(2,1)S(1)} %get-tuple-element.98), channel_id=1, source_target_pairs={{0,12},{4,8},{8,4},{12,0},{1,13},{5,9},{9,5},{13,1},{2,14},{6,10},... | collective-permute-start | bytes 393224 | tf_op jit(solution)/shard_map/ppermute | solution.py:267
  84.8 9.6 %collective-permute-start.16 = (bf16[128,768]{1,0:T(8,128)(2,1)S(1)}, bf16[128,768]{1,0:T(8,128)(2,1)S(1)}, u32[]{:S(2)}, u32[]{:S(2)}) collective-permute-start(bf16[128,768]{1,0:T(8,128)(2,1)S(1)} %fusion.4), channel_id=1, source_target_pairs={{0,4},{4,0},{8,12},{12,8},{1,5},{5,1},{9,13},{13,9},{2,6},{6,2},{1... | collective-permute-start | bytes 589832 | tf_op jit(solution)/shard_map/ppermute | solution.py:267
  86.2 8.1 %collective-permute-start.17 = (bf16[128,768]{1,0:T(8,128)(2,1)S(1)}, bf16[128,768]{1,0:T(8,128)(2,1)S(1)}, u32[]{:S(2)}, u32[]{:S(2)}) collective-permute-start(bf16[128,768]{1,0:T(8,128)(2,1)S(1)} %add_convert_fusion.1), channel_id=1, source_target_pairs={{0,3},{1,2},{2,1},{3,0},{4,7},{5,6},{6,5},{7,4},{8,11},{9,10},{10,... | collective-permute-start | bytes 589832 | tf_op jit(solution)/shard_map/ppermute | solution.py:267
  94.2 3.4 %copy-start.1 = (bf16[768,1280]{1,0:T(8,128)(2,1)S(1)}, bf16[768,1280]{1,0:T(8,128)(2,1)}, u32[]{:S(2)}) copy-start(bf16[768,1280]{1,0:T(8,128)(2,1)} %get-tuple-element.111.refs_7_) | copy-start | bytes 5898244
  94.5 9.6 %collective-permute-start.18 = (bf16[128,512]{1,0:T(8,128)(2,1)S(1)}, bf16[128,512]{1,0:T(8,128)(2,1)S(1)}, u32[]{:S(2)}, u32[]{:S(2)}) collective-permute-start(bf16[128,512]{1,0:T(8,128)(2,1)S(1)} %fusion.17), channel_id=1, source_target_pairs={{0,4},{4,0},{8,12},{12,8},{1,5},{5,1},{9,13},{13,9},{2,6},{6,2},{1... | collective-permute-start | bytes 393224 | tf_op jit(solution)/shard_map/ppermute | solution.py:267
  95.3 9.1 %collective-permute-start.19 = (bf16[128,768]{1,0:T(8,128)(2,1)S(1)}, bf16[128,768]{1,0:T(8,128)(2,1)S(1)}, u32[]{:S(2)}, u32[]{:S(2)}) collective-permute-start(bf16[128,768]{1,0:T(8,128)(2,1)S(1)} %add_convert_fusion), channel_id=1, source_target_pairs={{0,3},{1,2},{2,1},{3,0},{4,7},{5,6},{6,5},{7,4},{8,11},{9,10},{10,... | collective-permute-start | bytes 589832 | tf_op jit(solution)/shard_map/ppermute | solution.py:267
  97.6 6.6 %collective-permute-start.20 = (bf16[128,768]{1,0:T(8,128)(2,1)S(1)}, bf16[128,768]{1,0:T(8,128)(2,1)S(1)}, u32[]{:S(2)}, u32[]{:S(2)}) collective-permute-start(bf16[128,768]{1,0:T(8,128)(2,1)S(1)} %fusion.7), channel_id=1, source_target_pairs={{0,1},{1,0},{2,3},{3,2},{4,5},{5,4},{6,7},{7,6},{8,9},{9,8},{10,11... | collective-permute-start | bytes 589832 | tf_op jit(solution)/shard_map/ppermute | solution.py:267
  109.2 6.3 %collective-permute-start.22 = (bf16[128,512]{1,0:T(8,128)(2,1)S(1)}, bf16[128,512]{1,0:T(8,128)(2,1)S(1)}, u32[]{:S(2)}, u32[]{:S(2)}) collective-permute-start(bf16[128,512]{1,0:T(8,128)(2,1)S(1)} %add_convert_fusion.2), channel_id=1, source_target_pairs={{0,3},{1,2},{2,1},{3,0},{4,7},{5,6},{6,5},{7,4},{8,11},{9,10},{10,... | collective-permute-start | bytes 393224 | tf_op jit(solution)/shard_map/ppermute | solution.py:267
  110.2 5.7 %collective-permute-start.21 = (bf16[128,768]{1,0:T(8,128)(2,1)S(1)}, bf16[128,768]{1,0:T(8,128)(2,1)S(1)}, u32[]{:S(2)}, u32[]{:S(2)}) collective-permute-start(bf16[128,768]{1,0:T(8,128)(2,1)S(1)} %fusion.15), channel_id=1, source_target_pairs={{0,1},{1,0},{2,3},{3,2},{4,5},{5,4},{6,7},{7,6},{8,9},{9,8},{10,11... | collective-permute-start | bytes 589832 | tf_op jit(solution)/shard_map/ppermute | solution.py:267
  115.9 5.0 %collective-permute-start.23 = (bf16[128,512]{1,0:T(8,128)(2,1)S(1)}, bf16[128,512]{1,0:T(8,128)(2,1)S(1)}, u32[]{:S(2)}, u32[]{:S(2)}) collective-permute-start(bf16[128,512]{1,0:T(8,128)(2,1)S(1)} %fusion.23), channel_id=1, source_target_pairs={{0,1},{1,0},{2,3},{3,2},{4,5},{5,4},{6,7},{7,6},{8,9},{9,8},{10,11... | collective-permute-start | bytes 393224 | tf_op jit(solution)/shard_map/ppermute | solution.py:267

commit v4 on v2

--- a/solution.py
+++ b/solution.py
@@ -15,14 +15,16 @@
 BIG = 2.0**30
 SCALE = 1.0 / math.sqrt(D)
 EXP2_SCALE = SCALE * math.log2(math.e)
-CHUNKS = (3, 3, 2)
+CHUNKS = (4, 4)
 
 SWAP = ((0, 1), (1, 0), (2, 3), (3, 2))
 ONWARD = ((0, 3), (1, 2), (2, 1), (3, 0))
-X_SWAP = [(4 * y + s, 4 * y + t) for y in range(4) for s, t in SWAP]
-X_ONWARD = [(4 * y + s, 4 * y + t) for y in range(4) for s, t in ONWARD]
-Y_SWAP = [(4 * s + x, 4 * t + x) for x in range(4) for s, t in SWAP]
-Y_ONWARD = [(4 * s + x, 4 * t + x) for x in range(4) for s, t in ONWARD]
+
+
+def pairs(axis, ring):
+    if axis == "x":
+        return [(4 * y + s, 4 * y + t) for y in range(4) for s, t in ring]
+    return [(4 * s + x, 4 * t + x) for x in range(4) for s, t in ring]
 
 
 def dot(a, b, ca, cb):
@@ -182,42 +184,81 @@
     g = out_grad.reshape(2 * R, -1)
     keys2, values2 = keys.reshape(2 * R, -1), values.reshape(2 * R, -1)
 
-    def permute(array, pairs):
-        return lax.ppermute(array, "leaf", pairs)
-
-    grad_queries = None
-    inner, leaf = [], []
-    first = 0
-    for count in CHUNKS:
-        cols = slice(first * D, (first + count) * D)
-        own = jnp.concatenate([keys2[:R, cols], values2[:R, cols]], axis=1)
-        if first:
-            own, _ = lax.optimization_barrier((own, a))
-        a = permute(own, X_SWAP)
-        b = permute(jnp.where(x_even, own, a), X_ONWARD)
-        upper = jnp.where(x == 0, own, jnp.where(x == 1, a, b))
-        c = permute(upper, Y_SWAP)
-        d = permute(jnp.where(y_even, upper, c), Y_ONWARD)
-        got = [a, b, c, d]
-        k_slots = [(keys2, 0, first)] + [(s, 0, 0) for s in got] + [(keys2, 1, first)]
-        v_slots = [(values2, 0, first)] + [(s, 0, count) for s in got] + [(values2, 1, first)]
-        grad_queries, g_own, g_a, g_b, g_c, g_d, g_leaf = attend_backward(
-            info, q, g, k_slots, v_slots, first, count, grad_queries
-        )
-        f32, bf = jnp.float32, jnp.bfloat16
-        back = permute(g_d, Y_ONWARD).astype(f32)
-        up = jnp.where(y_even, back, 0.0)
-        back2 = permute((g_c.astype(f32) + jnp.where(y_even, 0.0, back)).astype(bf), Y_SWAP).astype(f32)
-        up = up + back2
-        g_own = g_own + jnp.where(x == 0, up, 0.0)
-        g_a = g_a.astype(f32) + jnp.where(x == 1, up, 0.0)
-        g_b = g_b.astype(f32) + jnp.where(x >= 2, up, 0.0)
-        back = permute(g_b.astype(bf), X_ONWARD).astype(f32)
-        back2 = permute((g_a + jnp.where(x_even, 0.0, back)).astype(bf), X_SWAP).astype(f32)
-        g_own = g_own + jnp.where(x_even, back, 0.0) + back2
-        inner.append(g_own.astype(bf))
-        leaf.append(g_leaf)
-        first += count
+    f32, bf = jnp.float32, jnp.bfloat16
+    firsts = [sum(CHUNKS[:c]) for c in range(len(CHUNKS))]
+    sent, got, scored = {}, {}, {}
+
+    def permute(value, axis, ring):
+        return lax.ppermute(value, "leaf", pairs(axis, ring))
+
+    def tie(value, after):
+        return lax.optimization_barrier((value, tuple(after)))[0] if after else value
+
+    def upper_of(c):
+        return jnp.where(x == 0, sent[c], jnp.where(x == 1, got["a", c], got["b", c]))
+
+    def move(name, c, after):
+        if name == "g0":
+            cols = slice(firsts[c] * D, (firsts[c] + CHUNKS[c]) * D)
+            sent[c] = tie(jnp.concatenate([keys2[:R, cols], values2[:R, cols]], axis=1), after)
+            got["a", c] = permute(sent[c], "x", SWAP)
+            return [got["a", c]]
+        if name == "g1":
+            got["b", c] = permute(tie(jnp.where(x_even, sent[c], got["a", c]), after), "x", ONWARD)
+            return [got["b", c]]
+        if name == "g2":
+            got["u", c] = tie(upper_of(c), after)
+            got["c", c] = permute(got["u", c], "y", SWAP)
+            return [got["c", c]]
+        if name == "g3":
+            got["d", c] = permute(tie(jnp.where(y_even, got["u", c], got["c", c]), after), "y", ONWARD)
+            return [got["d", c]]
+        own, a, b, near, far = scored[c][1:6]
+        up = got.get(("up", c))
+        if name == "r0":
+            got[name, c] = permute(tie(far, after), "y", ONWARD).astype(f32)
+        elif name == "r1":
+            value = near.astype(f32) + jnp.where(y_even, 0.0, got["r0", c])
+            got[name, c] = permute(tie(value.astype(bf), after), "y", SWAP).astype(f32)
+            got["up", c] = jnp.where(y_even, got["r0", c], 0.0) + got[name, c]
+        elif name == "r2":
+            value = b.astype(f32) + jnp.where(x >= 2, up, 0.0)
+            got[name, c] = permute(tie(value.astype(bf), after), "x", ONWARD).astype(f32)
+        else:
+            value = a.astype(f32) + jnp.where(x == 1, up, 0.0) + jnp.where(x_even, 0.0, got["r2", c])
+            got[name, c] = permute(tie(value.astype(bf), after), "x", SWAP).astype(f32)
+            total = own + jnp.where(x == 0, up, 0.0) + jnp.where(x_even, got["r2", c], 0.0)
+            got["own", c] = (total + got[name, c]).astype(bf)
+        back = [got[name, c]]
+        return back
+
+    def stage(moves, after):
+        return [r for name, c in moves for r in move(name, c, after)]
+
+    def score(c, after):
+        k_slots = [(keys2, 0, firsts[c])] + [(got[n, c], 0, 0) for n in "abcd"] + [(keys2, 1, firsts[c])]
+        v_slots = [(values2, 0, firsts[c])] + [(got[n, c], 0, CHUNKS[c]) for n in "abcd"]
+        v_slots += [(values2, 1, firsts[c])]
+        before = scored[c - 1][0] if c else None
+        scored[c] = attend_backward(tie(info, after), q, g, k_slots, v_slots, firsts[c], CHUNKS[c], before)
+        return list(scored[c][1:2])
+
+    s1 = stage([("g0", 0)], [])
+    s2 = stage([("g1", 0)], []) + stage([("g0", 1)], s1)
+    s3 = stage([("g2", 0), ("g1", 1)], [])
+    s4 = stage([("g3", 0), ("g2", 1)], [])
+    k0 = score(0, s4)
+    s5 = stage([("g3", 1)], [])
+    s6 = stage([("r0", 0)], s5 + k0)
+    k1 = score(1, s5 + k0)
+    s7 = stage([("r0", 1), ("r1", 0)], s6 + k1)
+    s8 = stage([("r1", 1), ("r2", 0)], [])
+    s9 = stage([("r2", 1), ("r3", 0)], [])
+    stage([("r3", 1)], [])
+
+    grad_queries = scored[len(CHUNKS) - 1][0]
+    inner = [got["own", c] for c in range(len(CHUNKS))]
+    leaf = [scored[c][6] for c in range(len(CHUNKS))]
 
     def assemble(half):
         rows = []

time: 117 us -> 107 us (0.915)
  starting transfers between devices: 34.5 us -> 25.8 us
  Pallas kernels: 38.3 us -> 36.1 us
  local copies, waits for them, and re-layouts: 5.23 us -> 3.49 us
  other arithmetic: 3.96 us -> 5.41 us
    ppermute x24 -> x16, starting transfers between devices: 34.5 us -> 25.8 us  [permute(): return lax.ppermute(value, 'leaf', pairs(axis, ring))]
    pallas_call x3 -> x2, Pallas kernels: 38.3 us -> 36.1 us  [attend_backward(): pl.pallas_call(functools.partial(kernel, count), input_output_aliases=ali...]
    slice x3 -> x1, local copies, waits for them, and re-layouts: 2.77 us -> 1.13 us  [move(): keys2[:R, cols]]
    select_n x9 -> x6, other arithmetic: 0.29 us -> 1.73 us  [the longest x2 0.8 us: move(): jnp.where(x_even, sent[c], got['a', c])]
    ppermute x24 -> x16, waiting for transfers between devices: 33.9 us -> 34 us  [permute(): return lax.ppermute(value, 'leaf', pairs(axis, ring))]
  transfers between devices with their start and end apart: 24 -> 16, of which waited for: 13 -> 12; matrix products, arithmetic and copies ran while one was open for 5% -> 5% of each run, Pallas kernels for 33% -> 34%
where the time goes in v4:
time: 107 us; the launch traced here: 106 us
  Pallas kernels  36.1 us (34%)
  waiting for transfers between devices  34 us (32%)
  starting transfers between devices  25.8 us (24%)
  other arithmetic  5.41 us (5%)
  local copies, waits for them, and re-layouts  3.49 us (3%)
    pallas_call x2, Pallas kernels, attend_backward(): pl.pallas_call(functools.partial(kernel, count), input_output_aliases=ali...  36.1 us
    ppermute x16, waiting for transfers between devices, permute(): return lax.ppermute(value, 'leaf', pairs(axis, ring))  34 us
    ppermute x16, starting transfers between devices, permute(): return lax.ppermute(value, 'leaf', pairs(axis, ring))  25.8 us
  transfers between devices with their start and end apart: 16, of which 12 were waited for; matrix products, arithmetic and copies ran while one was open for 5% of the time, Pallas kernels for 34%

profile of v4, /device:TPU:128, one launch (start us, length us, event | category | flops | bytes accessed | tf_op | source)
XLA Modules:
  0.0 105.7 jit_solution(3944672437825696920)
XLA Ops:
  0.6 1.1 %fusion.14 = (bf16[128,512]{1,0:T(8,128)(2,1)S(1)}, bf16[128,512]{1,0:T(8,128)(2,1)S(1)}, bf16[128,512]{1,0:T(8,128)(2,1)S(1)}, bf16[128,512]{1,0:T(8,128)(2,1)S(1)}) fusion(bf16[256,1024]{1,0:T(8,128)(2,1)} %bitcast.35, bf16[256,1024]{1,0:T(8,128)(2,1)} %bitcast.40), kind=kLoop, calls=%fused_computation.52 | loop fusion | bytes 1048576 | tf_op jit(solution)/shard_map/slice | solution.py:203
  1.8 1.6 %collective-permute-start = (bf16[128,1024]{1,0:T(8,128)(2,1)S(1)}, bf16[128,1024]{1,0:T(8,128)(2,1)S(1)}, u32[]{:S(2)}, u32[]{:S(2)}) collective-permute-start(bf16[128,1024]{1,0:T(8,128)(2,1)S(1)} %pad_maximum_fusion.1), channel_id=1, source_target_pairs={{0,1},{1,0},{2,3},{3,2},{4,5},{5,4},{6,7},{7,6},{8,9},{9,8},{10,11... | collective-permute-start | bytes 786440 | tf_op jit(solution)/shard_map/ppermute | solution.py:192
  3.4 0.8 fusion.20
  4.1 5.8 %collective-permute-done.refs_1_.refs_7_ = bf16[128,1024]{1,0:T(8,128)(2,1)S(1)} collective-permute-done((bf16[128,1024]{1,0:T(8,128)(2,1)S(1)}, bf16[128,1024]{1,0:T(8,128)(2,1)S(1)}, u32[]{:S(2)}, u32[]{:S(2)}) %collective-permute-start) | collective-permute-done | bytes 262176 | tf_op jit(solution)/shard_map/ppermute | solution.py:192
  10.0 2.8 %collective-permute-start.5 = (bf16[128,1024]{1,0:T(8,128)(2,1)S(1)}, bf16[128,1024]{1,0:T(8,128)(2,1)S(1)}, u32[]{:S(2)}, u32[]{:S(2)}) collective-permute-start(bf16[128,1024]{1,0:T(8,128)(2,1)S(1)} %broadcast_select_fusion), channel_id=1, source_target_pairs={{0,3},{1,2},{2,1},{3,0},{4,7},{5,6},{6,5},{7,4},{8,11},{9,10},{10,... | collective-permute-start | bytes 786440 | tf_op jit(solution)/shard_map/ppermute | solution.py:192
  12.9 0.1 stack.60
  13.0 0.2 collective-permute-start.1
  13.3 5.2 %collective-permute-done.5.refs_2_.refs_8_ = bf16[128,1024]{1,0:T(8,128)(2,1)S(1)} collective-permute-done((bf16[128,1024]{1,0:T(8,128)(2,1)S(1)}, bf16[128,1024]{1,0:T(8,128)(2,1)S(1)}, u32[]{:S(2)}, u32[]{:S(2)}) %collective-permute-start.5) | collective-permute-done | bytes 262176 | tf_op jit(solution)/shard_map/ppermute | solution.py:192
  18.5 0.1 select_select_fusion
  18.6 1.7 %collective-permute-start.6 = (bf16[128,1024]{1,0:T(8,128)(2,1)S(1)}, bf16[128,1024]{1,0:T(8,128)(2,1)S(1)}, u32[]{:S(2)}, u32[]{:S(2)}) collective-permute-start(bf16[128,1024]{1,0:T(8,128)(2,1)S(1)} %select_select_fusion), channel_id=1, source_target_pairs={{0,4},{4,0},{8,12},{12,8},{1,5},{5,1},{9,13},{13,9},{2,6},{6,2},{1... | collective-permute-start | bytes 786440 | tf_op jit(solution)/shard_map/ppermute | solution.py:192
  20.3 0.7 broadcast_select_fusion.1
  21.0 2.8 %collective-permute-start.2 = (bf16[128,1024]{1,0:T(8,128)(2,1)}, bf16[128,1024]{1,0:T(8,128)(2,1)S(1)}, u32[]{:S(2)}, u32[]{:S(2)}) collective-permute-start(bf16[128,1024]{1,0:T(8,128)(2,1)} %broadcast_select_fusion.1), channel_id=1, source_target_pairs={{0,3},{1,2},{2,1},{3,0},{4,7},{5,6},{6,5},{7,4},{8,11},{9,10},{10,... | collective-permute-start | bytes 786440 | tf_op jit(solution)/shard_map/ppermute | solution.py:192
  23.7 0.6 gather_fusion
  24.4 0.1 stack.54
  24.5 0.6 collective-permute-done.6.refs_3_.refs_9_
  25.0 0.7 broadcast_select_fusion.2
  25.8 3.0 %collective-permute-start.7 = (bf16[128,1024]{1,0:T(8,128)(2,1)}, bf16[128,1024]{1,0:T(8,128)(2,1)S(1)}, u32[]{:S(2)}, u32[]{:S(2)}) collective-permute-start(bf16[128,1024]{1,0:T(8,128)(2,1)} %broadcast_select_fusion.2), channel_id=1, source_target_pairs={{0,12},{4,8},{8,4},{12,0},{1,13},{5,9},{9,5},{13,1},{2,14},{6,10},... | collective-permute-start | bytes 786440 | tf_op jit(solution)/shard_map/ppermute | solution.py:192
  28.9 1.3 %collective-permute-start.3 = (bf16[128,1024]{1,0:T(8,128)(2,1)S(1)}, bf16[128,1024]{1,0:T(8,128)(2,1)S(1)}, u32[]{:S(2)}, u32[]{:S(2)}) collective-permute-start(bf16[128,1024]{1,0:T(8,128)(2,1)S(1)} %select_select_fusion.1), channel_id=1, source_target_pairs={{0,4},{4,0},{8,12},{12,8},{1,5},{5,1},{9,13},{13,9},{2,6},{6,2},{1... | collective-permute-start | bytes 786440 | tf_op jit(solution)/shard_map/ppermute | solution.py:192
  30.2 0.6 constant_dynamic-update-slice_fusion
  30.8 0.7 concatenate.44.info
  31.5 2.1 %collective-permute-done.7.refs_4_.refs_10_ = bf16[128,1024]{1,0:T(8,128)(2,1)S(1)} collective-permute-done((bf16[128,1024]{1,0:T(8,128)(2,1)}, bf16[128,1024]{1,0:T(8,128)(2,1)S(1)}, u32[]{:S(2)}, u32[]{:S(2)}) %collective-permute-start.7) | collective-permute-done | bytes 262176 | tf_op jit(solution)/shard_map/ppermute | solution.py:192
  33.6 1.7 %collective-permute-done.3.refs_3_.refs_9_ = bf16[128,1024]{1,0:T(8,128)(2,1)S(1)} collective-permute-done((bf16[128,1024]{1,0:T(8,128)(2,1)S(1)}, bf16[128,1024]{1,0:T(8,128)(2,1)S(1)}, u32[]{:S(2)}, u32[]{:S(2)}) %collective-permute-start.3) | collective-permute-done | bytes 262176 | tf_op jit(solution)/shard_map/ppermute | solution.py:192
  35.3 2.8 %collective-permute-start.4 = (bf16[128,1024]{1,0:T(8,128)(2,1)S(1)}, bf16[128,1024]{1,0:T(8,128)(2,1)S(1)}, u32[]{:S(2)}, u32[]{:S(2)}) collective-permute-start(bf16[128,1024]{1,0:T(8,128)(2,1)S(1)} %broadcast_select_fusion.3), channel_id=1, source_target_pairs={{0,12},{4,8},{8,4},{12,0},{1,13},{5,9},{9,5},{13,1},{2,14},{6,10},... | collective-permute-start | bytes 786440 | tf_op jit(solution)/shard_map/ppermute | solution.py:192
  38.1 18.1 %shard_map.76 = (bf16[256,5120]{1,0:T(8,128)(2,1)}, f32[128,1024]{1,0:T(8,128)S(1)}, bf16[128,1024]{1,0:T(8,128)(2,1)S(1)}, bf16[128,1024]{1,0:T(8,128)(2,1)S(1)...) custom-call(s32[16]{0:T(128)S(1)} %concatenate.44.info, ...), custom_call_target="tpu_custom_call" | custom-call | flops 18400000000 | bytes 4194304 | tf_op jit(solution)/shard_map/pallas_call | solution.py:133
  56.2 0.8 collective-permute-start.8
  57.0 18.1 %shard_map.77 = (bf16[256,5120]{1,0:T(8,128)(2,1)}, f32[128,1024]{1,0:T(8,128)S(1)}, bf16[128,1024]{1,0:T(8,128)(2,1)S(1)}, bf16[128,1024]{1,0:T(8,128)(2,1)S(1)...) custom-call(s32[16]{0:T(128)S(1)} %concatenate.44.info, ...), custom_call_target="tpu_custom_call", output_to_operand_aliasing={{0}: (15, {})} | custom-call | flops 18400000000 | bytes 4194304 | tf_op jit(solution)/shard_map/pallas_call | solution.py:133
  75.1 2.7 %collective-permute-start.12 = (bf16[128,1024]{1,0:T(8,128)(2,1)S(1)}, bf16[128,1024]{1,0:T(8,128)(2,1)S(1)}, u32[]{:S(2)}, u32[]{:S(2)}) collective-permute-start(bf16[128,1024]{1,0:T(8,128)(2,1)S(1)} %get-tuple-element.49), channel_id=1, source_target_pairs={{0,12},{4,8},{8,4},{12,0},{1,13},{5,9},{9,5},{13,1},{2,14},{6,10},... | collective-permute-start | bytes 786440 | tf_op jit(solution)/shard_map/ppermute | solution.py:192
  77.9 0.1 collective-permute-start.9
  78.0 4.7 %collective-permute-done.12 = bf16[128,1024]{1,0:T(8,128)(2,1)S(1)} collective-permute-done((bf16[128,1024]{1,0:T(8,128)(2,1)S(1)}, bf16[128,1024]{1,0:T(8,128)(2,1)S(1)}, u32[]{:S(2)}, u32[]{:S(2)}) %collective-permute-start.12) | collective-permute-done | bytes 262176 | tf_op jit(solution)/shard_map/ppermute | solution.py:192
  82.8 0.1 collective-permute-start.13
  82.9 2.3 %collective-permute-done.9 = bf16[128,1024]{1,0:T(8,128)(2,1)S(1)} collective-permute-done((bf16[128,1024]{1,0:T(8,128)(2,1)S(1)}, bf16[128,1024]{1,0:T(8,128)(2,1)S(1)}, u32[]{:S(2)}, u32[]{:S(2)}) %collective-permute-start.9) | collective-permute-done | bytes 262176 | tf_op jit(solution)/shard_map/ppermute | solution.py:192
  85.1 0.1 add_convert_fusion.1
  85.3 2.8 %collective-permute-start.10 = (bf16[128,1024]{1,0:T(8,128)(2,1)S(1)}, bf16[128,1024]{1,0:T(8,128)(2,1)S(1)}, u32[]{:S(2)}, u32[]{:S(2)}) collective-permute-start(bf16[128,1024]{1,0:T(8,128)(2,1)S(1)} %add_convert_fusion.1), channel_id=1, source_target_pairs={{0,3},{1,2},{2,1},{3,0},{4,7},{5,6},{6,5},{7,4},{8,11},{9,10},{10,... | collective-permute-start | bytes 786440 | tf_op jit(solution)/shard_map/ppermute | solution.py:192
  88.1 1.1 %collective-permute-done.13 = bf16[128,1024]{1,0:T(8,128)(2,1)S(1)} collective-permute-done((bf16[128,1024]{1,0:T(8,128)(2,1)S(1)}, bf16[128,1024]{1,0:T(8,128)(2,1)S(1)}, u32[]{:S(2)}, u32[]{:S(2)}) %collective-permute-start.13) | collective-permute-done | bytes 262176 | tf_op jit(solution)/shard_map/ppermute | solution.py:192
  89.2 0.1 add_convert_fusion
  89.4 2.9 %collective-permute-start.14 = (bf16[128,1024]{1,0:T(8,128)(2,1)S(1)}, bf16[128,1024]{1,0:T(8,128)(2,1)S(1)}, u32[]{:S(2)}, u32[]{:S(2)}) collective-permute-start(bf16[128,1024]{1,0:T(8,128)(2,1)S(1)} %add_convert_fusion), channel_id=1, source_target_pairs={{0,3},{1,2},{2,1},{3,0},{4,7},{5,6},{6,5},{7,4},{8,11},{9,10},{10,... | collective-permute-start | bytes 786440 | tf_op jit(solution)/shard_map/ppermute | solution.py:192
  92.2 0.9 collective-permute-done.10
  93.1 0.2 fusion.4
  93.3 0.1 collective-permute-start.11
  93.5 3.6 %collective-permute-done.14 = bf16[128,1024]{1,0:T(8,128)(2,1)S(1)} collective-permute-done((bf16[128,1024]{1,0:T(8,128)(2,1)S(1)}, bf16[128,1024]{1,0:T(8,128)(2,1)S(1)}, u32[]{:S(2)}, u32[]{:S(2)}) %collective-permute-start.14) | collective-permute-done | bytes 262176 | tf_op jit(solution)/shard_map/ppermute | solution.py:192
  97.0 0.2 fusion.12
  97.2 0.1 collective-permute-start.15
  97.3 2.4 %collective-permute-done.11 = bf16[128,1024]{1,0:T(8,128)(2,1)S(1)} collective-permute-done((bf16[128,1024]{1,0:T(8,128)(2,1)S(1)}, bf16[128,1024]{1,0:T(8,128)(2,1)S(1)}, u32[]{:S(2)}, u32[]{:S(2)}) %collective-permute-start.11) | collective-permute-done | bytes 262176 | tf_op jit(solution)/shard_map/ppermute | solution.py:192
  99.8 0.2 fusion.2
  100.0 3.7 %collective-permute-done.15 = bf16[128,1024]{1,0:T(8,128)(2,1)S(1)} collective-permute-done((bf16[128,1024]{1,0:T(8,128)(2,1)S(1)}, bf16[128,1024]{1,0:T(8,128)(2,1)S(1)}, u32[]{:S(2)}, u32[]{:S(2)}) %collective-permute-start.15) | collective-permute-done | bytes 262176 | tf_op jit(solution)/shard_map/ppermute | solution.py:192
  103.7 0.2 fusion.10
  104.0 0.8 maximum_bitcast_fusion.1
  104.8 0.8 maximum_bitcast_fusion
  (28 shorter events, 0.6 us)
Async XLA Ops:
  1.8 8.1 %collective-permute-start = (bf16[128,1024]{1,0:T(8,128)(2,1)S(1)}, bf16[128,1024]{1,0:T(8,128)(2,1)S(1)}, u32[]{:S(2)}, u32[]{:S(2)}) collective-permute-start(bf16[128,1024]{1,0:T(8,128)(2,1)S(1)} %pad_maximum_fusion.1), channel_id=1, source_target_pairs={{0,1},{1,0},{2,3},{3,2},{4,5},{5,4},{6,7},{7,6},{8,9},{9,8},{10,11... | collective-permute-start | bytes 786440 | tf_op jit(solution)/shard_map/ppermute | solution.py:192
  10.0 8.5 %collective-permute-start.5 = (bf16[128,1024]{1,0:T(8,128)(2,1)S(1)}, bf16[128,1024]{1,0:T(8,128)(2,1)S(1)}, u32[]{:S(2)}, u32[]{:S(2)}) collective-permute-start(bf16[128,1024]{1,0:T(8,128)(2,1)S(1)} %broadcast_select_fusion), channel_id=1, source_target_pairs={{0,3},{1,2},{2,1},{3,0},{4,7},{5,6},{6,5},{7,4},{8,11},{9,10},{10,... | collective-permute-start | bytes 786440 | tf_op jit(solution)/shard_map/ppermute | solution.py:192
  12.9 25.2 %copy-start = (bf16[1,2,128,1024]{3,2,1,0:T(8,128)(2,1)S(1)}, bf16[1,2,128,1024]{3,2,1,0:T(8,128)(2,1)}, u32[]{:S(2)}) copy-start(bf16[1,2,128,1024]{3,2,1,0:T(8,128)(2,1)} %param.8) | copy-start | bytes 1572868
  12.9 25.2 %copy-start.1 = (bf16[1,2,128,1024]{3,2,1,0:T(8,128)(2,1)S(1)}, bf16[1,2,128,1024]{3,2,1,0:T(8,128)(2,1)}, u32[]{:S(2)}) copy-start(bf16[1,2,128,1024]{3,2,1,0:T(8,128)(2,1)} %param.9) | copy-start | bytes 1572868
  13.0 7.2 %collective-permute-start.1 = (bf16[128,1024]{1,0:T(8,128)(2,1)S(1)}, bf16[128,1024]{1,0:T(8,128)(2,1)S(1)}, u32[]{:S(2)}, u32[]{:S(2)}) collective-permute-start(bf16[128,1024]{1,0:T(8,128)(2,1)S(1)} %pad_maximum_fusion), channel_id=1, source_target_pairs={{0,1},{1,0},{2,3},{3,2},{4,5},{5,4},{6,7},{7,6},{8,9},{9,8},{10,11... | collective-permute-start | bytes 786440 | tf_op jit(solution)/shard_map/ppermute | solution.py:192
  18.6 6.5 %collective-permute-start.6 = (bf16[128,1024]{1,0:T(8,128)(2,1)S(1)}, bf16[128,1024]{1,0:T(8,128)(2,1)S(1)}, u32[]{:S(2)}, u32[]{:S(2)}) collective-permute-start(bf16[128,1024]{1,0:T(8,128)(2,1)S(1)} %select_select_fusion), channel_id=1, source_target_pairs={{0,4},{4,0},{8,12},{12,8},{1,5},{5,1},{9,13},{13,9},{2,6},{6,2},{1... | collective-permute-start | bytes 786440 | tf_op jit(solution)/shard_map/ppermute | solution.py:192
  21.0 7.8 %collective-permute-start.2 = (bf16[128,1024]{1,0:T(8,128)(2,1)}, bf16[128,1024]{1,0:T(8,128)(2,1)S(1)}, u32[]{:S(2)}, u32[]{:S(2)}) collective-permute-start(bf16[128,1024]{1,0:T(8,128)(2,1)} %broadcast_select_fusion.1), channel_id=1, source_target_pairs={{0,3},{1,2},{2,1},{3,0},{4,7},{5,6},{6,5},{7,4},{8,11},{9,10},{10,... | collective-permute-start | bytes 786440 | tf_op jit(solution)/shard_map/ppermute | solution.py:192
  25.8 7.8 %collective-permute-start.7 = (bf16[128,1024]{1,0:T(8,128)(2,1)}, bf16[128,1024]{1,0:T(8,128)(2,1)S(1)}, u32[]{:S(2)}, u32[]{:S(2)}) collective-permute-start(bf16[128,1024]{1,0:T(8,128)(2,1)} %broadcast_select_fusion.2), channel_id=1, source_target_pairs={{0,12},{4,8},{8,4},{12,0},{1,13},{5,9},{9,5},{13,1},{2,14},{6,10},... | collective-permute-start | bytes 786440 | tf_op jit(solution)/shard_map/ppermute | solution.py:192
  28.9 6.5 %collective-permute-start.3 = (bf16[128,1024]{1,0:T(8,128)(2,1)S(1)}, bf16[128,1024]{1,0:T(8,128)(2,1)S(1)}, u32[]{:S(2)}, u32[]{:S(2)}) collective-permute-start(bf16[128,1024]{1,0:T(8,128)(2,1)S(1)} %select_select_fusion.1), channel_id=1, source_target_pairs={{0,4},{4,0},{8,12},{12,8},{1,5},{5,1},{9,13},{13,9},{2,6},{6,2},{1... | collective-permute-start | bytes 786440 | tf_op jit(solution)/shard_map/ppermute | solution.py:192
  35.3 20.8 %collective-permute-start.4 = (bf16[128,1024]{1,0:T(8,128)(2,1)S(1)}, bf16[128,1024]{1,0:T(8,128)(2,1)S(1)}, u32[]{:S(2)}, u32[]{:S(2)}) collective-permute-start(bf16[128,1024]{1,0:T(8,128)(2,1)S(1)} %broadcast_select_fusion.3), channel_id=1, source_target_pairs={{0,12},{4,8},{8,4},{12,0},{1,13},{5,9},{9,5},{13,1},{2,14},{6,10},... | collective-permute-start | bytes 786440 | tf_op jit(solution)/shard_map/ppermute | solution.py:192
  56.2 18.9 %collective-permute-start.8 = (bf16[128,1024]{1,0:T(8,128)(2,1)S(1)}, bf16[128,1024]{1,0:T(8,128)(2,1)S(1)}, u32[]{:S(2)}, u32[]{:S(2)}) collective-permute-start(bf16[128,1024]{1,0:T(8,128)(2,1)S(1)} %get-tuple-element.42), channel_id=1, source_target_pairs={{0,12},{4,8},{8,4},{12,0},{1,13},{5,9},{9,5},{13,1},{2,14},{6,10},... | collective-permute-start | bytes 786440 | tf_op jit(solution)/shard_map/ppermute | solution.py:192
  75.1 7.6 %collective-permute-start.12 = (bf16[128,1024]{1,0:T(8,128)(2,1)S(1)}, bf16[128,1024]{1,0:T(8,128)(2,1)S(1)}, u32[]{:S(2)}, u32[]{:S(2)}) collective-permute-start(bf16[128,1024]{1,0:T(8,128)(2,1)S(1)} %get-tuple-element.49), channel_id=1, source_target_pairs={{0,12},{4,8},{8,4},{12,0},{1,13},{5,9},{9,5},{13,1},{2,14},{6,10},... | collective-permute-start | bytes 786440 | tf_op jit(solution)/shard_map/ppermute | solution.py:192
  77.9 7.3 %collective-permute-start.9 = (bf16[128,1024]{1,0:T(8,128)(2,1)S(1)}, bf16[128,1024]{1,0:T(8,128)(2,1)S(1)}, u32[]{:S(2)}, u32[]{:S(2)}) collective-permute-start(bf16[128,1024]{1,0:T(8,128)(2,1)S(1)} %add_convert_fusion.2), channel_id=1, source_target_pairs={{0,4},{4,0},{8,12},{12,8},{1,5},{5,1},{9,13},{13,9},{2,6},{6,2},{1... | collective-permute-start | bytes 786440 | tf_op jit(solution)/shard_map/ppermute | solution.py:192
  82.8 6.5 %collective-permute-start.13 = (bf16[128,1024]{1,0:T(8,128)(2,1)S(1)}, bf16[128,1024]{1,0:T(8,128)(2,1)S(1)}, u32[]{:S(2)}, u32[]{:S(2)}) collective-permute-start(bf16[128,1024]{1,0:T(8,128)(2,1)S(1)} %fusion.7), channel_id=1, source_target_pairs={{0,4},{4,0},{8,12},{12,8},{1,5},{5,1},{9,13},{13,9},{2,6},{6,2},{1... | collective-permute-start | bytes 786440 | tf_op jit(solution)/shard_map/ppermute | solution.py:192
  85.3 7.9 %collective-permute-start.10 = (bf16[128,1024]{1,0:T(8,128)(2,1)S(1)}, bf16[128,1024]{1,0:T(8,128)(2,1)S(1)}, u32[]{:S(2)}, u32[]{:S(2)}) collective-permute-start(bf16[128,1024]{1,0:T(8,128)(2,1)S(1)} %add_convert_fusion.1), channel_id=1, source_target_pairs={{0,3},{1,2},{2,1},{3,0},{4,7},{5,6},{6,5},{7,4},{8,11},{9,10},{10,... | collective-permute-start | bytes 786440 | tf_op jit(solution)/shard_map/ppermute | solution.py:192
  89.4 7.7 %collective-permute-start.14 = (bf16[128,1024]{1,0:T(8,128)(2,1)S(1)}, bf16[128,1024]{1,0:T(8,128)(2,1)S(1)}, u32[]{:S(2)}, u32[]{:S(2)}) collective-permute-start(bf16[128,1024]{1,0:T(8,128)(2,1)S(1)} %add_convert_fusion), channel_id=1, source_target_pairs={{0,3},{1,2},{2,1},{3,0},{4,7},{5,6},{6,5},{7,4},{8,11},{9,10},{10,... | collective-permute-start | bytes 786440 | tf_op jit(solution)/shard_map/ppermute | solution.py:192
  93.3 6.5 %collective-permute-start.11 = (bf16[128,1024]{1,0:T(8,128)(2,1)S(1)}, bf16[128,1024]{1,0:T(8,128)(2,1)S(1)}, u32[]{:S(2)}, u32[]{:S(2)}) collective-permute-start(bf16[128,1024]{1,0:T(8,128)(2,1)S(1)} %fusion.4), channel_id=1, source_target_pairs={{0,1},{1,0},{2,3},{3,2},{4,5},{5,4},{6,7},{7,6},{8,9},{9,8},{10,11... | collective-permute-start | bytes 786440 | tf_op jit(solution)/shard_map/ppermute | solution.py:192
  97.2 6.5 %collective-permute-start.15 = (bf16[128,1024]{1,0:T(8,128)(2,1)S(1)}, bf16[128,1024]{1,0:T(8,128)(2,1)S(1)}, u32[]{:S(2)}, u32[]{:S(2)}) collective-permute-start(bf16[128,1024]{1,0:T(8,128)(2,1)S(1)} %fusion.12), channel_id=1, source_target_pairs={{0,1},{1,0},{2,3},{3,2},{4,5},{5,4},{6,7},{7,6},{8,9},{9,8},{10,11... | collective-permute-start | bytes 786440 | tf_op jit(solution)/shard_map/ppermute | solution.py:192

commit v5 on v4

--- a/solution.py
+++ b/solution.py
@@ -33,8 +33,8 @@
 
 def kernel(count, info, q_ref, g_ref, *refs):
     k_refs, v_refs = refs[0:6], refs[6:12]
-    dq_ref, out_refs = refs[-11], refs[-10:-4]
-    w_s, ds_s, mask_s, tri_s = refs[-4:]
+    dq_ref, out_refs = refs[-12], refs[-11:-5]
+    w_s, ds_s, mask_s, tri_s, bias_s = refs[-5:]
     bf = jnp.bfloat16
     row = lax.broadcasted_iota(jnp.int32, (R, D), 0)
     col = lax.broadcasted_iota(jnp.int32, (R, D), 1)
@@ -48,6 +48,12 @@
                 if (t, j) in ((0, 0), (1, 5)):
                     hot = hot | ((col == row) & (col > 0))
                 mask_s[t, j * R : (j + 1) * R, :] = jnp.where(hot, 1.0, 0.0).astype(bf)
+                ok = row < info[6 * t + j]
+                if (t, j) in ((0, 0), (1, 5)):
+                    ok = ok & (row <= col)
+                if (t, j) == (0, 5):
+                    ok = ok & (row < 0)
+                bias_s[j * R : (j + 1) * R, t * R : (t + 1) * R] = jnp.where(ok, 0.0, -BIG)
 
     k = jnp.concatenate([r[...] for r in k_refs], axis=0)
     v = jnp.concatenate([r[...] for r in v_refs], axis=0)
@@ -60,18 +66,31 @@
         gs.append(
             jnp.concatenate([jnp.where(live, g_ref[rows, h], jnp.zeros((), bf)) for h in heads], axis=0)
         )
-    tri = jnp.concatenate([tri_s[...]] * GROUP, axis=0)
+    pair = 2 * R
+    tri = jnp.concatenate([tri_s[...]] * 2, axis=0)
     sizes = (5 * R, 6 * R)
     k_wide = [jnp.concatenate([k[:n], mask_s[t, :n, :]], axis=1) for t, n in enumerate(sizes)]
-    q_wide = [jnp.concatenate([qs[t], tri], axis=1) for t in range(2)]
     k_turned = k.T
-
-    def products(t, h0, h1):
-        n, part = sizes[t], slice(h0 * R, h1 * R)
-        return dot(k_wide[t], q_wide[t][part], 1, 1), dot(v[:n], gs[t][part], 1, 1)
-
-    def softmax_backward(t, h0, h1, s, dw):
-        n, place = sizes[t], slice((t * GROUP + h0) * R, (t * GROUP + h1) * R)
+    todo = [(t, h, sizes[t]) for t in range(2) for h in (0, 2)] + [(None, 4, 6 * R)]
+
+    def rows_of(stacks, t, h):
+        if t is None:
+            return jnp.concatenate([one[h * R :] for one in stacks], axis=0)
+        return stacks[t][h * R : (h + 2) * R]
+
+    q_parts = [rows_of(qs, t, h) for t, h, _ in todo]
+    g_parts = [rows_of(gs, t, h) for t, h, _ in todo]
+
+    def products(step):
+        t, _, n = todo[step]
+        if t is None:
+            s = dot(k, q_parts[step], 1, 1) + bias_s[...]
+        else:
+            s = dot(k_wide[t], jnp.concatenate([q_parts[step], tri], axis=1), 1, 1)
+        return s, dot(v[:n], g_parts[step], 1, 1)
+
+    def softmax_backward(step, s, dw):
+        n, place = todo[step][2], slice(step * pair, (step + 1) * pair)
         m = jnp.max(s, axis=0, keepdims=True)
         e = jnp.exp2((s - m) * EXP2_SCALE)
         w = e * (1.0 / jnp.sum(e, axis=0, keepdims=True))
@@ -81,37 +100,35 @@
 
     total = {}
 
-    def gradients(t, h0, h1):
-        n, place = sizes[t], slice((t * GROUP + h0) * R, (t * GROUP + h1) * R)
-        part = slice(h0 * R, h1 * R)
+    def gradients(step):
+        t, h, n = todo[step]
+        place = slice(step * pair, (step + 1) * pair)
         ds = ds_s[:n, place]
         for name, term in (
-            (("k", t), dot(ds, qs[t][part], 1, 0)),
-            (("v", t), dot(w_s[:n, place], gs[t][part], 1, 0)),
+            (("k", n), dot(ds, q_parts[step], 1, 0)),
+            (("v", n), dot(w_s[:n, place], g_parts[step], 1, 0)),
         ):
             total[name] = term if name not in total else total[name] + term
-        dq = (dot(k_turned[:, :n], ds, 1, 0) * SCALE).T
-        for h in range(h0, h1):
-            dq_ref[t * R : (t + 1) * R, h * D : (h + 1) * D] = dq[
-                (h - h0) * R : (h - h0 + 1) * R
-            ].astype(bf)
-
-    todo = [(t, h0, h1) for t in range(2) for h0, h1 in ((0, 2), (2, 4), (4, 5))]
-    ahead = products(*todo[0])
-    for step, part in enumerate(todo):
+        dq = (dot(k_turned[:, :n], ds, 1, 0) * SCALE).T.astype(bf)
+        for j in range(2):
+            at, head = (j, h) if t is None else (t, h + j)
+            dq_ref[at * R : (at + 1) * R, head * D : (head + 1) * D] = dq[j * R : (j + 1) * R]
+
+    ahead = products(0)
+    for step in range(len(todo)):
         now = ahead
         if step + 1 < len(todo):
-            ahead = products(*todo[step + 1])
+            ahead = products(step + 1)
         if step:
-            gradients(*todo[step - 1])
-        softmax_backward(*part, *now)
-    gradients(*todo[-1])
+            gradients(step - 1)
+        softmax_backward(step, *now)
+    gradients(len(todo) - 1)
 
     i = pl.program_id(0)
     n = 5 * R
     for name, at, scale in (("k", i, SCALE), ("v", count + i, 1.0)):
         cols = pl.ds(pl.multiple_of(at * D, D), D)
-        inner, leaf = total[name, 0], total[name, 1]
+        inner, leaf = total[name, 5 * R], total[name, 6 * R]
         both = (inner + leaf[:n]) * scale
         for j in range(5):
             out_refs[j][:, cols] = both[j * R : (j + 1) * R].astype(out_refs[j].dtype)
@@ -146,6 +163,7 @@
                 pltpu.VMEM((6 * R, 2 * GROUP * R), jnp.bfloat16),
                 pltpu.VMEM((2, 6 * R, D), jnp.bfloat16),
                 pltpu.VMEM((R, D), jnp.bfloat16),
+                pltpu.VMEM((6 * R, 2 * R), jnp.float32),
             ],
         ),
         compiler_params=pltpu.CompilerParams(vmem_limit_bytes=50 * 2**20),

time: 107 us -> 102 us (0.953)
  Pallas kernels: 36.1 us -> 31.5 us
    pallas_call x2, Pallas kernels: 36.1 us -> 31.5 us  [attend_backward(): pl.pallas_call(functools.partial(kernel, count), input_output_aliases=ali...]
  transfers between devices with their start and end apart: 16 -> 16, of which waited for: 12 -> 12; matrix products, arithmetic and copies ran while one was open for 5% -> 6% of each run, Pallas kernels for 34% -> 31%
where the time goes in v5:
time: 102 us; the launch traced here: 101 us
  waiting for transfers between devices  34 us (33%)
  Pallas kernels  31.5 us (31%)
  starting transfers between devices  25.8 us (25%)
  other arithmetic  5.41 us (5%)
  local copies, waits for them, and re-layouts  3.49 us (3%)
    ppermute x16, waiting for transfers between devices, permute(): return lax.ppermute(value, 'leaf', pairs(axis, ring))  34 us
    pallas_call x2, Pallas kernels, attend_backward(): pl.pallas_call(functools.partial(kernel, count), input_output_aliases=ali...  31.5 us
    ppermute x16, starting transfers between devices, permute(): return lax.ppermute(value, 'leaf', pairs(axis, ring))  25.8 us
  transfers between devices with their start and end apart: 16, of which 12 were waited for; matrix products, arithmetic and copies ran while one was open for 6% of the time, Pallas kernels for 31%

profile of v5, /device:TPU:128, one launch (start us, length us, event | category | flops | bytes accessed | tf_op | source)
XLA Modules:
  0.0 101.1 jit_solution(1219948030787004802)
XLA Ops:
  0.6 1.1 %fusion.14 = (bf16[128,512]{1,0:T(8,128)(2,1)S(1)}, bf16[128,512]{1,0:T(8,128)(2,1)S(1)}, bf16[128,512]{1,0:T(8,128)(2,1)S(1)}, bf16[128,512]{1,0:T(8,128)(2,1)S(1)}) fusion(bf16[256,1024]{1,0:T(8,128)(2,1)} %bitcast.35, bf16[256,1024]{1,0:T(8,128)(2,1)} %bitcast.40), kind=kLoop, calls=%fused_computation.52 | loop fusion | bytes 1048576 | tf_op jit(solution)/shard_map/slice | solution.py:221
  1.8 1.6 %collective-permute-start = (bf16[128,1024]{1,0:T(8,128)(2,1)S(1)}, bf16[128,1024]{1,0:T(8,128)(2,1)S(1)}, u32[]{:S(2)}, u32[]{:S(2)}) collective-permute-start(bf16[128,1024]{1,0:T(8,128)(2,1)S(1)} %pad_maximum_fusion.1), channel_id=1, source_target_pairs={{0,1},{1,0},{2,3},{3,2},{4,5},{5,4},{6,7},{7,6},{8,9},{9,8},{10,11... | collective-permute-start | bytes 786440 | tf_op jit(solution)/shard_map/ppermute | solution.py:210
  3.4 0.8 fusion.20
  4.1 5.8 %collective-permute-done.refs_1_.refs_7_ = bf16[128,1024]{1,0:T(8,128)(2,1)S(1)} collective-permute-done((bf16[128,1024]{1,0:T(8,128)(2,1)S(1)}, bf16[128,1024]{1,0:T(8,128)(2,1)S(1)}, u32[]{:S(2)}, u32[]{:S(2)}) %collective-permute-start) | collective-permute-done | bytes 262176 | tf_op jit(solution)/shard_map/ppermute | solution.py:210
  10.0 2.8 %collective-permute-start.5 = (bf16[128,1024]{1,0:T(8,128)(2,1)S(1)}, bf16[128,1024]{1,0:T(8,128)(2,1)S(1)}, u32[]{:S(2)}, u32[]{:S(2)}) collective-permute-start(bf16[128,1024]{1,0:T(8,128)(2,1)S(1)} %broadcast_select_fusion), channel_id=1, source_target_pairs={{0,3},{1,2},{2,1},{3,0},{4,7},{5,6},{6,5},{7,4},{8,11},{9,10},{10,... | collective-permute-start | bytes 786440 | tf_op jit(solution)/shard_map/ppermute | solution.py:210
  12.9 0.1 stack.60
  13.0 0.2 collective-permute-start.1
  13.3 5.2 %collective-permute-done.5.refs_2_.refs_8_ = bf16[128,1024]{1,0:T(8,128)(2,1)S(1)} collective-permute-done((bf16[128,1024]{1,0:T(8,128)(2,1)S(1)}, bf16[128,1024]{1,0:T(8,128)(2,1)S(1)}, u32[]{:S(2)}, u32[]{:S(2)}) %collective-permute-start.5) | collective-permute-done | bytes 262176 | tf_op jit(solution)/shard_map/ppermute | solution.py:210
  18.5 0.1 select_select_fusion
  18.6 1.7 %collective-permute-start.6 = (bf16[128,1024]{1,0:T(8,128)(2,1)S(1)}, bf16[128,1024]{1,0:T(8,128)(2,1)S(1)}, u32[]{:S(2)}, u32[]{:S(2)}) collective-permute-start(bf16[128,1024]{1,0:T(8,128)(2,1)S(1)} %select_select_fusion), channel_id=1, source_target_pairs={{0,4},{4,0},{8,12},{12,8},{1,5},{5,1},{9,13},{13,9},{2,6},{6,2},{1... | collective-permute-start | bytes 786440 | tf_op jit(solution)/shard_map/ppermute | solution.py:210
  20.3 0.7 broadcast_select_fusion.1
  21.0 2.8 %collective-permute-start.2 = (bf16[128,1024]{1,0:T(8,128)(2,1)}, bf16[128,1024]{1,0:T(8,128)(2,1)S(1)}, u32[]{:S(2)}, u32[]{:S(2)}) collective-permute-start(bf16[128,1024]{1,0:T(8,128)(2,1)} %broadcast_select_fusion.1), channel_id=1, source_target_pairs={{0,3},{1,2},{2,1},{3,0},{4,7},{5,6},{6,5},{7,4},{8,11},{9,10},{10,... | collective-permute-start | bytes 786440 | tf_op jit(solution)/shard_map/ppermute | solution.py:210
  23.7 0.6 gather_fusion
  24.4 0.1 stack.54
  24.5 0.6 collective-permute-done.6.refs_3_.refs_9_
  25.0 0.7 broadcast_select_fusion.2
  25.8 3.0 %collective-permute-start.7 = (bf16[128,1024]{1,0:T(8,128)(2,1)}, bf16[128,1024]{1,0:T(8,128)(2,1)S(1)}, u32[]{:S(2)}, u32[]{:S(2)}) collective-permute-start(bf16[128,1024]{1,0:T(8,128)(2,1)} %broadcast_select_fusion.2), channel_id=1, source_target_pairs={{0,12},{4,8},{8,4},{12,0},{1,13},{5,9},{9,5},{13,1},{2,14},{6,10},... | collective-permute-start | bytes 786440 | tf_op jit(solution)/shard_map/ppermute | solution.py:210
  28.9 1.3 %collective-permute-start.3 = (bf16[128,1024]{1,0:T(8,128)(2,1)S(1)}, bf16[128,1024]{1,0:T(8,128)(2,1)S(1)}, u32[]{:S(2)}, u32[]{:S(2)}) collective-permute-start(bf16[128,1024]{1,0:T(8,128)(2,1)S(1)} %select_select_fusion.1), channel_id=1, source_target_pairs={{0,4},{4,0},{8,12},{12,8},{1,5},{5,1},{9,13},{13,9},{2,6},{6,2},{1... | collective-permute-start | bytes 786440 | tf_op jit(solution)/shard_map/ppermute | solution.py:210
  30.2 0.6 constant_dynamic-update-slice_fusion
  30.8 0.7 concatenate.44.info
  31.5 2.1 %collective-permute-done.7.refs_4_.refs_10_ = bf16[128,1024]{1,0:T(8,128)(2,1)S(1)} collective-permute-done((bf16[128,1024]{1,0:T(8,128)(2,1)}, bf16[128,1024]{1,0:T(8,128)(2,1)S(1)}, u32[]{:S(2)}, u32[]{:S(2)}) %collective-permute-start.7) | collective-permute-done | bytes 262176 | tf_op jit(solution)/shard_map/ppermute | solution.py:210
  33.6 1.7 %collective-permute-done.3.refs_3_.refs_9_ = bf16[128,1024]{1,0:T(8,128)(2,1)S(1)} collective-permute-done((bf16[128,1024]{1,0:T(8,128)(2,1)S(1)}, bf16[128,1024]{1,0:T(8,128)(2,1)S(1)}, u32[]{:S(2)}, u32[]{:S(2)}) %collective-permute-start.3) | collective-permute-done | bytes 262176 | tf_op jit(solution)/shard_map/ppermute | solution.py:210
  35.3 2.8 %collective-permute-start.4 = (bf16[128,1024]{1,0:T(8,128)(2,1)S(1)}, bf16[128,1024]{1,0:T(8,128)(2,1)S(1)}, u32[]{:S(2)}, u32[]{:S(2)}) collective-permute-start(bf16[128,1024]{1,0:T(8,128)(2,1)S(1)} %broadcast_select_fusion.3), channel_id=1, source_target_pairs={{0,12},{4,8},{8,4},{12,0},{1,13},{5,9},{9,5},{13,1},{2,14},{6,10},... | collective-permute-start | bytes 786440 | tf_op jit(solution)/shard_map/ppermute | solution.py:210
  38.1 15.8 %shard_map.76 = (bf16[256,5120]{1,0:T(8,128)(2,1)}, f32[128,1024]{1,0:T(8,128)S(1)}, bf16[128,1024]{1,0:T(8,128)(2,1)S(1)}, bf16[128,1024]{1,0:T(8,128)(2,1)S(1)...) custom-call(s32[16]{0:T(128)S(1)} %concatenate.44.info, ...), custom_call_target="tpu_custom_call" | custom-call | flops 18400000000 | bytes 4194304 | tf_op jit(solution)/shard_map/pallas_call | solution.py:150
  53.9 0.8 collective-permute-start.8
  54.7 15.8 %shard_map.77 = (bf16[256,5120]{1,0:T(8,128)(2,1)}, f32[128,1024]{1,0:T(8,128)S(1)}, bf16[128,1024]{1,0:T(8,128)(2,1)S(1)}, bf16[128,1024]{1,0:T(8,128)(2,1)S(1)...) custom-call(s32[16]{0:T(128)S(1)} %concatenate.44.info, ...), custom_call_target="tpu_custom_call", output_to_operand_aliasing={{0}: (15, {})} | custom-call | flops 18400000000 | bytes 4194304 | tf_op jit(solution)/shard_map/pallas_call | solution.py:150
  70.5 2.7 %collective-permute-start.12 = (bf16[128,1024]{1,0:T(8,128)(2,1)S(1)}, bf16[128,1024]{1,0:T(8,128)(2,1)S(1)}, u32[]{:S(2)}, u32[]{:S(2)}) collective-permute-start(bf16[128,1024]{1,0:T(8,128)(2,1)S(1)} %get-tuple-element.49), channel_id=1, source_target_pairs={{0,12},{4,8},{8,4},{12,0},{1,13},{5,9},{9,5},{13,1},{2,14},{6,10},... | collective-permute-start | bytes 786440 | tf_op jit(solution)/shard_map/ppermute | solution.py:210
  73.3 0.1 collective-permute-start.9
  73.4 4.7 %collective-permute-done.12 = bf16[128,1024]{1,0:T(8,128)(2,1)S(1)} collective-permute-done((bf16[128,1024]{1,0:T(8,128)(2,1)S(1)}, bf16[128,1024]{1,0:T(8,128)(2,1)S(1)}, u32[]{:S(2)}, u32[]{:S(2)}) %collective-permute-start.12) | collective-permute-done | bytes 262176 | tf_op jit(solution)/shard_map/ppermute | solution.py:210
  78.2 0.1 collective-permute-start.13
  78.3 2.2 %collective-permute-done.9 = bf16[128,1024]{1,0:T(8,128)(2,1)S(1)} collective-permute-done((bf16[128,1024]{1,0:T(8,128)(2,1)S(1)}, bf16[128,1024]{1,0:T(8,128)(2,1)S(1)}, u32[]{:S(2)}, u32[]{:S(2)}) %collective-permute-start.9) | collective-permute-done | bytes 262176 | tf_op jit(solution)/shard_map/ppermute | solution.py:210
  80.5 0.1 add_convert_fusion.1
  80.7 2.8 %collective-permute-start.10 = (bf16[128,1024]{1,0:T(8,128)(2,1)S(1)}, bf16[128,1024]{1,0:T(8,128)(2,1)S(1)}, u32[]{:S(2)}, u32[]{:S(2)}) collective-permute-start(bf16[128,1024]{1,0:T(8,128)(2,1)S(1)} %add_convert_fusion.1), channel_id=1, source_target_pairs={{0,3},{1,2},{2,1},{3,0},{4,7},{5,6},{6,5},{7,4},{8,11},{9,10},{10,... | collective-permute-start | bytes 786440 | tf_op jit(solution)/shard_map/ppermute | solution.py:210
  83.5 1.1 %collective-permute-done.13 = bf16[128,1024]{1,0:T(8,128)(2,1)S(1)} collective-permute-done((bf16[128,1024]{1,0:T(8,128)(2,1)S(1)}, bf16[128,1024]{1,0:T(8,128)(2,1)S(1)}, u32[]{:S(2)}, u32[]{:S(2)}) %collective-permute-start.13) | collective-permute-done | bytes 262176 | tf_op jit(solution)/shard_map/ppermute | solution.py:210
  84.6 0.1 add_convert_fusion
  84.8 2.8 %collective-permute-start.14 = (bf16[128,1024]{1,0:T(8,128)(2,1)S(1)}, bf16[128,1024]{1,0:T(8,128)(2,1)S(1)}, u32[]{:S(2)}, u32[]{:S(2)}) collective-permute-start(bf16[128,1024]{1,0:T(8,128)(2,1)S(1)} %add_convert_fusion), channel_id=1, source_target_pairs={{0,3},{1,2},{2,1},{3,0},{4,7},{5,6},{6,5},{7,4},{8,11},{9,10},{10,... | collective-permute-start | bytes 786440 | tf_op jit(solution)/shard_map/ppermute | solution.py:210
  87.6 0.9 collective-permute-done.10
  88.5 0.2 fusion.4
  88.7 0.1 collective-permute-start.11
  88.9 3.6 %collective-permute-done.14 = bf16[128,1024]{1,0:T(8,128)(2,1)S(1)} collective-permute-done((bf16[128,1024]{1,0:T(8,128)(2,1)S(1)}, bf16[128,1024]{1,0:T(8,128)(2,1)S(1)}, u32[]{:S(2)}, u32[]{:S(2)}) %collective-permute-start.14) | collective-permute-done | bytes 262176 | tf_op jit(solution)/shard_map/ppermute | solution.py:210
  92.5 0.2 fusion.12
  92.6 0.1 collective-permute-start.15
  92.8 2.4 %collective-permute-done.11 = bf16[128,1024]{1,0:T(8,128)(2,1)S(1)} collective-permute-done((bf16[128,1024]{1,0:T(8,128)(2,1)S(1)}, bf16[128,1024]{1,0:T(8,128)(2,1)S(1)}, u32[]{:S(2)}, u32[]{:S(2)}) %collective-permute-start.11) | collective-permute-done | bytes 262176 | tf_op jit(solution)/shard_map/ppermute | solution.py:210
  95.2 0.2 fusion.2
  95.4 3.7 %collective-permute-done.15 = bf16[128,1024]{1,0:T(8,128)(2,1)S(1)} collective-permute-done((bf16[128,1024]{1,0:T(8,128)(2,1)S(1)}, bf16[128,1024]{1,0:T(8,128)(2,1)S(1)}, u32[]{:S(2)}, u32[]{:S(2)}) %collective-permute-start.15) | collective-permute-done | bytes 262176 | tf_op jit(solution)/shard_map/ppermute | solution.py:210
  99.1 0.2 fusion.10
  99.4 0.8 maximum_bitcast_fusion.1
  100.3 0.8 maximum_bitcast_fusion
  (28 shorter events, 0.6 us)
Async XLA Ops:
  1.8 8.1 %collective-permute-start = (bf16[128,1024]{1,0:T(8,128)(2,1)S(1)}, bf16[128,1024]{1,0:T(8,128)(2,1)S(1)}, u32[]{:S(2)}, u32[]{:S(2)}) collective-permute-start(bf16[128,1024]{1,0:T(8,128)(2,1)S(1)} %pad_maximum_fusion.1), channel_id=1, source_target_pairs={{0,1},{1,0},{2,3},{3,2},{4,5},{5,4},{6,7},{7,6},{8,9},{9,8},{10,11... | collective-permute-start | bytes 786440 | tf_op jit(solution)/shard_map/ppermute | solution.py:210
  10.0 8.5 %collective-permute-start.5 = (bf16[128,1024]{1,0:T(8,128)(2,1)S(1)}, bf16[128,1024]{1,0:T(8,128)(2,1)S(1)}, u32[]{:S(2)}, u32[]{:S(2)}) collective-permute-start(bf16[128,1024]{1,0:T(8,128)(2,1)S(1)} %broadcast_select_fusion), channel_id=1, source_target_pairs={{0,3},{1,2},{2,1},{3,0},{4,7},{5,6},{6,5},{7,4},{8,11},{9,10},{10,... | collective-permute-start | bytes 786440 | tf_op jit(solution)/shard_map/ppermute | solution.py:210
  12.9 25.2 %copy-start = (bf16[1,2,128,1024]{3,2,1,0:T(8,128)(2,1)S(1)}, bf16[1,2,128,1024]{3,2,1,0:T(8,128)(2,1)}, u32[]{:S(2)}) copy-start(bf16[1,2,128,1024]{3,2,1,0:T(8,128)(2,1)} %param.8) | copy-start | bytes 1572868
  12.9 25.2 %copy-start.1 = (bf16[1,2,128,1024]{3,2,1,0:T(8,128)(2,1)S(1)}, bf16[1,2,128,1024]{3,2,1,0:T(8,128)(2,1)}, u32[]{:S(2)}) copy-start(bf16[1,2,128,1024]{3,2,1,0:T(8,128)(2,1)} %param.9) | copy-start | bytes 1572868
  13.0 7.2 %collective-permute-start.1 = (bf16[128,1024]{1,0:T(8,128)(2,1)S(1)}, bf16[128,1024]{1,0:T(8,128)(2,1)S(1)}, u32[]{:S(2)}, u32[]{:S(2)}) collective-permute-start(bf16[128,1024]{1,0:T(8,128)(2,1)S(1)} %pad_maximum_fusion), channel_id=1, source_target_pairs={{0,1},{1,0},{2,3},{3,2},{4,5},{5,4},{6,7},{7,6},{8,9},{9,8},{10,11... | collective-permute-start | bytes 786440 | tf_op jit(solution)/shard_map/ppermute | solution.py:210
  18.6 6.5 %collective-permute-start.6 = (bf16[128,1024]{1,0:T(8,128)(2,1)S(1)}, bf16[128,1024]{1,0:T(8,128)(2,1)S(1)}, u32[]{:S(2)}, u32[]{:S(2)}) collective-permute-start(bf16[128,1024]{1,0:T(8,128)(2,1)S(1)} %select_select_fusion), channel_id=1, source_target_pairs={{0,4},{4,0},{8,12},{12,8},{1,5},{5,1},{9,13},{13,9},{2,6},{6,2},{1... | collective-permute-start | bytes 786440 | tf_op jit(solution)/shard_map/ppermute | solution.py:210
  21.0 7.8 %collective-permute-start.2 = (bf16[128,1024]{1,0:T(8,128)(2,1)}, bf16[128,1024]{1,0:T(8,128)(2,1)S(1)}, u32[]{:S(2)}, u32[]{:S(2)}) collective-permute-start(bf16[128,1024]{1,0:T(8,128)(2,1)} %broadcast_select_fusion.1), channel_id=1, source_target_pairs={{0,3},{1,2},{2,1},{3,0},{4,7},{5,6},{6,5},{7,4},{8,11},{9,10},{10,... | collective-permute-start | bytes 786440 | tf_op jit(solution)/shard_map/ppermute | solution.py:210
  25.8 7.8 %collective-permute-start.7 = (bf16[128,1024]{1,0:T(8,128)(2,1)}, bf16[128,1024]{1,0:T(8,128)(2,1)S(1)}, u32[]{:S(2)}, u32[]{:S(2)}) collective-permute-start(bf16[128,1024]{1,0:T(8,128)(2,1)} %broadcast_select_fusion.2), channel_id=1, source_target_pairs={{0,12},{4,8},{8,4},{12,0},{1,13},{5,9},{9,5},{13,1},{2,14},{6,10},... | collective-permute-start | bytes 786440 | tf_op jit(solution)/shard_map/ppermute | solution.py:210
  28.9 6.5 %collective-permute-start.3 = (bf16[128,1024]{1,0:T(8,128)(2,1)S(1)}, bf16[128,1024]{1,0:T(8,128)(2,1)S(1)}, u32[]{:S(2)}, u32[]{:S(2)}) collective-permute-start(bf16[128,1024]{1,0:T(8,128)(2,1)S(1)} %select_select_fusion.1), channel_id=1, source_target_pairs={{0,4},{4,0},{8,12},{12,8},{1,5},{5,1},{9,13},{13,9},{2,6},{6,2},{1... | collective-permute-start | bytes 786440 | tf_op jit(solution)/shard_map/ppermute | solution.py:210
  35.3 18.6 %collective-permute-start.4 = (bf16[128,1024]{1,0:T(8,128)(2,1)S(1)}, bf16[128,1024]{1,0:T(8,128)(2,1)S(1)}, u32[]{:S(2)}, u32[]{:S(2)}) collective-permute-start(bf16[128,1024]{1,0:T(8,128)(2,1)S(1)} %broadcast_select_fusion.3), channel_id=1, source_target_pairs={{0,12},{4,8},{8,4},{12,0},{1,13},{5,9},{9,5},{13,1},{2,14},{6,10},... | collective-permute-start | bytes 786440 | tf_op jit(solution)/shard_map/ppermute | solution.py:210
  53.9 16.6 %collective-permute-start.8 = (bf16[128,1024]{1,0:T(8,128)(2,1)S(1)}, bf16[128,1024]{1,0:T(8,128)(2,1)S(1)}, u32[]{:S(2)}, u32[]{:S(2)}) collective-permute-start(bf16[128,1024]{1,0:T(8,128)(2,1)S(1)} %get-tuple-element.42), channel_id=1, source_target_pairs={{0,12},{4,8},{8,4},{12,0},{1,13},{5,9},{9,5},{13,1},{2,14},{6,10},... | collective-permute-start | bytes 786440 | tf_op jit(solution)/shard_map/ppermute | solution.py:210
  70.5 7.6 %collective-permute-start.12 = (bf16[128,1024]{1,0:T(8,128)(2,1)S(1)}, bf16[128,1024]{1,0:T(8,128)(2,1)S(1)}, u32[]{:S(2)}, u32[]{:S(2)}) collective-permute-start(bf16[128,1024]{1,0:T(8,128)(2,1)S(1)} %get-tuple-element.49), channel_id=1, source_target_pairs={{0,12},{4,8},{8,4},{12,0},{1,13},{5,9},{9,5},{13,1},{2,14},{6,10},... | collective-permute-start | bytes 786440 | tf_op jit(solution)/shard_map/ppermute | solution.py:210
  73.3 7.3 %collective-permute-start.9 = (bf16[128,1024]{1,0:T(8,128)(2,1)S(1)}, bf16[128,1024]{1,0:T(8,128)(2,1)S(1)}, u32[]{:S(2)}, u32[]{:S(2)}) collective-permute-start(bf16[128,1024]{1,0:T(8,128)(2,1)S(1)} %add_convert_fusion.2), channel_id=1, source_target_pairs={{0,4},{4,0},{8,12},{12,8},{1,5},{5,1},{9,13},{13,9},{2,6},{6,2},{1... | collective-permute-start | bytes 786440 | tf_op jit(solution)/shard_map/ppermute | solution.py:210
  78.2 6.5 %collective-permute-start.13 = (bf16[128,1024]{1,0:T(8,128)(2,1)S(1)}, bf16[128,1024]{1,0:T(8,128)(2,1)S(1)}, u32[]{:S(2)}, u32[]{:S(2)}) collective-permute-start(bf16[128,1024]{1,0:T(8,128)(2,1)S(1)} %fusion.7), channel_id=1, source_target_pairs={{0,4},{4,0},{8,12},{12,8},{1,5},{5,1},{9,13},{13,9},{2,6},{6,2},{1... | collective-permute-start | bytes 786440 | tf_op jit(solution)/shard_map/ppermute | solution.py:210
  80.7 7.9 %collective-permute-start.10 = (bf16[128,1024]{1,0:T(8,128)(2,1)S(1)}, bf16[128,1024]{1,0:T(8,128)(2,1)S(1)}, u32[]{:S(2)}, u32[]{:S(2)}) collective-permute-start(bf16[128,1024]{1,0:T(8,128)(2,1)S(1)} %add_convert_fusion.1), channel_id=1, source_target_pairs={{0,3},{1,2},{2,1},{3,0},{4,7},{5,6},{6,5},{7,4},{8,11},{9,10},{10,... | collective-permute-start | bytes 786440 | tf_op jit(solution)/shard_map/ppermute | solution.py:210
  84.8 7.7 %collective-permute-start.14 = (bf16[128,1024]{1,0:T(8,128)(2,1)S(1)}, bf16[128,1024]{1,0:T(8,128)(2,1)S(1)}, u32[]{:S(2)}, u32[]{:S(2)}) collective-permute-start(bf16[128,1024]{1,0:T(8,128)(2,1)S(1)} %add_convert_fusion), channel_id=1, source_target_pairs={{0,3},{1,2},{2,1},{3,0},{4,7},{5,6},{6,5},{7,4},{8,11},{9,10},{10,... | collective-permute-start | bytes 786440 | tf_op jit(solution)/shard_map/ppermute | solution.py:210
  88.7 6.5 %collective-permute-start.11 = (bf16[128,1024]{1,0:T(8,128)(2,1)S(1)}, bf16[128,1024]{1,0:T(8,128)(2,1)S(1)}, u32[]{:S(2)}, u32[]{:S(2)}) collective-permute-start(bf16[128,1024]{1,0:T(8,128)(2,1)S(1)} %fusion.4), channel_id=1, source_target_pairs={{0,1},{1,0},{2,3},{3,2},{4,5},{5,4},{6,7},{7,6},{8,9},{9,8},{10,11... | collective-permute-start | bytes 786440 | tf_op jit(solution)/shard_map/ppermute | solution.py:210
  92.6 6.5 %collective-permute-start.15 = (bf16[128,1024]{1,0:T(8,128)(2,1)S(1)}, bf16[128,1024]{1,0:T(8,128)(2,1)S(1)}, u32[]{:S(2)}, u32[]{:S(2)}) collective-permute-start(bf16[128,1024]{1,0:T(8,128)(2,1)S(1)} %fusion.12), channel_id=1, source_target_pairs={{0,1},{1,0},{2,3},{3,2},{4,5},{5,4},{6,7},{7,6},{8,9},{9,8},{10,11... | collective-permute-start | bytes 786440 | tf_op jit(solution)/shard_map/ppermute | solution.py:210
